TPU v7x, 256 devices: a whole 4x4x8 slice. The times are simulated.
256 devices in a mesh: blk: 128 (over y, x_hi, z, core), rep: 2 (over x_lo).
Axes of the slice: x: 4 (x_hi: 2, x_lo: 2; x = x_hi * 2 + x_lo), y: 4, z: 8, core: 2. Of those that a mesh axis runs over, the one named last changes fastest.
Arguments:
- entities: bfloat16 [65536, 400], P('blk'), may hold values from -1.75 to 1.75
- hot_entities: bfloat16 [1024, 400], replicated, may hold values from -1.75 to 1.75
- relations: bfloat16 [4096, 400], replicated, may hold values from -3.5 to 3.5
- src_ids: int32 [128, 2, 3, 256], P('blk', 'rep'), may hold values from 0 to 511
- rel_ids: int32 [128, 2, 3, 256], P('blk', 'rep'), may hold values from 0 to 4095
- dst_ids: int32 [128, 2, 3, 256], P('blk', 'rep'), may hold values from 0 to 511
- neg_ids: int32 [128, 2, 3, 512], P('blk', 'rep'), may hold values from 0 to 1535
- counts: int32 [128, 2, 3], P('blk', 'rep'), may hold values from 1 to 256, as said below
- hot_slot: int32 [1024], replicated, may hold values from 0 to 1023, each once
Outputs:
- entity_grad: float32 [65536, 400], P('blk')
- relation_grad: float32 [4096, 400], replicated
- hot_grad: float32 [1024, 400], P(('blk', 'rep'))
Inputs may be any that keep to these rules, and one draw needn't show every extreme that they name: `counts`: some slot block of every draw is full.
All inputs are finite; a program needn't handle non-finite values.
Results may differ from a plain program's by a relative error of at most 0.0044.
Values may be sent and summed in bfloat16 or wider, within the bound.
No kernel may reach another device: no remote copies, remote signals or barrier semaphores. Data moves between devices by JAX's collectives and lax.ppermute only.
A program may use at most 128 MiB of HBM per device.

v0:
```python
import jax
import jax.numpy as jnp
from jax import lax
from jax.sharding import PartitionSpec as P

HALF = 1
BUCKETS = 3


def passed_along(value, axis, steps):
    count = lax.axis_size(axis)
    pairs = [(source, (source + steps) % count) for source in range(count)]
    return lax.ppermute(value, axis, pairs)


def complex_mul(left_real, left_imag, right_real, right_imag):
    return (
        left_real * right_real - left_imag * right_imag,
        left_real * right_imag + left_imag * right_real,
    )


def edge_grads(src_rows, rel_rows, dst_rows, neg_rows, live_mask):
    width = src_rows.shape[1] // 2
    src_float = src_rows.astype(jnp.float32)
    rel_float = rel_rows.astype(jnp.float32)
    dst_float = dst_rows.astype(jnp.float32)
    src_real, src_imag = (src_float[:, :width], src_float[:, width:])
    rel_real, rel_imag = (rel_float[:, :width], rel_float[:, width:])
    prod_real, prod_imag = complex_mul(src_real, src_imag, rel_real, rel_imag)
    product = jnp.concatenate([prod_real, prod_imag], axis=1)
    product_low = product.astype(jnp.bfloat16)
    positive = jnp.sum(product * dst_float, axis=1)
    negative = lax.dot_general(
        product_low, neg_rows, (((1,), (1,)), ((), ())), preferred_element_type=jnp.float32
    )
    peak_score = jnp.maximum(positive, jnp.max(negative, axis=1))
    exp_positive = jnp.exp(positive - peak_score)
    exp_negative = jnp.exp(negative - peak_score[:, None])
    total_mass = exp_positive + jnp.sum(exp_negative, axis=1)
    g_positive = live_mask * (exp_positive / total_mass - 1.0)
    weights = (live_mask[:, None] * exp_negative / total_mass[:, None]).astype(jnp.bfloat16)
    g_pool = lax.dot_general(
        weights, product_low, (((0,), (0,)), ((), ())), preferred_element_type=jnp.float32
    )
    g_product = g_positive[:, None] * dst_float + jnp.dot(
        weights, neg_rows, preferred_element_type=jnp.float32
    )
    grad_real, grad_imag = (g_product[:, :width], g_product[:, width:])
    source_real, source_imag = complex_mul(grad_real, grad_imag, rel_real, -rel_imag)
    relation_real, relation_imag = complex_mul(grad_real, grad_imag, src_real, -src_imag)
    g_source = jnp.concatenate([source_real, source_imag], axis=1)
    g_relation = jnp.concatenate([relation_real, relation_imag], axis=1)
    g_target = g_positive[:, None] * product
    return (g_source, g_relation, g_target, g_pool)


def shards(entities, hot_entities, relations, src_ids, rel_ids, dst_ids, neg_ids, counts, hot_slot):
    ent_rows = entities.shape[0]
    width_all = entities.shape[1]
    slot_total = src_ids.shape[3]
    src_table = src_ids.reshape(BUCKETS, slot_total)
    rel_table = rel_ids.reshape(BUCKETS, slot_total)
    dst_table = dst_ids.reshape(BUCKETS, slot_total)
    neg_table = neg_ids.reshape(BUCKETS, neg_ids.shape[3])
    count_table = counts.reshape(BUCKETS)
    slot_index = jnp.arange(slot_total, dtype=jnp.int32)
    totals = (
        jnp.zeros((ent_rows, width_all), jnp.float32),
        jnp.zeros(relations.shape, jnp.float32),
        jnp.zeros(hot_entities.shape, jnp.float32),
    )
    start_block = passed_along(entities, "blk", -HALF)
    held_block = start_block
    bucket_list = list(range(BUCKETS))
    walk_totals = totals
    carried = None
    for position, bucket in enumerate(bucket_list):
        if position > 0:
            held_block = passed_along(held_block, "blk", 1)
        bucket_source_total, bucket_relation_total, bucket_hot_total = walk_totals
        live_mask = (slot_index < count_table[bucket]).astype(jnp.float32)
        neg_pool = jnp.concatenate([held_block, hot_entities], axis=0)
        src_local = src_table[bucket]
        rel_local = rel_table[bucket]
        dst_local = dst_table[bucket]
        neg_local = neg_table[bucket]
        g_source, g_relation, g_target, g_pool = edge_grads(
            entities[src_local],
            relations[rel_local],
            held_block[dst_local],
            neg_pool[neg_local],
            live_mask,
        )
        pool_grad = jnp.zeros((neg_pool.shape[0], width_all), jnp.float32).at[neg_local].add(g_pool)
        held_grad = pool_grad[:ent_rows].at[dst_local].add(g_target)
        bucket_source_total = bucket_source_total.at[src_local].add(g_source)
        bucket_relation_total = bucket_relation_total.at[rel_local].add(g_relation)
        bucket_hot_total = bucket_hot_total + pool_grad[ent_rows:]
        held_grad, walk_totals = (
            held_grad,
            (bucket_source_total, bucket_relation_total, bucket_hot_total),
        )
        if carried is None:
            carried = held_grad
        else:
            carried = passed_along(carried, "blk", 1) + held_grad
    returned = passed_along(carried, "blk", HALF - bucket_list[-1])
    returned, totals = (returned, walk_totals)
    source_total, relation_total, hot_total = totals
    entity_grad = lax.psum(source_total + returned, "rep")
    relation_grad = lax.psum(relation_total, ("blk", "rep"))
    by_owner = jnp.zeros(hot_total.shape, jnp.float32).at[hot_slot].set(hot_total)
    hot_grad = lax.psum_scatter(by_owner, ("blk", "rep"), scatter_dimension=0, tiled=True)
    return (entity_grad, relation_grad, hot_grad)


def solution(mesh):
    return jax.shard_map(
        shards,
        mesh=mesh,
        in_specs=(
            P("blk", None),
            P(),
            P(),
            P("blk", "rep", None, None),
            P("blk", "rep", None, None),
            P("blk", "rep", None, None),
            P("blk", "rep", None, None),
            P("blk", "rep", None),
            P(),
        ),
        out_specs=(P("blk", None), P(), P(("blk", "rep"), None)),
        check_vma=False,
    )
```

profile of v0, /device:TPU:2, one launch (start us, length us, event | category | flops | bytes accessed | tf_op | source)
XLA Modules:
  0.0 539.3 jit_solution(7532300201263800990)
XLA Ops:
  8.4 9.4 %collective-permute-start = (bf16[512,400]{1,0:T(8,128)(2,1)S(1)}, bf16[512,400]{1,0:T(8,128)(2,1)S(1)}, u32[]{:S(2)}, u32[]{:S(2)}) collective-permute-start(bf16[512,400]{1,0:T(8,128)(2,1)S(1)} %copy.65), channel_id=1, source_target_pairs={{0,254},{2,0},{4,2},{6,4},{8,6},{10,8},{12,10},{14,12},{16,14},{18... | collective-permute-start | bytes 1228808 | tf_op jit(solution)/shard_map/ppermute | solution.py:13
  24.3 6.0 %copy.67 = bf16[4096,400]{1,0:T(8,128)(2,1)} copy(bf16[4096,400]{0,1:T(8,128)(2,1)} %param.11) | data formatting | bytes 6553600 | tf_op args[2]
  30.3 3.9 gather_fusion.1
  36.9 4.1 gather_fusion.5
  44.5 4.1 gather_fusion.9
  52.0 4.5 collective-permute-done.2
  64.7 6.3 %collective-permute-done.4 = bf16[512,400]{1,0:T(8,128)(2,1)} collective-permute-done((bf16[512,400]{1,0:T(8,128)(2,1)S(1)}, bf16[512,400]{1,0:T(8,128)(2,1)}, u32[]{:S(2)}, u32[]{:S(2)}) %collective-permute-start.4) | collective-permute-done | bytes 409632 | tf_op jit(solution)/shard_map/ppermute | solution.py:13
  71.0 3.3 pad_maximum_fusion
  74.3 4.4 gather_fusion.6
  83.7 2.8 gather_fusion.2
  95.5 6.1 %scatter_custom_fusion = f32[1536,400]{1,0:T(8,128)} fusion(s32[512]{0:T(512)} %bitcast.67, f32[512,400]{1,0:T(8,128)} %fusion.26, f32[]{:T(128)} %constant.8.clone.1), kind=kCustom, calls=%fused_computation.38 | custom fusion | flops 204800 | bytes 2458112 | tf_op jit(solution)/shard_map/scatter-add | solution.py:95
  106.9 2.8 fusion.17
  115.8 6.0 %scatter_custom_fusion.2 = f32[1536,400]{1,0:T(8,128)} fusion(s32[512]{0:T(512)} %bitcast.65, f32[512,400]{1,0:T(8,128)} %fusion.30, f32[]{:T(128)} %constant.8.clone.1), kind=kCustom, calls=%fused_computation.36 | custom fusion | flops 204800 | bytes 2458112 | tf_op jit(solution)/shard_map/scatter-add | solution.py:95
  129.1 2.8 scatter_fusion.1
  138.0 6.1 %scatter_custom_fusion.4 = f32[1536,400]{1,0:T(8,128)} fusion(s32[512]{0:T(512)} %bitcast.63, f32[512,400]{1,0:T(8,128)} %fusion.34, f32[]{:T(128)} %constant.8.clone.1), kind=kCustom, calls=%fused_computation.34 | custom fusion | flops 204800 | bytes 2458112 | tf_op jit(solution)/shard_map/scatter-add | solution.py:95
  145.0 6.3 %collective-permute-done.3 = f32[512,400]{0,1:T(8,128)} collective-permute-done((f32[512,400]{0,1:T(8,128)}, f32[512,400]{0,1:T(8,128)}, u32[]{:S(2)}, u32[]{:S(2)}) %collective-permute-start.3) | collective-permute-done | bytes 819232 | tf_op jit(solution)/shard_map/ppermute | solution.py:13
  163.6 5.7 %collective-permute-done.5 = f32[512,400]{0,1:T(8,128)} collective-permute-done((f32[512,400]{0,1:T(8,128)}, f32[512,400]{0,1:T(8,128)}, u32[]{:S(2)}, u32[]{:S(2)}) %collective-permute-start.5) | collective-permute-done | bytes 819232 | tf_op jit(solution)/shard_map/ppermute | solution.py:13
  186.6 7.5 %scatter_custom_fusion.12 = f32[1024,400]{1,0:T(8,128)} fusion(s32[1024]{0:T(1024)} %compare_select_fusion.3, f32[1536,400]{1,0:T(8,128)} %scatter_custom_fusion.4, f32[1536,400]{1,0:T(8,128)} %scatter_custom_fusion.2, f32[1536,400]{1,0:T(8,128)S(1)} %copy-done.3, f32[]{:T(128)} %constant.8.clone.1), kind=kCustom, calls=%fused_computation.28 | custom fusion | flops 819200 | bytes 7930368 | tf_op jit(solution)/shard_map/scatter | solution.py:113
  194.1 6.3 %scatter_custom_fusion.9 = f32[4096,400]{1,0:T(8,128)} fusion(s32[256]{0:T(256)} %bitcast.69, f32[256,400]{1,0:T(8,128)} %copy.99, f32[]{:T(128)} %constant.8.clone.1), kind=kCustom, calls=%fused_computation.25 | custom fusion | flops 102400 | bytes 6554112 | tf_op jit(solution)/shard_map/scatter-add | solution.py:98
  200.4 8.8 %scatter_fusion.6 = f32[4096,400]{1,0:T(8,128)} fusion(f32[4096,400]{1,0:T(8,128)} %scatter_custom_fusion.9, s32[256]{0:T(256)S(1)} %bitcast.49, f32[256,400]{1,0:T(8,128)S(1)} %copy-done.15), kind=kCustom, calls=%fused_computation.22 | custom fusion | flops 102400 | bytes 1229824 | tf_op jit(solution)/shard_map/scatter-add | solution.py:98
  209.2 8.6 %scatter_fusion.7 = f32[4096,400]{1,0:T(8,128)} fusion(f32[4096,400]{1,0:T(8,128)} %scatter_fusion.6, s32[256]{0:T(256)S(1)} %bitcast.47, f32[256,400]{1,0:T(8,128)S(1)} %copy-done.14), kind=kCustom, calls=%fused_computation.23 | custom fusion | flops 102400 | bytes 1229824 | tf_op jit(solution)/shard_map/scatter-add | solution.py:98
  217.9 11.6 %all-reduce.5.cloned.1.call-done = f32[512,400]{1,0:T(8,128)} async-done(((f32[512,400]{1,0:T(8,128)}), f32[512,400]{1,0:T(8,128)}) %all-reduce.5.cloned.1.call-update) | async-done | bytes 819216 | tf_op jit(solution)/shard_map/psum | solution.py:111
  231.9 290.6 %all-reduce.7.cloned.1.call-done = (f32[4096,400]{1,0:T(8,128)}, f32[1024,400]{1,0:T(8,128)}) async-done(((f32[4096,400]{1,0:T(8,128)}, f32[1024,400]{1,0:T(8,128)}), (f32[4096,400]{1,0:T(8,128)}, f32[1024,400]{1,0:T(8,128)})) %all-reduce.7.cloned.1.call-update) | async-done | bytes 8192016 | tf_op jit(solution)/shard_map/psum | solution.py:112
  522.4 8.5 %copy.103 = f32[4096,400]{0,1:T(8,128)} copy(f32[4096,400]{1,0:T(8,128)} %get-tuple-element.12) | data formatting | bytes 13107200
  (249 shorter events, 97.6 us)
Async XLA Ops:
  7.2 222.3 %all-reduce.5.cloned.1.call-start = ((), (), s32[]{:S(2)}) async-start(), calls=%async_computation | async-start | bytes 2097152 | tf_op jit(solution)/shard_map/psum | solution.py:111
  8.4 33.6 %collective-permute-start = (bf16[512,400]{1,0:T(8,128)(2,1)S(1)}, bf16[512,400]{1,0:T(8,128)(2,1)S(1)}, u32[]{:S(2)}, u32[]{:S(2)}) collective-permute-start(bf16[512,400]{1,0:T(8,128)(2,1)S(1)} %copy.65), channel_id=1, source_target_pairs={{0,254},{2,0},{4,2},{6,4},{8,6},{10,8},{12,10},{14,12},{16,14},{18... | collective-permute-start | bytes 1228808 | tf_op jit(solution)/shard_map/ppermute | solution.py:13
  22.9 18.3 %copy-start.60 = (s32[512,1]{0,1:T(1,128)}, s32[512,1]{0,1:T(1,128)S(1)}, u32[]{:S(2)}) copy-start(s32[512,1]{0,1:T(1,128)S(1)} %get-tuple-element.42) | copy-start | bytes 6148
  22.9 27.5 %copy-start.58 = (s32[512,1]{0,1:T(1,128)}, s32[512,1]{0,1:T(1,128)S(1)}, u32[]{:S(2)}) copy-start(s32[512,1]{0,1:T(1,128)S(1)} %get-tuple-element.41) | copy-start | bytes 6148
  23.0 37.2 %copy-start.59 = (s32[512,1]{0,1:T(1,128)}, s32[512,1]{0,1:T(1,128)S(1)}, u32[]{:S(2)}) copy-start(s32[512,1]{0,1:T(1,128)S(1)} %get-tuple-element.43) | copy-start | bytes 6148
  34.5 27.5 %copy-start.29 = (f32[256,200]{0,1:T(8,128)}, f32[256,200]{0,1:T(8,128)S(1)}, u32[]{:S(2)}) copy-start(f32[256,200]{0,1:T(8,128)S(1)} %get-tuple-element.33) | copy-start | bytes 614404
  34.5 27.5 %copy-start.31 = (f32[256,200]{0,1:T(8,128)}, f32[256,200]{0,1:T(8,128)S(1)}, u32[]{:S(2)}) copy-start(f32[256,200]{0,1:T(8,128)S(1)} %get-tuple-element.34) | copy-start | bytes 614404
  42.0 22.0 %copy-start.25 = (f32[256,200]{0,1:T(8,128)}, f32[256,200]{0,1:T(8,128)S(1)}, u32[]{:S(2)}) copy-start(f32[256,200]{0,1:T(8,128)S(1)} %get-tuple-element.31) | copy-start | bytes 614404
  42.0 22.0 %copy-start.27 = (f32[256,200]{0,1:T(8,128)}, f32[256,200]{0,1:T(8,128)S(1)}, u32[]{:S(2)}) copy-start(f32[256,200]{0,1:T(8,128)S(1)} %get-tuple-element.32) | copy-start | bytes 614404
  42.0 18.7 %copy-start.1 = (bf16[512,400]{1,0:T(8,128)(2,1)}, bf16[512,400]{1,0:T(8,128)(2,1)S(1)}, u32[]{:S(2)}) copy-start(bf16[512,400]{1,0:T(8,128)(2,1)S(1)} %collective-permute-done) | copy-start | bytes 1228804
  42.0 14.4 %collective-permute-start.2 = (bf16[512,400]{1,0:T(8,128)(2,1)S(1)}, bf16[512,400]{1,0:T(8,128)(2,1)S(1)}, u32[]{:S(2)}, u32[]{:S(2)}) collective-permute-start(bf16[512,400]{1,0:T(8,128)(2,1)S(1)} %collective-permute-done), channel_id=1, source_target_pairs={{0,2},{2,4},{4,6},{6,8},{8,10},{10,12},{12,14},{14,16},{16,18},{18... | collective-permute-start | bytes 1228808 | tf_op jit(solution)/shard_map/ppermute | solution.py:13
  44.5 15.6 %copy-start.10 = (f32[256,400]{0,1:T(8,128)}, f32[256,400]{0,1:T(8,128)S(1)}, u32[]{:S(2)}) copy-start(f32[256,400]{0,1:T(8,128)S(1)} %convert_element_type.79) | copy-start | bytes 1228804
  50.4 12.3 %copy-start.12 = (f32[256,400]{0,1:T(8,128)}, f32[256,400]{0,1:T(8,128)S(1)}, u32[]{:S(2)}) copy-start(f32[256,400]{0,1:T(8,128)S(1)} %convert_element_type.80) | copy-start | bytes 1228804
  56.4 14.6 %collective-permute-start.4 = (bf16[512,400]{1,0:T(8,128)(2,1)S(1)}, bf16[512,400]{1,0:T(8,128)(2,1)}, u32[]{:S(2)}, u32[]{:S(2)}) collective-permute-start(bf16[512,400]{1,0:T(8,128)(2,1)S(1)} %collective-permute-done.2), channel_id=1, source_target_pairs={{0,2},{2,4},{4,6},{6,8},{8,10},{10,12},{12,14},{14,16},{16,18},{18... | collective-permute-start | bytes 1228808 | tf_op jit(solution)/shard_map/ppermute | solution.py:13
  106.7 19.4 %collective-permute-start.1 = (f32[512,400]{0,1:T(8,128)}, f32[512,400]{0,1:T(8,128)}, u32[]{:S(2)}, u32[]{:S(2)}) collective-permute-start(f32[512,400]{0,1:T(8,128)} %copy.74), channel_id=1, source_target_pairs={{0,2},{2,4},{4,6},{6,8},{8,10},{10,12},{12,14},{14,16},{16,18},{18... | collective-permute-start | bytes 2457608 | tf_op jit(solution)/shard_map/ppermute | solution.py:13
  133.1 18.2 %collective-permute-start.3 = (f32[512,400]{0,1:T(8,128)}, f32[512,400]{0,1:T(8,128)}, u32[]{:S(2)}, u32[]{:S(2)}) collective-permute-start(f32[512,400]{0,1:T(8,128)} %copy.84), channel_id=1, source_target_pairs={{0,2},{2,4},{4,6},{6,8},{8,10},{10,12},{12,14},{14,16},{16,18},{18... | collective-permute-start | bytes 2457608 | tf_op jit(solution)/shard_map/ppermute | solution.py:13
  136.5 7.6 %copy-start.11 = (f32[256,400]{0,1:T(8,128)S(1)}, f32[256,400]{0,1:T(8,128)}, u32[]{:S(2)}) copy-start(f32[256,400]{0,1:T(8,128)} %copy-done.10) | copy-start | bytes 1228804
  136.5 7.6 %copy-start.13 = (f32[256,400]{0,1:T(8,128)S(1)}, f32[256,400]{0,1:T(8,128)}, u32[]{:S(2)}) copy-start(f32[256,400]{0,1:T(8,128)} %copy-done.12) | copy-start | bytes 1228804
  144.1 10.1 %copy-start.49 = (s32[256,1]{0,1:T(1,128)S(1)}, s32[256,1]{0,1:T(1,128)}, u32[]{:S(2)}) copy-start(s32[256,1]{0,1:T(1,128)} %copy-done.48) | copy-start | bytes 3076
  157.9 11.3 %collective-permute-start.5 = (f32[512,400]{0,1:T(8,128)}, f32[512,400]{0,1:T(8,128)}, u32[]{:S(2)}, u32[]{:S(2)}) collective-permute-start(f32[512,400]{0,1:T(8,128)} %copy.94), channel_id=1, source_target_pairs={{0,254},{2,0},{4,2},{6,4},{8,6},{10,8},{12,10},{14,12},{16,14},{18... | collective-permute-start | bytes 2457608 | tf_op jit(solution)/shard_map/ppermute | solution.py:13
  161.2 9.5 %copy-start.47 = (s32[256,1]{0,1:T(1,128)S(1)}, s32[256,1]{0,1:T(1,128)}, u32[]{:S(2)}) copy-start(s32[256,1]{0,1:T(1,128)} %copy-done.46) | copy-start | bytes 3076
  179.5 343.0 %all-reduce.7.cloned.1.call-start = ((), (), s32[]{:S(2)}) async-start(), calls=%async_computation.1 | async-start | bytes 20971520 | tf_op jit(solution)/shard_map/psum | solution.py:112
  200.4 8.8 %copy-start.14 = (f32[256,400]{1,0:T(8,128)S(1)}, f32[256,400]{1,0:T(8,128)}, u32[]{:S(2)}) copy-start(f32[256,400]{1,0:T(8,128)} %copy.101) | copy-start | bytes 1228804
  200.4 8.8 %copy-start.39 = (s32[256,1]{0,1:T(1,128)S(1)}, s32[256,1]{0,1:T(1,128)}, u32[]{:S(2)}) copy-start(s32[256,1]{0,1:T(1,128)} %copy-done.38) | copy-start | bytes 3076
  (52 other events, 205.0 us)
Sparse Core Ops, SparseCore 0:
  179.6 49.8 all-reduce.4
  236.6 285.7 all-reduce.6
where the time goes:
time: 548 us; the launch traced here: 539 us
  waiting for transfers between devices  325 us (59%)
  other arithmetic  99.6 us (18%)
  local copies, waits for them, and re-layouts  72.3 us (13%)
  matrix products  15.7 us (3%)
  between operations  15.4 us (3%)
  starting transfers between devices  11.5 us (2%)
    psum x1, waiting for transfers between devices, shards(): relation_grad = lax.psum(relation_total, ('blk', 'rep'))  291 us
    scatter-add x3, other arithmetic, shards(): bucket_relation_total = bucket_relation_total.at[rel_local].add(g_relation)  23.7 us
    unnamed x142, local copies, waits for them, and re-layouts  23.4 us
    ppermute x6, waiting for transfers between devices, passed_along(): return lax.ppermute(value, axis, pairs)  22.7 us
    scatter-add x3, other arithmetic, shards(): jnp.zeros((neg_pool.shape[0], width_all), jnp.float32).at[neg_local]  18.2 us
    gather x6, local copies, waits for them, and re-layouts, shards(): relations[rel_local]  13.2 us
    psum x1, waiting for transfers between devices, shards(): entity_grad = lax.psum(source_total + returned, 'rep')  11.6 us
    ppermute x6, starting transfers between devices, passed_along(): return lax.ppermute(value, axis, pairs)  11.4 us
  transfers between devices with their start and end apart: 8, of which 6 were waited for; matrix products, arithmetic and copies ran while one was open for 22% of the time, Pallas kernels for 0%

commit v1 on v0

v1 whole, which is shorter than its diff:
```python
import functools
import jax
import jax.numpy as jnp
import numpy as np
from jax import lax
from jax.experimental import pallas as pl
from jax.experimental.pallas import tpu as pltpu
from jax.sharding import Mesh, PartitionSpec as P

F32 = jnp.float32
BF16 = jnp.bfloat16
D = 400
HALF_D = 200
NREL = 4096
EDGES = 256
NEG = 512
ENT = 512
HOT = 1024
PLANE = 16
DEPTH = 8
LANES = 128
REL_ROWS = D + 16
HOT_BASE = 6 * REL_ROWS
HOT_BLOCKS = 4
MSG_ROWS = HOT_BASE + HOT_BLOCKS * 512
SLAB = D + HOT_BLOCKS * 32
Z_REL = 64
Z_ROWS = Z_REL + 16
BLK = ("y", "xh", "z", "core")
YX = ("y", "xh", "rep")


def onehot(rows, ids):
    grid = lax.broadcasted_iota(jnp.int32, (rows, ids.shape[1]), 0)
    return jnp.where(grid == ids, 1.0, 0.0).astype(BF16)


def dot(a, b):
    return lax.dot_general(a, b, (((1,), (0,)), ((), ())), preferred_element_type=F32)


def dot_nt(a, b):
    return lax.dot_general(a, b, (((1,), (1,)), ((), ())), preferred_element_type=F32)


def to_column(row):
    return jnp.transpose(jnp.broadcast_to(row, (8, row.shape[1])))[:, :1]


def to_row(column):
    return jnp.transpose(jnp.broadcast_to(column, (column.shape[0], LANES)))[:1]


def halves(value):
    return value[:HALF_D], value[HALF_D:]


def complex_product(left, right):
    lr, li = halves(left)
    rr, ri = halves(right)
    return jnp.concatenate([lr * rr - li * ri, lr * ri + li * rr], axis=0)


def conj_product(left, right):
    lr, li = halves(left)
    rr, ri = halves(right)
    return jnp.concatenate([lr * rr + li * ri, li * rr - lr * ri], axis=0)


def bucket_grads(src, rel, low, low_t, far, hot, hot_scores, dst, neg, count):
    src = src.astype(F32)
    rel = rel.astype(F32)
    product = complex_product(src, rel)
    dst_hot = onehot(ENT, dst)
    target = dot(far, dst_hot)
    positive = to_column(jnp.sum(product * target, axis=0, keepdims=True))
    neg_hot = onehot(ENT + HOT, neg)
    times = dot_nt(jnp.ones((8, NEG), BF16), neg_hot)[:1]
    bias = jnp.where(times > 0.0, jnp.log(jnp.maximum(times, 1.0)), -1e30)
    score_far = dot(low_t, far) + bias[:, :ENT]
    score_hot = hot_scores + bias[:, ENT:]
    peak = jnp.maximum(
        jnp.max(score_far, axis=1, keepdims=True), jnp.max(score_hot, axis=1, keepdims=True)
    )
    peak = jnp.maximum(peak, positive)
    exp_far = jnp.exp(score_far - peak)
    exp_hot = jnp.exp(score_hot - peak)
    exp_positive = jnp.exp(positive - peak)
    total = (
        exp_positive
        + jnp.sum(exp_far, axis=1, keepdims=True)
        + jnp.sum(exp_hot, axis=1, keepdims=True)
    )
    live = jnp.where(lax.broadcasted_iota(jnp.int32, (EDGES, 1), 0) < count, 1.0, 0.0)
    g_positive = to_row(live * (exp_positive / total - 1.0))
    scale = live / total
    w_far = (exp_far * scale).astype(BF16)
    w_hot = (exp_hot * scale).astype(BF16)
    g_product = g_positive * target + dot_nt(far, w_far) + dot_nt(hot, w_hot)
    g_source = conj_product(g_product, rel).astype(BF16)
    g_relation = conj_product(g_product, src).astype(BF16)
    g_target = (g_positive * product).astype(BF16)
    g_far = dot(low, w_far) + dot_nt(g_target, dst_hot)
    g_hot = dot(low, w_hot)
    return g_source, g_relation, g_far, g_hot


def front_kernel(
    rel_ref, own_ref, hot_ref, src_ref, rid_ref, dst_ref, neg_ref, count_ref,
    src_out, rel_out, low_out, low_t_out, score_out, gs_out, gr_out, own_out, ghot_out, acc,
):
    chunk = 512
    rel_ids = rid_ref[...]
    acc[...] = jnp.zeros_like(acc)

    def gather(i, carry):
        base = pl.multiple_of(i * chunk, chunk)
        acc[...] += dot(rel_ref[:, pl.ds(base, chunk)], onehot(chunk, rel_ids - base))
        return carry

    lax.fori_loop(0, NREL // chunk, gather, 0)
    rel = acc[...]
    src = dot(own_ref[...], onehot(ENT, src_ref[...]))
    low = complex_product(src, rel).astype(BF16)
    low_t = jnp.transpose(low.astype(F32)).astype(BF16)
    src = src.astype(BF16)
    rel = rel.astype(BF16)
    src_out[...] = src
    rel_out[...] = rel
    low_out[...] = low
    low_t_out[...] = low_t
    hot = hot_ref[...]
    scores = dot(low_t, hot)
    score_out[...] = scores
    mid = slice(EDGES, 2 * EDGES)
    g_source, g_relation, g_far, g_hot = bucket_grads(
        src[:, mid], rel[:, mid], low[:, mid], low_t[mid], own_ref[...], hot, scores[mid],
        dst_ref[:, mid], neg_ref[:, NEG : 2 * NEG], count_ref[1],
    )
    gs_out[...] = g_source
    gr_out[...] = g_relation
    own_out[...] = g_far
    ghot_out[...] = g_hot


def back_kernel(
    next_ref, prev_ref, hot_ref, src_ref, rel_ref, low_ref, low_t_ref, score_ref,
    gs_ref, gr_ref, own_ref, ghot_ref, sid_ref, rid_ref, dst_ref, neg_ref, slot_ref, count_ref, core_ref,
    msg_out, hot_out, own_out, next_out, prev_out,
):
    hot = hot_ref[...]
    sources = [None, gs_ref[...], None]
    relations = [None, gr_ref[...], None]
    g_hot = ghot_ref[...]
    for k, far_ref, far_out in ((0, next_ref, next_out), (2, prev_ref, prev_out)):
        part = slice(k * EDGES, (k + 1) * EDGES)
        g_source, g_relation, g_far, g_hot_k = bucket_grads(
            src_ref[:, part], rel_ref[:, part], low_ref[:, part], low_t_ref[part], far_ref[...],
            hot, score_ref[part], dst_ref[:, part], neg_ref[:, k * NEG : (k + 1) * NEG], count_ref[k],
        )
        sources[k] = g_source
        relations[k] = g_relation
        far_out[...] = g_far.astype(BF16)
        g_hot = g_hot + g_hot_k
    own_out[...] = own_ref[...] + dot_nt(
        jnp.concatenate(sources, axis=1), onehot(ENT, sid_ref[...])
    )
    rel_ids = rid_ref[...]
    place = lax.broadcasted_iota(jnp.int32, (16, LANES), 0)
    for b in range(6):
        ids = rel_ids[:, b * LANES : (b + 1) * LANES]
        high = jnp.right_shift(ids, 6).astype(F32)
        low = jnp.bitwise_and(ids, 63).astype(F32)
        tail = jnp.where(place == 0, high, jnp.where(place == 1, low, 0.0)).astype(BF16)
        piece = relations[b // 2][:, (b % 2) * LANES : (b % 2 + 1) * LANES]
        msg_out[b * REL_ROWS : b * REL_ROWS + D, :] = piece
        msg_out[b * REL_ROWS + D : (b + 1) * REL_ROWS, :] = tail
    slot = slot_ref[...]
    owner = jnp.right_shift(slot, 2)
    spot = (
        jnp.bitwise_and(jnp.right_shift(owner, 1), 1) * 512
        + (jnp.right_shift(owner, 5) * 2 + jnp.bitwise_and(owner, 1)) * 32
        + jnp.bitwise_and(jnp.right_shift(owner, 2), 7) * 4
        + jnp.bitwise_and(slot, 3)
    )
    g_hot = g_hot.astype(BF16)
    core = core_ref[0]
    for base, out, first in ((core * 512, hot_out, 0), ((1 - core) * 512, msg_out, HOT_BASE)):
        rows = dot_nt(onehot(512, spot - base), g_hot).astype(BF16)
        for b in range(HOT_BLOCKS):
            start = first + b * 512
            if b < 3:
                out[start : start + 512, :] = rows[:, b * LANES : (b + 1) * LANES]
            else:
                out[start : start + 512, :] = jnp.concatenate(
                    [rows[:, 3 * LANES :], jnp.zeros((512, HOT_BLOCKS * LANES - D), BF16)], axis=1
                )


def scatter_kernel(mine_ref, got_ref, hot_ref, core_ref, out_ref, grads, id_ref):
    for n, ref in enumerate((mine_ref, got_ref)):
        for b in range(6):
            col = (n * 6 + b) * LANES
            grads[:, col : col + LANES] = ref[b * REL_ROWS : b * REL_ROWS + D, :]
            tail = ref[b * REL_ROWS + D : (b + 1) * REL_ROWS, :].astype(F32)
            ids = tail[0:1] * 64.0 + tail[1:2]
            id_ref[:, col : col + LANES] = ids.astype(jnp.int32)
    first = core_ref[0] * (NREL // 2)

    def step(i, carry):
        hits = onehot(2 * LANES, id_ref[...] - (first + i * 2 * LANES))
        both = dot_nt(grads[...], hits).astype(BF16)
        out_ref[2 * i, :D, :] = both[:, :LANES]
        out_ref[2 * i + 1, :D, :] = both[:, LANES:]
        return carry

    lax.fori_loop(0, PLANE // 2, step, 0)
    for j in range(PLANE):
        for b in range(HOT_BLOCKS):
            row = b * 512 + j * 32
            added = hot_ref[row : row + 32, :].astype(F32) + got_ref[
                HOT_BASE + row : HOT_BASE + row + 32, :
            ].astype(F32)
            out_ref[j, D + b * 32 : D + (b + 1) * 32, :] = added.astype(BF16)


def plane_sum_kernel(in_ref, out_ref):
    total = in_ref[0].astype(F32)
    for j in range(1, PLANE):
        total = total + in_ref[j].astype(F32)
    for z in range(DEPTH):
        low = min(z * Z_REL, D)
        high = min(low + Z_REL, D)
        parts = []
        if high > low:
            parts.append(total[low:high])
        if high - low < Z_REL:
            parts.append(jnp.zeros((Z_REL - (high - low), LANES), F32))
        for b in range(HOT_BLOCKS):
            row = D + b * 32 + z * 4
            parts.append(total[row : row + 4])
        out_ref[z] = jnp.concatenate(parts, axis=0).astype(BF16)


def depth_sum_kernel(in_ref, rel_ref, hot_ref):
    total = in_ref[0].astype(F32)
    for z in range(1, DEPTH):
        total = total + in_ref[z].astype(F32)
    rel = total[:Z_REL].astype(BF16)
    for z in range(DEPTH):
        rel_ref[z] = rel
    for b in range(HOT_BLOCKS):
        width = min(LANES, D - b * LANES)
        hot_ref[:, b * LANES : b * LANES + width] = total[Z_REL + 4 * b : Z_REL + 4 * b + 4, :width]


def merge_kernel(core_ref, mine_ref, got_ref, out_ref):
    same = pl.program_id(0) == core_ref[0]
    for j in range(mine_ref.shape[0]):
        col = j * LANES

        @pl.when(same)
        def _():
            out_ref[:, col : col + LANES] = mine_ref[j].astype(F32)

        @pl.when(jnp.logical_not(same))
        def _():
            out_ref[:, col : col + LANES] = got_ref[j].astype(F32)


def struct(shape, dtype):
    return jax.ShapeDtypeStruct(shape, dtype)


PARAMS = pltpu.CompilerParams(vmem_limit_bytes=48 * 1024 * 1024)
VMEM = pl.BlockSpec(memory_space=pltpu.VMEM)
SMEM = pl.BlockSpec(memory_space=pltpu.SMEM)


def moved(value, axis, count, steps):
    return lax.ppermute(value, axis, [(i, (i + steps) % count) for i in range(count)])


def shards(entities, hot_entities, relations, src_ids, rel_ids, dst_ids, neg_ids, counts, hot_slot):
    blocks = lax.axis_size(BLK)
    own = entities.T
    hot = hot_entities.T
    rel = relations.T
    sid = src_ids.reshape(1, -1)
    rid = rel_ids.reshape(1, -1)
    did = dst_ids.reshape(1, -1)
    nid = neg_ids.reshape(1, -1)
    count = counts.reshape(-1)
    slot = hot_slot.reshape(1, -1)
    core = lax.axis_index("core").astype(jnp.int32).reshape(1)
    after = moved(own, BLK, blocks, -1)
    before = moved(own, BLK, blocks, 1)
    edges = sid.shape[1]
    src, relg, low, low_t, scores, gs, gr, own_grad, ghot = pl.pallas_call(
        front_kernel,
        out_shape=(
            struct((D, edges), BF16), struct((D, edges), BF16), struct((D, edges), BF16),
            struct((edges, D), BF16), struct((edges, HOT), F32),
            struct((D, EDGES), BF16), struct((D, EDGES), BF16), struct((D, ENT), F32),
            struct((D, HOT), F32),
        ),
        in_specs=[VMEM] * 7 + [SMEM],
        out_specs=[VMEM] * 9,
        scratch_shapes=[pltpu.VMEM((D, edges), F32)],
        compiler_params=PARAMS,
        cost_estimate=pl.CostEstimate(flops=5 * 10**9, bytes_accessed=10**7, transcendentals=0),
        name="front",
    )(rel, own, hot, sid, rid, did, nid, count)
    msg, hot_mine, own_grad, next_grad, prev_grad = pl.pallas_call(
        back_kernel,
        out_shape=(
            struct((MSG_ROWS, LANES), BF16), struct((HOT_BLOCKS * 512, LANES), BF16),
            struct((D, ENT), F32), struct((D, ENT), BF16), struct((D, ENT), BF16),
        ),
        in_specs=[VMEM] * 17 + [SMEM] * 2,
        out_specs=[VMEM] * 5,
        compiler_params=PARAMS,
        cost_estimate=pl.CostEstimate(flops=4 * 10**9, bytes_accessed=10**7, transcendentals=0),
        name="back",
    )(after, before, hot, src, relg, low, low_t, scores, gs, gr, own_grad, ghot,
      sid, rid, did, nid, slot, count, core)
    swap = [(0, 1), (1, 0)]
    got = lax.ppermute(msg, "core", swap)
    from_prev = moved(next_grad, BLK, blocks, 1)
    from_next = moved(prev_grad, BLK, blocks, -1)
    slabs = pl.pallas_call(
        scatter_kernel,
        out_shape=struct((PLANE, SLAB, LANES), BF16),
        in_specs=[VMEM] * 3 + [SMEM],
        out_specs=VMEM,
        scratch_shapes=[pltpu.VMEM((D, 2 * edges), BF16), pltpu.VMEM((1, 2 * edges), jnp.int32)],
        compiler_params=PARAMS,
        cost_estimate=pl.CostEstimate(flops=2 * 10**9, bytes_accessed=10**7, transcendentals=0),
        name="spread",
    )(msg, got, hot_mine, core)
    slabs = lax.all_to_all(slabs, YX, 0, 0, tiled=True)
    pieces = pl.pallas_call(
        plane_sum_kernel,
        out_shape=struct((DEPTH, Z_ROWS, LANES), BF16),
        in_specs=[VMEM],
        out_specs=VMEM,
        compiler_params=PARAMS,
        name="plane_sum",
    )(slabs)
    pieces = lax.all_to_all(pieces, "z", 0, 0, tiled=True)
    column, hot_grad = pl.pallas_call(
        depth_sum_kernel,
        out_shape=(struct((DEPTH, Z_REL, LANES), BF16), struct((4, D), F32)),
        in_specs=[VMEM],
        out_specs=(VMEM, VMEM),
        compiler_params=PARAMS,
        name="depth_sum",
    )(pieces)
    column = lax.all_to_all(column, "z", 0, 0, tiled=True)
    column = column.reshape(DEPTH * Z_REL, LANES)[:D]
    mine = lax.all_to_all(
        jnp.broadcast_to(column[None], (PLANE, D, LANES)), YX, 0, 0, tiled=True
    )
    other = lax.ppermute(mine, "core", swap)
    group = 4
    relation_grad = pl.pallas_call(
        merge_kernel,
        out_shape=struct((D, NREL), F32),
        grid_spec=pltpu.PrefetchScalarGridSpec(
            num_scalar_prefetch=1,
            grid=(2, PLANE // group),
            in_specs=[
                pl.BlockSpec((group, D, LANES), lambda h, i, c: (i, 0, 0)),
                pl.BlockSpec((group, D, LANES), lambda h, i, c: (i, 0, 0)),
            ],
            out_specs=pl.BlockSpec((D, group * LANES), lambda h, i, c: (0, h * (PLANE // group) + i)),
        ),
        compiler_params=PARAMS,
        name="merge",
    )(core, mine, other)
    part = (own_grad + from_prev.astype(F32) + from_next.astype(F32)).astype(BF16)
    twin = lax.ppermute(part, "rep", swap)
    entity_grad = part.astype(F32) + twin.astype(F32)
    return entity_grad.T, relation_grad.T, hot_grad


def solution(mesh):
    inner = Mesh(mesh.devices.reshape(4, 2, 8, 2, 2), ("y", "xh", "z", "core", "rep"))
    return jax.shard_map(
        shards,
        mesh=inner,
        in_specs=(
            P(BLK, None),
            P(),
            P(),
            P(BLK, "rep", None, None),
            P(BLK, "rep", None, None),
            P(BLK, "rep", None, None),
            P(BLK, "rep", None, None),
            P(BLK, "rep", None),
            P(),
        ),
        out_specs=(P(BLK, None), P(), P(BLK + ("rep",), None)),
        check_vma=False,
    )
```

time: 548 us -> 157 us (0.29); the launches traced: 539 us -> 157 us
  waiting for transfers between devices: 325 us -> 15.3 us
  other arithmetic: 99.6 us -> 1.22 us
  blocking collectives: 0 us -> 81.5 us
  local copies, waits for them, and re-layouts: 72.3 us -> 7.94 us
  Pallas kernels: 0 us -> 31.7 us
  matrix products: 15.7 us -> 0 us
  between operations: 15.4 us -> 0.75 us
  starting transfers between devices: 11.5 us -> 18.4 us
    psum x2 -> x0, waiting for transfers between devices: 302 us -> none  [the longest x1 291 us: shards(): relation_grad = lax.psum(relation_total, ('blk', 'rep'))]
    all_to_all x0 -> x4, blocking collectives: none -> 81.5 us  [the longest x1 32.4 us: shards(): slabs = lax.all_to_all(slabs, YX, 0, 0, tiled=True)]
    scatter-add x12 -> x0, other arithmetic: 57.5 us -> none  [the longest x3 23.7 us: shards(): bucket_relation_total = bucket_relation_total.at[rel_local].add(g_relation)]
    gather x21 -> x0, local copies, waits for them, and re-layouts: 32.1 us -> none  [the longest x6 13.2 us: shards(): relations[rel_local]]
    pallas_call x0 -> x6, Pallas kernels: none -> 31.7 us  [the longest x1 12 us: shards(): pl.pallas_call(front_kernel, out_shape=(struct((D, edges), BF16), struct(...]
    dot_general x9 -> x0, matrix products: 15.7 us -> none  [the longest x3 6.37 us: edge_grads(): jnp.dot(weights, neg_rows, preferred_element_type=jnp.float32)]
    unnamed x142 -> x30, local copies, waits for them, and re-layouts: 23.4 us -> 7.72 us
    scatter x1 -> x0, other arithmetic: 7.48 us -> none  [shards(): jnp.zeros(hot_total.shape, jnp.float32).at[hot_slot].set(hot_total)]
  transfers between devices with their start and end apart: 8 -> 7, of which waited for: 6 -> 3; matrix products, arithmetic and copies ran while one was open for 22% -> 1% of each run, Pallas kernels for 0% -> 8%
where the time goes in v1:
time: 157 us
  blocking collectives  81.5 us (52%)
  Pallas kernels  31.7 us (20%)
  starting transfers between devices  18.4 us (12%)
  waiting for transfers between devices  15.3 us (10%)
  local copies, waits for them, and re-layouts  7.94 us (5%)
    all_to_all x1, blocking collectives, shards(): slabs = lax.all_to_all(slabs, YX, 0, 0, tiled=True)  32.4 us
    all_to_all x1, blocking collectives, shards(): lax.all_to_all(jnp.broadcast_to(column[None], (PLANE, D, LANES)), YX, 0,...  23.5 us
    ppermute x4, starting transfers between devices, moved(): lax.ppermute(value, axis, [(i, (i + steps) % count) for i in range(count)])  16.9 us
    all_to_all x1, blocking collectives, shards(): pieces = lax.all_to_all(pieces, 'z', 0, 0, tiled=True)  14.2 us
    pallas_call x1, Pallas kernels, shards(): pl.pallas_call(front_kernel, out_shape=(struct((D, edges), BF16), struct(...  12 us
    all_to_all x1, blocking collectives, shards(): column = lax.all_to_all(column, 'z', 0, 0, tiled=True)  11.4 us
    pallas_call x1, Pallas kernels, shards(): pl.pallas_call(back_kernel, out_shape=(struct((MSG_ROWS, LANES), BF16), s...  10.1 us
    unnamed x30, local copies, waits for them, and re-layouts  7.72 us
  transfers between devices with their start and end apart: 7, of which 3 were waited for; matrix products, arithmetic and copies ran while one was open for 1% of the time, Pallas kernels for 8%

profile of v1, /device:TPU:2, one launch (start us, length us, event | category | flops | bytes accessed | tf_op | source)
XLA Modules:
  0.0 156.8 jit_solution(11098024674276648461)
XLA Ops:
  0.7 9.4 %collective-permute-start = (bf16[400,512]{1,0:T(8,128)(2,1)}, bf16[400,512]{1,0:T(8,128)(2,1)S(1)}, u32[]{:S(2)}, u32[]{:S(2)}) collective-permute-start(bf16[400,512]{1,0:T(8,128)(2,1)} %bitcast.17), channel_id=1, source_target_pairs={{0,254},{2,0},{4,2},{6,4},{8,6},{10,8},{12,10},{14,12},{16,14},{18... | collective-permute-start | bytes 1228808 | tf_op jit(solution)/shard_map/ppermute | solution.py:281
  10.1 1.1 copy-done.1
  11.3 1.0 copy-done.2
  12.3 0.7 copy-done.3
  12.9 0.7 copy-done.6
  13.6 0.7 copy-done.8
  14.3 0.7 copy-done.10
  15.0 0.7 copy-done.12
  15.7 12.0 %front.1 = (bf16[400,768]{1,0:T(8,128)(2,1)S(1)}, bf16[400,768]{1,0:T(8,128)(2,1)S(1)}, bf16[400,768]{1,0:T(8,128)(2,1)S(1)}, bf16[768,400]{1,0:T(8,128)(2,1)S(1...) custom-call(bf16[400,4096]{1,0:T(8,128)(2,1)} %bitcast.32, ...), custom_call_target="tpu_custom_call" | custom-call | flops 5000000000 | bytes 10000000 | tf_op jit(solution)/shard_map/front/pallas_call | solution.py:299
  27.7 0.9 copy-done.14
  28.6 10.1 %back.1 = (bf16[4544,128]{1,0:T(8,128)(2,1)}, bf16[2048,128]{1,0:T(8,128)(2,1)S(1)}, f32[400,512]{1,0:T(8,128)S(1)}, bf16[400,512]{1,0:T(8,128)(2,1)S(1)}, bf16[400,512]{1,0:T(8,128)(2,1)S(1)}) custom-call(bf16[400,512]{1,0:T(8,128)(2,1)S(1)} %collective-permute-done.next_ref, bf16[400,512]{1,0:T(8,128)(2,1)S(1)} %collective-permute-done.1.prev_ref, ...), custom_call_target="tpu_custom_call" | custom-call | flops 4000000000 | bytes 10000000 | tf_op jit(solution)/shard_map/back/pallas_call | solution.py:314
  38.7 3.0 %collective-permute-done.5.got_ref = bf16[4544,128]{1,0:T(8,128)(2,1)S(1)} collective-permute-done((bf16[4544,128]{1,0:T(8,128)(2,1)}, bf16[4544,128]{1,0:T(8,128)(2,1)S(1)}, u32[]{:S(2)}, u32[]{:S(2)}) %collective-permute-start.5) | collective-permute-done | bytes 1163296 | tf_op jit(solution)/shard_map/ppermute | solution.py:328
  41.7 1.3 copy-done
  43.0 4.5 %spread.1 = bf16[16,528,128]{2,1,0:T(8,128)(2,1)S(1)} custom-call(bf16[4544,128]{1,0:T(8,128)(2,1)S(1)} %copy-done, bf16[4544,128]{1,0:T(8,128)(2,1)S(1)} %collective-permute-done.5.got_ref, bf16[2048,128]{1,0:T(8,128)(2,1)S(1)} %get-tuple-element.32.hot_ref, s32[1]{0:T(128)} %bitcast.9.core_ref), custom_call_target="tpu_custom_call" | custom-call | flops 2000000000 | bytes 10000000 | tf_op jit(solution)/shard_map/spread/pallas_call | solution.py:331
  47.5 32.4 %all_to_all.20.in_ref = bf16[16,528,128]{2,1,0:T(8,128)(2,1)S(1)} all-to-all(bf16[16,528,128]{2,1,0:T(8,128)(2,1)S(1)} %spread.1), channel_id=1, replica_groups=mesh['y'=4,'xh'=2,'z'=8,'core'=2,'rep'=2] {'y','xh','rep'}, dimensions={0} | all-to-all | bytes 4325376 | tf_op jit(solution)/shard_map/all_to_all | solution.py:341
  80.1 14.2 %all_to_all.21.in_ref = bf16[8,80,128]{2,1,0:T(8,128)(2,1)S(1)} all-to-all(bf16[8,80,128]{2,1,0:T(8,128)(2,1)S(1)} %plane_sum.1), channel_id=1, replica_groups=mesh['y'=4,'xh'=2,'z'=8,'core'=2,'rep'=2] {'z'}, dimensions={0} | all-to-all | bytes 327680 | tf_op jit(solution)/shard_map/all_to_all | solution.py:350
  95.0 11.4 %all_to_all.22 = bf16[8,64,128]{2,1,0:T(8,128)(2,1)S(1)} all-to-all(bf16[8,64,128]{2,1,0:T(8,128)(2,1)S(1)} %get-tuple-element.33), channel_id=1, replica_groups=mesh['y'=4,'xh'=2,'z'=8,'core'=2,'rep'=2] {'z'}, dimensions={0} | all-to-all | bytes 262144 | tf_op jit(solution)/shard_map/all_to_all | solution.py:359
  106.6 23.5 %all_to_all.23.mine_ref = bf16[16,400,128]{2,1,0:T(8,128)(2,1)S(1)} all-to-all(bf16[16,400,128]{2,1,0:T(8,128)(2,1)S(1)} %broadcast_in_dim.2), channel_id=1, replica_groups=mesh['y'=4,'xh'=2,'z'=8,'core'=2,'rep'=2] {'y','xh','rep'}, dimensions={0} | all-to-all | bytes 3276800 | tf_op jit(solution)/shard_map/all_to_all | solution.py:361
  130.6 7.0 %collective-permute-start.3 = (bf16[400,512]{1,0:T(8,128)(2,1)S(1)}, bf16[400,512]{1,0:T(8,128)(2,1)S(1)}, u32[]{:S(2)}, u32[]{:S(2)}) collective-permute-start(bf16[400,512]{1,0:T(8,128)(2,1)S(1)} %get-tuple-element.30), channel_id=1, source_target_pairs={{0,254},{2,0},{4,2},{6,4},{8,6},{10,8},{12,10},{14,12},{16,14},{18... | collective-permute-start | bytes 1228808 | tf_op jit(solution)/shard_map/ppermute | solution.py:281
  137.6 5.7 %collective-permute-done.2 = bf16[400,512]{1,0:T(8,128)(2,1)S(1)} collective-permute-done((bf16[400,512]{1,0:T(8,128)(2,1)S(1)}, bf16[400,512]{1,0:T(8,128)(2,1)S(1)}, u32[]{:S(2)}, u32[]{:S(2)}) %collective-permute-start.2) | collective-permute-done | bytes 409632 | tf_op jit(solution)/shard_map/ppermute | solution.py:281
  143.5 1.5 collective-permute-start.4
  145.0 6.5 %collective-permute-done.4 = bf16[400,512]{1,0:T(8,128)(2,1)S(1)} collective-permute-done((bf16[400,512]{1,0:T(8,128)(2,1)S(1)}, bf16[400,512]{1,0:T(8,128)(2,1)S(1)}, u32[]{:S(2)}, u32[]{:S(2)}) %collective-permute-start.4) | collective-permute-done | bytes 409632 | tf_op jit(solution)/shard_map/ppermute | solution.py:382
  151.6 1.0 add_bitcast_fusion
  152.6 4.3 %merge.1 = f32[400,4096]{1,0:T(8,128)} custom-call(s32[1]{0:T(128)} %bitcast.9.core_ref, bf16[16,400,128]{2,1,0:T(8,128)(2,1)S(1)} %all_to_all.23.mine_ref, bf16[16,400,128]{2,1,0:T(8,128)(2,1)S(1)} %collective-permute-done.6.got_ref), custom_call_target="tpu_custom_call" | custom-call | tf_op jit(solution)/shard_map/merge/pallas_call | solution.py:366
  (34 shorter events, 2.0 us)
Async XLA Ops:
  0.6 27.9 %collective-permute-start.1 = (bf16[400,512]{1,0:T(8,128)(2,1)}, bf16[400,512]{1,0:T(8,128)(2,1)S(1)}, u32[]{:S(2)}, u32[]{:S(2)}) collective-permute-start(bf16[400,512]{1,0:T(8,128)(2,1)} %bitcast.16), channel_id=1, source_target_pairs={{0,2},{2,4},{4,6},{6,8},{8,10},{10,12},{12,14},{14,16},{16,18},{18... | collective-permute-start | bytes 1228808 | tf_op jit(solution)/shard_map/ppermute | solution.py:281
  0.7 27.8 %collective-permute-start = (bf16[400,512]{1,0:T(8,128)(2,1)}, bf16[400,512]{1,0:T(8,128)(2,1)S(1)}, u32[]{:S(2)}, u32[]{:S(2)}) collective-permute-start(bf16[400,512]{1,0:T(8,128)(2,1)} %bitcast.17), channel_id=1, source_target_pairs={{0,254},{2,0},{4,2},{6,4},{8,6},{10,8},{12,10},{14,12},{16,14},{18... | collective-permute-start | bytes 1228808 | tf_op jit(solution)/shard_map/ppermute | solution.py:281
  10.1 1.1 copy-start.1
  11.3 1.0 copy-start.2
  12.3 0.7 copy-start.3
  12.9 0.7 copy-start.6
  13.6 0.7 copy-start.8
  14.3 0.7 copy-start.10
  15.0 0.7 copy-start.12
  15.7 12.9 %copy-start.4 = (s32[1,1,3,512]{3,1,2,0:T(1,128)S(1)}, s32[1,1,3,512]{3,1,2,0:T(1,128)}, u32[]{:S(2)}) copy-start(s32[1,1,3,512]{3,1,2,0:T(1,128)} %param.15) | copy-start | bytes 18436
  15.7 12.9 %copy-start.5 = (s32[1024]{0:T(1024)S(1)}, s32[1024]{0:T(1024)}, u32[]{:S(2)}) copy-start(s32[1024]{0:T(1024)} %param.17) | copy-start | bytes 12292
  15.7 12.9 %copy-start.7 = (s32[1,1,3,256]{3,1,2,0:T(1,128)S(1)}, s32[1,1,3,256]{3,1,2,0:T(1,128)}, u32[]{:S(2)}) copy-start(s32[1,1,3,256]{3,1,2,0:T(1,128)} %param.12) | copy-start | bytes 9220
  15.7 12.9 %copy-start.9 = (s32[1,1,3,256]{3,1,2,0:T(1,128)S(1)}, s32[1,1,3,256]{3,1,2,0:T(1,128)}, u32[]{:S(2)}) copy-start(s32[1,1,3,256]{3,1,2,0:T(1,128)} %param.13) | copy-start | bytes 9220
  15.7 12.9 %copy-start.11 = (s32[1,1,3,256]{3,1,2,0:T(1,128)S(1)}, s32[1,1,3,256]{3,1,2,0:T(1,128)}, u32[]{:S(2)}) copy-start(s32[1,1,3,256]{3,1,2,0:T(1,128)} %param.14) | copy-start | bytes 9220
  15.7 12.9 %copy-start.13 = (s32[1,1,3]{2,1,0:T(1,128)S(1)}, s32[1,1,3]{2,1,0:T(1,128)}, u32[]{:S(2)}) copy-start(s32[1,1,3]{2,1,0:T(1,128)} %param.16) | copy-start | bytes 40
  27.7 0.9 copy-start.14
  38.7 3.0 %collective-permute-start.5 = (bf16[4544,128]{1,0:T(8,128)(2,1)}, bf16[4544,128]{1,0:T(8,128)(2,1)S(1)}, u32[]{:S(2)}, u32[]{:S(2)}) collective-permute-start(bf16[4544,128]{1,0:T(8,128)(2,1)} %get-tuple-element.31.mine_ref), channel_id=1, source_target_pairs={{0,2},{2,0},{1,3},{3,1},{4,6},{6,4},{5,7},{7,5},{8,10},{10,8},{9,1... | collective-permute-start | bytes 3489800 | tf_op jit(solution)/shard_map/ppermute | solution.py:328
  41.7 1.3 copy-start
  130.1 22.5 %collective-permute-start.6 = (bf16[16,400,128]{2,1,0:T(8,128)(2,1)S(1)}, bf16[16,400,128]{2,1,0:T(8,128)(2,1)S(1)}, u32[]{:S(2)}, u32[]{:S(2)}) collective-permute-start(bf16[16,400,128]{2,1,0:T(8,128)(2,1)S(1)} %all_to_all.23.mine_ref), channel_id=1, source_target_pairs={{0,2},{2,0},{1,3},{3,1},{4,6},{6,4},{5,7},{7,5},{8,10},{10,8},{9,1... | collective-permute-start | bytes 4915208 | tf_op jit(solution)/shard_map/ppermute | solution.py:364
  130.1 13.2 %collective-permute-start.2 = (bf16[400,512]{1,0:T(8,128)(2,1)S(1)}, bf16[400,512]{1,0:T(8,128)(2,1)S(1)}, u32[]{:S(2)}, u32[]{:S(2)}) collective-permute-start(bf16[400,512]{1,0:T(8,128)(2,1)S(1)} %get-tuple-element.29), channel_id=1, source_target_pairs={{0,2},{2,4},{4,6},{6,8},{8,10},{10,12},{12,14},{14,16},{16,18},{18... | collective-permute-start | bytes 1228808 | tf_op jit(solution)/shard_map/ppermute | solution.py:281
  130.6 12.7 %collective-permute-start.3 = (bf16[400,512]{1,0:T(8,128)(2,1)S(1)}, bf16[400,512]{1,0:T(8,128)(2,1)S(1)}, u32[]{:S(2)}, u32[]{:S(2)}) collective-permute-start(bf16[400,512]{1,0:T(8,128)(2,1)S(1)} %get-tuple-element.30), channel_id=1, source_target_pairs={{0,254},{2,0},{4,2},{6,4},{8,6},{10,8},{12,10},{14,12},{16,14},{18... | collective-permute-start | bytes 1228808 | tf_op jit(solution)/shard_map/ppermute | solution.py:281
  143.5 8.0 %collective-permute-start.4 = (bf16[400,512]{1,0:T(8,128)(2,1)S(1)}, bf16[400,512]{1,0:T(8,128)(2,1)S(1)}, u32[]{:S(2)}, u32[]{:S(2)}) collective-permute-start(bf16[400,512]{1,0:T(8,128)(2,1)S(1)} %add_convert_fusion), channel_id=1, source_target_pairs={{0,1},{1,0},{2,3},{3,2},{4,5},{5,4},{6,7},{7,6},{8,9},{9,8},{10,11... | collective-permute-start | bytes 1228808 | tf_op jit(solution)/shard_map/ppermute | solution.py:382

commit v2 on v1

v2 whole, which is shorter than its diff:
```python
import functools
import jax
import jax.numpy as jnp
import numpy as np
from jax import lax
from jax.experimental import pallas as pl
from jax.experimental.pallas import tpu as pltpu
from jax.sharding import Mesh, PartitionSpec as P

F32 = jnp.float32
BF16 = jnp.bfloat16
D = 400
HALF_D = 200
NREL = 4096
EDGES = 256
NEG = 512
ENT = 512
HOT = 1024
GROUP = 32
QUAD = 4
LANES = 128
REL_ROWS = D + 16
HOT_BASE = 6 * REL_ROWS
HOT_BLOCKS = 4
MSG_ROWS = HOT_BASE + HOT_BLOCKS * 512
TAIL = HALF_D
HOT_AT = HALF_D + 8
SLAB = HOT_AT + 3 * 16
PIECE = 224
PARTS = 4
SPREAD = 512
BLK = ("y", "xh", "zh", "zl", "core")
NEAR = ("y", "xh", "zl", "rep")


def onehot(rows, ids):
    grid = lax.broadcasted_iota(jnp.int32, (rows, ids.shape[1]), 0)
    return jnp.where(grid == ids, 1.0, 0.0).astype(BF16)


def dot(a, b):
    return lax.dot_general(a, b, (((1,), (0,)), ((), ())), preferred_element_type=F32)


def dot_nt(a, b):
    return lax.dot_general(a, b, (((1,), (1,)), ((), ())), preferred_element_type=F32)


def to_column(row):
    return jnp.transpose(jnp.broadcast_to(row, (8, row.shape[1])))[:, :1]


def to_row(column):
    return jnp.transpose(jnp.broadcast_to(column, (column.shape[0], LANES)))[:1]


def halves(value):
    return value[:HALF_D], value[HALF_D:]


def complex_product(left, right):
    lr, li = halves(left)
    rr, ri = halves(right)
    return jnp.concatenate([lr * rr - li * ri, lr * ri + li * rr], axis=0)


def conj_product(left, right):
    lr, li = halves(left)
    rr, ri = halves(right)
    return jnp.concatenate([lr * rr + li * ri, li * rr - lr * ri], axis=0)


def bucket_grads(src, rel, low, low_t, far, hot, hot_scores, dst, neg, count):
    src = src.astype(F32)
    rel = rel.astype(F32)
    product = complex_product(src, rel)
    dst_hot = onehot(ENT, dst)
    target = dot(far, dst_hot)
    positive = to_column(jnp.sum(product * target, axis=0, keepdims=True))
    table = dot_nt(
        onehot(16, jnp.right_shift(neg, 7)), onehot(LANES, jnp.bitwise_and(neg, LANES - 1))
    )
    times = jnp.concatenate(
        [table[i : i + 1] for i in range((ENT + HOT) // LANES)], axis=1
    )
    bias = jnp.where(times > 0.0, jnp.log(jnp.maximum(times, 1.0)), -1e30)
    score_far = dot(low_t, far) + bias[:, :ENT]
    score_hot = hot_scores + bias[:, ENT:]
    peak = jnp.maximum(
        jnp.max(score_far, axis=1, keepdims=True), jnp.max(score_hot, axis=1, keepdims=True)
    )
    peak = jnp.maximum(peak, positive)
    exp_far = jnp.exp(score_far - peak)
    exp_hot = jnp.exp(score_hot - peak)
    exp_positive = jnp.exp(positive - peak)
    total = (
        exp_positive
        + jnp.sum(exp_far, axis=1, keepdims=True)
        + jnp.sum(exp_hot, axis=1, keepdims=True)
    )
    live = jnp.where(lax.broadcasted_iota(jnp.int32, (EDGES, 1), 0) < count, 1.0, 0.0)
    g_positive = to_row(live * (exp_positive / total - 1.0))
    scale = live / total
    w_far = (exp_far * scale).astype(BF16)
    w_hot = (exp_hot * scale).astype(BF16)
    g_product = g_positive * target + dot_nt(far, w_far) + dot_nt(hot, w_hot)
    g_source = conj_product(g_product, rel).astype(BF16)
    g_relation = conj_product(g_product, src).astype(BF16)
    g_target = (g_positive * product).astype(BF16)
    g_hot = dot(low, w_hot)
    return g_source, g_relation, g_target, w_far, g_hot


def lookup_kernel(rel_hbm, rid_ref, rel_out, acc, rel_ref, sems):
    chunk = NREL // PARTS
    copies = []
    for i in range(PARTS):
        part = pl.ds(i * chunk, chunk)
        copies.append(
            pltpu.make_async_copy(rel_hbm.at[:, part], rel_ref.at[:, part], sems.at[i])
        )
    for copy in copies:
        copy.start()
    rel_ids = rid_ref[...]
    for i in range(PARTS):
        base = i * chunk
        hits = onehot(chunk, rel_ids - base)
        copies[i].wait()
        found = dot(rel_ref[:, base : base + chunk], hits)
        if i == 0:
            acc[...] = found
        elif i < PARTS - 1:
            acc[...] += found
        else:
            rel_out[...] = (acc[...] + found).astype(BF16)


def front_kernel(
    rel_ref, own_ref, hot_ref, src_ref, dst_ref, neg_ref, count_ref,
    src_out, low_out, low_t_out, score_out, gs_out, gr_out, gt_out, wf_out, ghot_out,
):
    rel = rel_ref[...]
    src = dot(own_ref[...], onehot(ENT, src_ref[...]))
    low = complex_product(src, rel.astype(F32)).astype(BF16)
    low_t = jnp.transpose(low.astype(F32)).astype(BF16)
    src = src.astype(BF16)
    src_out[...] = src
    low_out[...] = low
    low_t_out[...] = low_t
    hot = hot_ref[...]
    scores = dot(low_t, hot)
    score_out[...] = scores
    mid = slice(EDGES, 2 * EDGES)
    g_source, g_relation, g_target, w_far, g_hot = bucket_grads(
        src[:, mid], rel[:, mid], low[:, mid], low_t[mid], own_ref[...], hot, scores[mid],
        dst_ref[:, mid], neg_ref[:, NEG : 2 * NEG], count_ref[1],
    )
    gs_out[...] = g_source
    gr_out[...] = g_relation
    gt_out[...] = g_target
    wf_out[...] = w_far
    ghot_out[...] = g_hot


def back_kernel(
    next_ref, prev_ref, hot_ref, src_ref, rel_ref, low_ref, low_t_ref, score_ref,
    gr_ref, ghot_ref, rid_ref, dst_ref, neg_ref, slot_ref, count_ref, core_ref,
    msg_out, all_out, hot_out, gs0_out, gs2_out, gt0_out, gt2_out, wf0_out, wf2_out,
):
    hot = hot_ref[...]
    relations = [None, gr_ref[...], None]
    g_hot = ghot_ref[...]
    for k, far_ref, gs_out, gt_out, wf_out in (
        (0, next_ref, gs0_out, gt0_out, wf0_out),
        (2, prev_ref, gs2_out, gt2_out, wf2_out),
    ):
        part = slice(k * EDGES, (k + 1) * EDGES)
        g_source, g_relation, g_target, w_far, g_hot_k = bucket_grads(
            src_ref[:, part], rel_ref[:, part], low_ref[:, part], low_t_ref[part], far_ref[...],
            hot, score_ref[part], dst_ref[:, part], neg_ref[:, k * NEG : (k + 1) * NEG], count_ref[k],
        )
        relations[k] = g_relation
        gs_out[...] = g_source
        gt_out[...] = g_target
        wf_out[...] = w_far
        g_hot = g_hot + g_hot_k
    rel_ids = rid_ref[...]
    place = lax.broadcasted_iota(jnp.int32, (16, LANES), 0)
    for b in range(6):
        ids = rel_ids[:, b * LANES : (b + 1) * LANES]
        high = jnp.right_shift(ids, 6).astype(F32)
        low = jnp.bitwise_and(ids, 63).astype(F32)
        tail = jnp.where(place == 0, high, jnp.where(place == 1, low, 0.0)).astype(BF16)
        piece = relations[b // 2][:, (b % 2) * LANES : (b % 2 + 1) * LANES]
        msg_out[b * REL_ROWS : b * REL_ROWS + D, :] = piece
        all_out[:, b * LANES : (b + 1) * LANES] = piece
        msg_out[b * REL_ROWS + D : (b + 1) * REL_ROWS, :] = tail
    slot = slot_ref[...]
    owner = jnp.right_shift(slot, 2)
    spot = (
        jnp.bitwise_and(jnp.right_shift(owner, 1), 1) * 512
        + jnp.right_shift(owner, 5) * 64
        + jnp.bitwise_and(jnp.right_shift(owner, 2), 1) * 32
        + jnp.bitwise_and(owner, 1) * 16
        + jnp.bitwise_and(jnp.right_shift(owner, 3), 3) * 4
        + jnp.bitwise_and(slot, 3)
    )
    g_hot = g_hot.astype(BF16)
    core = core_ref[0]
    for base, out, first in ((core * 512, hot_out, 0), ((1 - core) * 512, msg_out, HOT_BASE)):
        rows = dot_nt(onehot(512, spot - base), g_hot).astype(BF16)
        for b in range(HOT_BLOCKS):
            start = first + b * 512
            if b < 3:
                out[start : start + 512, :] = rows[:, b * LANES : (b + 1) * LANES]
            else:
                out[start : start + 512, :] = jnp.concatenate(
                    [rows[:, 3 * LANES :], jnp.zeros((512, HOT_BLOCKS * LANES - D), BF16)], axis=1
                )


def tail_kernel(
    low_ref, gs0_ref, gs1_ref, gs2_ref, gt0_ref, gt1_ref, gt2_ref, wf0_ref, wf1_ref, wf2_ref,
    sid_ref, dst_ref, own_out, next_out, prev_out,
):
    ids = sid_ref[...]
    own = None
    for k, gs_ref, gt_ref, wf_ref, far_out in (
        (0, gs0_ref, gt0_ref, wf0_ref, next_out),
        (2, gs2_ref, gt2_ref, wf2_ref, prev_out),
        (1, gs1_ref, gt1_ref, wf1_ref, None),
    ):
        part = slice(k * EDGES, (k + 1) * EDGES)
        far = dot(low_ref[:, part], wf_ref[...]) + dot_nt(gt_ref[...], onehot(ENT, dst_ref[:, part]))
        near = dot_nt(gs_ref[...], onehot(ENT, ids[:, part]))
        own = near if own is None else own + near
        if far_out is None:
            own = own + far
        else:
            far_out[...] = far.astype(BF16)
    own_out[...] = own


def spread_kernel(grad_ref, rid_ref, got_ref, hot_ref, core_ref, out_ref, grads, id_ref, slabs, sems):
    edges = grad_ref.shape[1]
    grads[:, :edges] = grad_ref[...]
    id_ref[:, :edges] = rid_ref[...]
    for b in range(6):
        col = edges + b * LANES
        grads[:, col : col + LANES] = got_ref[b * REL_ROWS : b * REL_ROWS + D, :]
        tail = got_ref[b * REL_ROWS + D : (b + 1) * REL_ROWS, :].astype(F32)
        ids = tail[0:1] * 64.0 + tail[1:2]
        id_ref[:, col : col + LANES] = ids.astype(jnp.int32)
    ids = id_ref[...] - core_ref[0] * (NREL // 2)
    copies = []
    for i in range(NREL // 2 // SPREAD):
        wide = dot_nt(grads[...], onehot(SPREAD, ids - i * SPREAD))
        count = SPREAD // LANES
        for n in range(count):
            for zl in range(2):
                j = 2 * count * i + 4 * (n // 2) + 2 * zl + n % 2
                hot = []
                for b in range(HOT_BLOCKS):
                    row = b * 512 + j * 16
                    hot.append(
                        hot_ref[row : row + 16, :].astype(F32)
                        + got_ref[HOT_BASE + row : HOT_BASE + row + 16, :].astype(F32)
                    )
                last = hot.pop()
                tail = jnp.concatenate(
                    [last[:8, :16], last[8:, :16], jnp.zeros((8, LANES - 32), F32)], axis=1
                )
                piece = wide[zl * HALF_D : (zl + 1) * HALF_D, n * LANES : (n + 1) * LANES]
                slabs[j] = jnp.concatenate([piece, tail] + hot, axis=0).astype(BF16)
        part = pl.ds(2 * count * i, 2 * count)
        copy = pltpu.make_async_copy(slabs.at[part], out_ref.at[part], sems.at[i])
        copy.start()
        copies.append(copy)
    for copy in copies:
        copy.wait()


def near_sum_kernel(in_ref, out_ref):
    total = in_ref[0].astype(F32)
    for j in range(1, GROUP):
        total = total + in_ref[j].astype(F32)
    for zh in range(QUAD):
        parts = [total[:HALF_D]]
        for b in range(3):
            row = HOT_AT + b * 16 + zh * 4
            parts.append(total[row : row + 4])
        row, col = TAIL + (zh % 2) * 4, (zh // 2) * 16
        parts.append(
            jnp.concatenate(
                [total[row : row + 4, col : col + 16], jnp.zeros((4, LANES - 16), F32)], axis=1
            )
        )
        parts.append(jnp.zeros((PIECE - HALF_D - 16, LANES), F32))
        out_ref[zh] = jnp.concatenate(parts, axis=0).astype(BF16)


def quad_sum_kernel(in_ref, rel_ref, hot_ref):
    total = in_ref[0].astype(F32)
    for zh in range(1, QUAD):
        total = total + in_ref[zh].astype(F32)
    rel = total[:HALF_D].astype(BF16)
    for j in range(GROUP):
        rel_ref[j] = rel
    for b in range(HOT_BLOCKS):
        width = min(LANES, D - b * LANES)
        row = HALF_D + 4 * b
        hot_ref[:, b * LANES : b * LANES + width] = total[row : row + 4, :width]


def merge_kernel(core_ref, in_ref, *refs):
    out_ref = refs[-1]
    for near in range(2):
        for zl in range(2):
            for rep in range(2):
                col = (2 * near + rep) * LANES
                out_ref[zl * HALF_D : (zl + 1) * HALF_D, col : col + LANES] = in_ref[
                    4 * near + 2 * zl + rep
                ].astype(F32)


def merged(core, value, before):
    steps = GROUP // 8
    first = before is None
    if first:
        place = lambda i, c: (0, c[0] * steps + i)
    else:
        place = lambda i, c: (0, (1 - c[0]) * steps + i)
    in_specs = [pl.BlockSpec((8, HALF_D, LANES), lambda i, c: (i, 0, 0))]
    if not first:
        in_specs.append(pl.BlockSpec(memory_space=pl.ANY))
    return pl.pallas_call(
        merge_kernel,
        out_shape=struct((D, NREL), F32),
        grid_spec=pltpu.PrefetchScalarGridSpec(
            num_scalar_prefetch=1,
            grid=(steps,),
            in_specs=in_specs,
            out_specs=pl.BlockSpec((D, 4 * LANES), place),
        ),
        input_output_aliases={} if first else {2: 0},
        compiler_params=PARAMS,
        cost_estimate=pl.CostEstimate(flops=0, bytes_accessed=10**7, transcendentals=0),
        name="merge",
    )(core, value, *([] if first else [before]))


def struct(shape, dtype):
    return jax.ShapeDtypeStruct(shape, dtype)


PARAMS = pltpu.CompilerParams(vmem_limit_bytes=48 * 1024 * 1024)
VMEM = pl.BlockSpec(memory_space=pltpu.VMEM)
SMEM = pl.BlockSpec(memory_space=pltpu.SMEM)
HBM = pl.BlockSpec(memory_space=pltpu.HBM)


def moved(value, axis, count, steps):
    return lax.ppermute(value, axis, [(i, (i + steps) % count) for i in range(count)])


def shards(entities, hot_entities, relations, src_ids, rel_ids, dst_ids, neg_ids, counts, hot_slot):
    blocks = lax.axis_size(BLK)
    own = entities.T
    hot = hot_entities.T
    rel = relations.T
    sid = src_ids.reshape(1, -1)
    rid = rel_ids.reshape(1, -1)
    did = dst_ids.reshape(1, -1)
    nid = neg_ids.reshape(1, -1)
    count = counts.reshape(-1)
    slot = hot_slot.reshape(1, -1)
    core = lax.axis_index("core").astype(jnp.int32).reshape(1)
    after = moved(own, BLK, blocks, -1)
    before = moved(own, BLK, blocks, 1)
    edges = sid.shape[1]
    relg = pl.pallas_call(
        lookup_kernel,
        out_shape=struct((D, edges), BF16),
        in_specs=[HBM, VMEM],
        out_specs=VMEM,
        scratch_shapes=[
            pltpu.VMEM((D, edges), F32),
            pltpu.VMEM((D, NREL), BF16),
            pltpu.SemaphoreType.DMA((PARTS,)),
        ],
        compiler_params=PARAMS,
        cost_estimate=pl.CostEstimate(flops=3 * 10**9, bytes_accessed=10**7, transcendentals=0),
        name="lookup",
    )(rel, rid)
    half = struct((D, EDGES), BF16)
    weight = struct((EDGES, ENT), BF16)
    src, low, low_t, scores, gs1, gr, gt1, wf1, ghot = pl.pallas_call(
        front_kernel,
        out_shape=(
            struct((D, edges), BF16), struct((D, edges), BF16),
            struct((edges, D), BF16), struct((edges, HOT), F32),
            half, half, half, weight, struct((D, HOT), F32),
        ),
        in_specs=[VMEM] * 6 + [SMEM],
        out_specs=[VMEM] * 9,
        compiler_params=PARAMS,
        cost_estimate=pl.CostEstimate(flops=5 * 10**9, bytes_accessed=10**7, transcendentals=0),
        name="front",
    )(relg, own, hot, sid, did, nid, count)
    msg, grads, hot_mine, gs0, gs2, gt0, gt2, wf0, wf2 = pl.pallas_call(
        back_kernel,
        out_shape=(
            struct((MSG_ROWS, LANES), BF16), struct((D, edges), BF16),
            struct((HOT_BLOCKS * 512, LANES), BF16),
            half, half, half, half, weight, weight,
        ),
        in_specs=[VMEM] * 14 + [SMEM] * 2,
        out_specs=[VMEM] * 9,
        compiler_params=PARAMS,
        cost_estimate=pl.CostEstimate(flops=4 * 10**9, bytes_accessed=10**7, transcendentals=0),
        name="back",
    )(after, before, hot, src, relg, low, low_t, scores, gr, ghot,
      rid, did, nid, slot, count, core)
    own_grad, next_grad, prev_grad = pl.pallas_call(
        tail_kernel,
        out_shape=(struct((D, ENT), F32), struct((D, ENT), BF16), struct((D, ENT), BF16)),
        in_specs=[VMEM] * 12,
        out_specs=[VMEM] * 3,
        compiler_params=PARAMS,
        cost_estimate=pl.CostEstimate(flops=4 * 10**9, bytes_accessed=10**7, transcendentals=0),
        name="tail",
    )(low, gs0, gs1, gs2, gt0, gt1, gt2, wf0, wf1, wf2, sid, did)
    swap = [(0, 1), (1, 0)]
    got = lax.ppermute(msg, "core", swap)
    from_prev = moved(next_grad, BLK, blocks, 1)
    from_next = moved(prev_grad, BLK, blocks, -1)
    slabs = pl.pallas_call(
        spread_kernel,
        out_shape=struct((GROUP, SLAB, LANES), BF16),
        in_specs=[VMEM] * 4 + [SMEM],
        out_specs=HBM,
        scratch_shapes=[
            pltpu.VMEM((D, 2 * edges), BF16),
            pltpu.VMEM((1, 2 * edges), jnp.int32),
            pltpu.VMEM((GROUP, SLAB, LANES), BF16),
            pltpu.SemaphoreType.DMA((NREL // 2 // SPREAD,)),
        ],
        compiler_params=PARAMS,
        cost_estimate=pl.CostEstimate(flops=10**9, bytes_accessed=10**7, transcendentals=0),
        name="spread",
    )(grads, rid, got, hot_mine, core)
    slabs = lax.all_to_all(slabs, NEAR, 0, 0, tiled=True)
    part = (own_grad + from_prev.astype(F32) + from_next.astype(F32)).astype(BF16)
    slabs, part = lax.optimization_barrier((slabs, part))
    twin = lax.ppermute(part, "rep", swap)
    pieces = pl.pallas_call(
        near_sum_kernel,
        out_shape=struct((QUAD, PIECE, LANES), BF16),
        in_specs=[VMEM],
        out_specs=VMEM,
        compiler_params=PARAMS,
        name="near_sum",
    )(slabs)
    pieces = lax.all_to_all(pieces, "zh", 0, 0, tiled=True)
    pieces, twin = lax.optimization_barrier((pieces, twin))
    column, hot_grad = pl.pallas_call(
        quad_sum_kernel,
        out_shape=(struct((GROUP, HALF_D, LANES), BF16), struct((4, D), F32)),
        in_specs=[VMEM],
        out_specs=(VMEM, VMEM),
        compiler_params=PARAMS,
        name="quad_sum",
    )(pieces)
    mine = lax.all_to_all(column, NEAR, 0, 0, tiled=True)
    other = lax.ppermute(mine, "core", swap)
    relation_grad = merged(core, other, merged(core, mine, None))
    entity_grad = part.astype(F32) + twin.astype(F32)
    return entity_grad.T, relation_grad.T, hot_grad


def solution(mesh):
    inner = Mesh(mesh.devices.reshape(4, 2, 4, 2, 2, 2), BLK + ("rep",))
    return jax.shard_map(
        shards,
        mesh=inner,
        in_specs=(
            P(BLK, None),
            P(),
            P(),
            P(BLK, "rep", None, None),
            P(BLK, "rep", None, None),
            P(BLK, "rep", None, None),
            P(BLK, "rep", None, None),
            P(BLK, "rep", None),
            P(),
        ),
        out_specs=(P(BLK, None), P(), P(BLK + ("rep",), None)),
        check_vma=False,
    )
```

time: 157 us -> 133 us (0.85); the launches traced: 157 us -> 130 us
  blocking collectives: 81.5 us -> 43.6 us
  waiting for transfers between devices: 15.3 us -> 21.4 us
  starting transfers between devices: 18.4 us -> 23.8 us
  Pallas kernels: 31.7 us -> 30 us
  local copies, waits for them, and re-layouts: 7.94 us -> 9.61 us
    all_to_all x4 -> x2, blocking collectives: 81.5 us -> 43.6 us  [the longest x1 29.9 us: shards(): mine = lax.all_to_all(column, NEAR, 0, 0, tiled=True)]
    all_to_all x0 -> x1, waiting for transfers between devices: none -> 8.75 us  [shards(): slabs = lax.all_to_all(slabs, NEAR, 0, 0, tiled=True)]
    pallas_call x1, Pallas kernels: 12 us -> 4.98 us  [shards(): pl.pallas_call(front_kernel, out_shape=(struct((D, edges), BF16), struct(...]
    pallas_call x4 -> x7, Pallas kernels: 9.65 us -> 16.4 us  [the longest x1 6.01 us: shards(): pl.pallas_call(lookup_kernel, out_shape=struct((D, edges), BF16), in_spec...]
    ppermute x1, waiting for transfers between devices: 6.53 us -> 0.01 us  [shards(): twin = lax.ppermute(part, 'rep', swap)]
    all_to_all x0 -> x1, starting transfers between devices: none -> 5.11 us  [shards(): slabs = lax.all_to_all(slabs, NEAR, 0, 0, tiled=True)]
    ppermute x4, waiting for transfers between devices: 5.74 us -> 9.39 us  [moved(): lax.ppermute(value, axis, [(i, (i + steps) % count) for i in range(count)])]
    unnamed x30 -> x44, local copies, waits for them, and re-layouts: 7.72 us -> 9.61 us
  transfers between devices with their start and end apart: 7 -> 8, of which waited for: 3 -> 4; matrix products, arithmetic and copies ran while one was open for 1% -> 1% of each run, Pallas kernels for 8% -> 11%
where the time goes in v2:
time: 133 us; the launch traced here: 130 us
  blocking collectives  43.6 us (33%)
  Pallas kernels  30 us (23%)
  starting transfers between devices  23.8 us (18%)
  waiting for transfers between devices  21.4 us (16%)
  local copies, waits for them, and re-layouts  9.61 us (7%)
    all_to_all x1, blocking collectives, shards(): mine = lax.all_to_all(column, NEAR, 0, 0, tiled=True)  29.9 us
    ppermute x4, starting transfers between devices, moved(): lax.ppermute(value, axis, [(i, (i + steps) % count) for i in range(count)])  17 us
    all_to_all x1, blocking collectives, shards(): pieces = lax.all_to_all(pieces, 'zh', 0, 0, tiled=True)  13.7 us
    unnamed x44, local copies, waits for them, and re-layouts  9.61 us
    ppermute x4, waiting for transfers between devices, moved(): lax.ppermute(value, axis, [(i, (i + steps) % count) for i in range(count)])  9.39 us
    all_to_all x1, waiting for transfers between devices, shards(): slabs = lax.all_to_all(slabs, NEAR, 0, 0, tiled=True)  8.75 us
    pallas_call x1, Pallas kernels, shards(): pl.pallas_call(back_kernel, out_shape=(struct((MSG_ROWS, LANES), BF16), s...  8.64 us
    pallas_call x1, Pallas kernels, shards(): pl.pallas_call(lookup_kernel, out_shape=struct((D, edges), BF16), in_spec...  6.01 us
  transfers between devices with their start and end apart: 8, of which 4 were waited for; matrix products, arithmetic and copies ran while one was open for 1% of the time, Pallas kernels for 11%

profile of v2, /device:TPU:2, one launch (start us, length us, event | category | flops | bytes accessed | tf_op | source)
XLA Modules:
  0.0 130.4 jit_solution(4271409998255005465)
XLA Ops:
  0.7 9.4 %collective-permute-start = (bf16[400,512]{1,0:T(8,128)(2,1)}, bf16[400,512]{1,0:T(8,128)(2,1)S(1)}, u32[]{:S(2)}, u32[]{:S(2)}) collective-permute-start(bf16[400,512]{1,0:T(8,128)(2,1)} %bitcast.20), channel_id=1, source_target_pairs={{0,254},{2,0},{4,2},{6,4},{8,6},{10,8},{12,10},{14,12},{16,14},{18... | collective-permute-start | bytes 1228808 | tf_op jit(solution)/shard_map/ppermute | solution.py:363
  10.8 1.9 %copy-done.2 = bf16[4096,400]{0,1:T(8,128)(2,1)S(1)} copy-done((bf16[4096,400]{0,1:T(8,128)(2,1)S(1)}, bf16[4096,400]{0,1:T(8,128)(2,1)}, u32[]{:S(2)}) %copy-start.2) | copy-done | bytes 3276824
  12.7 6.0 %lookup.1.rel_ref = bf16[400,768]{1,0:T(8,128)(2,1)S(1)} custom-call(bf16[400,4096]{1,0:T(8,128)(2,1)S(1)} %bitcast.16, s32[1,768]{1,0:T(1,128)S(1)} %bitcast.13), custom_call_target="tpu_custom_call" | custom-call | flops 3000000000 | bytes 10000000 | tf_op jit(solution)/shard_map/lookup/pallas_call | solution.py:381
  18.9 5.0 %front.1 = (bf16[400,768]{1,0:T(8,128)(2,1)S(1)}, bf16[400,768]{1,0:T(8,128)(2,1)S(1)}, bf16[768,400]{1,0:T(8,128)(2,1)S(1)}, f32[768,1024]{1,0:T(8,128)}, bf16[...) custom-call(bf16[400,768]{1,0:T(8,128)(2,1)S(1)} %lookup.1.rel_ref, ...), custom_call_target="tpu_custom_call" | custom-call | flops 5000000000 | bytes 10000000 | tf_op jit(solution)/shard_map/front/pallas_call | solution.py:397
  24.5 8.6 %back.1 = (bf16[4544,128]{1,0:T(8,128)(2,1)}, bf16[400,768]{1,0:T(8,128)(2,1)S(1)}, bf16[2048,128]{1,0:T(8,128)(2,1)S(1)}, bf16[400,256]{1,0:T(8,128)(2,1)S(1)},...) custom-call(bf16[400,512]{1,0:T(8,128)(2,1)S(1)} %collective-permute, ...), custom_call_target="tpu_custom_call" | custom-call | flops 4000000000 | bytes 10000000 | tf_op jit(solution)/shard_map/back/pallas_call | solution.py:410
  33.9 3.0 %collective-permute-done.2.got_ref = bf16[4544,128]{1,0:T(8,128)(2,1)S(1)} collective-permute-done((bf16[4544,128]{1,0:T(8,128)(2,1)}, bf16[4544,128]{1,0:T(8,128)(2,1)S(1)}, u32[]{:S(2)}, u32[]{:S(2)}) %collective-permute-start.2) | collective-permute-done | bytes 1163296 | tf_op jit(solution)/shard_map/ppermute | solution.py:434
  36.9 3.6 %spread.1 = bf16[32,256,128]{2,1,0:T(8,128)(2,1)} custom-call(bf16[400,768]{1,0:T(8,128)(2,1)S(1)} %get-tuple-element.36.grad_ref, s32[1,768]{1,0:T(1,128)S(1)} %bitcast.15, bf16[4544,128]{1,0:T(8,128)(2,1)S(1)} %collective-permute-done.2.got_ref, bf16[2048,128]{1,0:T(8,128)(2,1)S(1)} %get-tuple-element.38.hot_ref, s32[1]{0:T(128)} %bitcast.9.core_ref), custom_call_target="tpu_custom_call" | custom-call | flops 1000000000 | bytes 10000000 | tf_op jit(solution)/shard_map/spread/pallas_call | solution.py:437
  40.5 5.1 %all-to-all-start = ((bf16[32,256,128]{2,1,0:T(8,128)(2,1)}), bf16[32,256,128]{2,1,0:T(8,128)(2,1)S(1)}, u32[]{:S(2)}, u32[]{:S(2)}) async-start(bf16[32,256,128]{2,1,0:T(8,128)(2,1)} %spread.1), calls=%async_computation | async-start | bytes 4194304 | tf_op jit(solution)/shard_map/all_to_all | solution.py:452
  45.7 0.9 copy-done.11
  46.6 0.9 copy-done.13
  47.5 0.9 copy-done.15
  48.5 0.9 copy-done.17
  49.4 0.9 copy-done.19
  50.3 0.9 copy-done.21
  51.3 1.1 tail.1
  52.5 7.5 %collective-permute-start.4 = (bf16[400,512]{1,0:T(8,128)(2,1)S(1)}, bf16[400,512]{1,0:T(8,128)(2,1)S(1)}, u32[]{:S(2)}, u32[]{:S(2)}) collective-permute-start(bf16[400,512]{1,0:T(8,128)(2,1)S(1)} %get-tuple-element.50), channel_id=1, source_target_pairs={{0,254},{2,0},{4,2},{6,4},{8,6},{10,8},{12,10},{14,12},{16,14},{18... | collective-permute-start | bytes 1228808 | tf_op jit(solution)/shard_map/ppermute | solution.py:363
  60.0 9.4 %collective-permute-done.3 = bf16[400,512]{1,0:T(8,128)(2,1)S(1)} collective-permute-done((bf16[400,512]{1,0:T(8,128)(2,1)S(1)}, bf16[400,512]{1,0:T(8,128)(2,1)S(1)}, u32[]{:S(2)}, u32[]{:S(2)}) %collective-permute-start.3) | collective-permute-done | bytes 409632 | tf_op jit(solution)/shard_map/ppermute | solution.py:363
  69.5 8.7 %all-to-all-done.in_ref = bf16[32,256,128]{2,1,0:T(8,128)(2,1)S(1)} async-done(((bf16[32,256,128]{2,1,0:T(8,128)(2,1)}), bf16[32,256,128]{2,1,0:T(8,128)(2,1)S(1)}, u32[]{:S(2)}, u32[]{:S(2)}) %all-to-all-start) | async-done | bytes 2097184 | tf_op jit(solution)/shard_map/all_to_all | solution.py:452
  78.3 1.7 %collective-permute-start.5 = (bf16[400,512]{1,0:T(8,128)(2,1)S(1)}, bf16[400,512]{1,0:T(8,128)(2,1)S(1)}, u32[]{:S(2)}, u32[]{:S(2)}) collective-permute-start(bf16[400,512]{1,0:T(8,128)(2,1)S(1)} %add_convert_fusion), channel_id=1, source_target_pairs={{0,1},{1,0},{2,3},{3,2},{4,5},{5,4},{6,7},{7,6},{8,9},{9,8},{10,11... | collective-permute-start | bytes 1228808 | tf_op jit(solution)/shard_map/ppermute | solution.py:455
  80.3 13.7 %all_to_all.15.in_ref = bf16[4,224,128]{2,1,0:T(8,128)(2,1)S(1)} all-to-all(bf16[4,224,128]{2,1,0:T(8,128)(2,1)S(1)} %near_sum.1), channel_id=1, replica_groups=mesh['y'=4,'xh'=2,'zh'=4,'zl'=2,'core'=2,'rep'=2] {'zh'}, dimensions={0} | all-to-all | bytes 458752 | tf_op jit(solution)/shard_map/all_to_all | solution.py:464
  94.8 29.9 %all_to_all.16.in_ref = bf16[32,200,128]{2,1,0:T(8,128)(2,1)S(1)} all-to-all(bf16[32,200,128]{2,1,0:T(8,128)(2,1)S(1)} %get-tuple-element.55), channel_id=1, replica_groups=mesh['y'=4,'xh'=2,'zh'=4,'zl'=2,'core'=2,'rep'=2] {'y','xh','zl','rep'}, dimensions={0} | all-to-all | bytes 3276800 | tf_op jit(solution)/shard_map/all_to_all | solution.py:474
  124.6 1.0 add_bitcast_fusion
  125.6 2.2 %merge.2.refs_0_ = f32[400,4096]{1,0:T(8,128)} custom-call(s32[1]{0:T(128)} %bitcast.9.core_ref, bf16[32,200,128]{2,1,0:T(8,128)(2,1)S(1)} %all_to_all.16.in_ref), custom_call_target="tpu_custom_call" | custom-call | bytes 10000000 | tf_op jit(solution)/shard_map/merge/pallas_call | solution.py:336
  128.1 2.2 %merge.3 = f32[400,4096]{1,0:T(8,128)} custom-call(s32[1]{0:T(128)} %bitcast.9.core_ref, bf16[32,200,128]{2,1,0:T(8,128)(2,1)S(1)} %collective-permute-done.6.in_ref, f32[400,4096]{1,0:T(8,128)} %merge.2.refs_0_), custom_call_target="tpu_custom_call", output_to_operand_aliasing={{}: (2, {})} | custom-call | bytes 10000000 | tf_op jit(solution)/shard_map/merge/pallas_call | solution.py:336
  (49 shorter events, 3.8 us)
Async XLA Ops:
  0.6 23.9 %collective-permute-start.1 = (bf16[400,512]{1,0:T(8,128)(2,1)}, bf16[400,512]{1,0:T(8,128)(2,1)S(1)}, u32[]{:S(2)}, u32[]{:S(2)}) collective-permute-start(bf16[400,512]{1,0:T(8,128)(2,1)} %bitcast.19), channel_id=1, source_target_pairs={{0,2},{2,4},{4,6},{6,8},{8,10},{10,12},{12,14},{14,16},{16,18},{18... | collective-permute-start | bytes 1228808 | tf_op jit(solution)/shard_map/ppermute | solution.py:363
  0.7 23.8 %collective-permute-start = (bf16[400,512]{1,0:T(8,128)(2,1)}, bf16[400,512]{1,0:T(8,128)(2,1)S(1)}, u32[]{:S(2)}, u32[]{:S(2)}) collective-permute-start(bf16[400,512]{1,0:T(8,128)(2,1)} %bitcast.20), channel_id=1, source_target_pairs={{0,254},{2,0},{4,2},{6,4},{8,6},{10,8},{12,10},{14,12},{16,14},{18... | collective-permute-start | bytes 1228808 | tf_op jit(solution)/shard_map/ppermute | solution.py:363
  10.8 1.9 %copy-start.2 = (bf16[4096,400]{0,1:T(8,128)(2,1)S(1)}, bf16[4096,400]{0,1:T(8,128)(2,1)}, u32[]{:S(2)}) copy-start(bf16[4096,400]{0,1:T(8,128)(2,1)} %param.11) | copy-start | bytes 9830404
  12.7 6.1 %copy-start.3 = (bf16[1024,400]{0,1:T(8,128)(2,1)S(1)}, bf16[1024,400]{0,1:T(8,128)(2,1)}, u32[]{:S(2)}) copy-start(bf16[1024,400]{0,1:T(8,128)(2,1)} %param.10) | copy-start | bytes 2457604
  12.7 6.1 %copy-start.4 = (bf16[512,400]{0,1:T(8,128)(2,1)S(1)}, bf16[512,400]{0,1:T(8,128)(2,1)}, u32[]{:S(2)}) copy-start(bf16[512,400]{0,1:T(8,128)(2,1)} %param.9) | copy-start | bytes 1228804
  12.7 6.1 %copy-start.5 = (s32[1,1,3,512]{3,1,2,0:T(1,128)S(1)}, s32[1,1,3,512]{3,1,2,0:T(1,128)}, u32[]{:S(2)}) copy-start(s32[1,1,3,512]{3,1,2,0:T(1,128)} %param.15) | copy-start | bytes 18436
  12.7 6.1 %copy-start.7 = (s32[1,1,3,256]{3,1,2,0:T(1,128)S(1)}, s32[1,1,3,256]{3,1,2,0:T(1,128)}, u32[]{:S(2)}) copy-start(s32[1,1,3,256]{3,1,2,0:T(1,128)} %param.12) | copy-start | bytes 9220
  12.7 6.1 %copy-start.8 = (s32[1,1,3,256]{3,1,2,0:T(1,128)S(1)}, s32[1,1,3,256]{3,1,2,0:T(1,128)}, u32[]{:S(2)}) copy-start(s32[1,1,3,256]{3,1,2,0:T(1,128)} %param.14) | copy-start | bytes 9220
  12.7 6.1 %copy-start.9 = (s32[1,1,3]{2,1,0:T(1,128)S(1)}, s32[1,1,3]{2,1,0:T(1,128)}, u32[]{:S(2)}) copy-start(s32[1,1,3]{2,1,0:T(1,128)} %param.16) | copy-start | bytes 40
  18.8 5.7 %copy-start.1 = (s32[1,1,3,256]{3,1,2,0:T(1,128)S(1)}, s32[1,1,3,256]{3,1,2,0:T(1,128)}, u32[]{:S(2)}) copy-start(s32[1,1,3,256]{3,1,2,0:T(1,128)} %param.13) | copy-start | bytes 9220
  18.8 5.7 %copy-start.6 = (s32[1024]{0:T(1024)S(1)}, s32[1024]{0:T(1024)}, u32[]{:S(2)}) copy-start(s32[1024]{0:T(1024)} %param.17) | copy-start | bytes 12292
  24.5 8.7 %copy-start.16 = (bf16[256,512]{1,0:T(8,128)(2,1)}, bf16[256,512]{1,0:T(8,128)(2,1)S(1)}, u32[]{:S(2)}) copy-start(bf16[256,512]{1,0:T(8,128)(2,1)S(1)} %get-tuple-element.46.wf1_ref) | copy-start | bytes 786436
  24.5 8.7 %copy-start.20 = (bf16[400,256]{1,0:T(8,128)(2,1)}, bf16[400,256]{1,0:T(8,128)(2,1)S(1)}, u32[]{:S(2)}) copy-start(bf16[400,256]{1,0:T(8,128)(2,1)S(1)} %get-tuple-element.43.gt1_ref) | copy-start | bytes 614404
  33.9 6.7 %copy-start.10 = (bf16[400,256]{1,0:T(8,128)(2,1)}, bf16[400,256]{1,0:T(8,128)(2,1)S(1)}, u32[]{:S(2)}) copy-start(bf16[400,256]{1,0:T(8,128)(2,1)S(1)} %get-tuple-element.41.gs2_ref) | copy-start | bytes 614404
  33.9 6.7 %copy-start.12 = (bf16[400,256]{1,0:T(8,128)(2,1)}, bf16[400,256]{1,0:T(8,128)(2,1)S(1)}, u32[]{:S(2)}) copy-start(bf16[400,256]{1,0:T(8,128)(2,1)S(1)} %get-tuple-element.42.gt0_ref) | copy-start | bytes 614404
  33.9 3.0 %collective-permute-start.2 = (bf16[4544,128]{1,0:T(8,128)(2,1)}, bf16[4544,128]{1,0:T(8,128)(2,1)S(1)}, u32[]{:S(2)}, u32[]{:S(2)}) collective-permute-start(bf16[4544,128]{1,0:T(8,128)(2,1)} %get-tuple-element.37), channel_id=1, source_target_pairs={{0,2},{2,0},{1,3},{3,1},{4,6},{6,4},{5,7},{7,5},{8,10},{10,8},{9,1... | collective-permute-start | bytes 3489800 | tf_op jit(solution)/shard_map/ppermute | solution.py:434
  40.5 37.7 %all-to-all-start = ((bf16[32,256,128]{2,1,0:T(8,128)(2,1)}), bf16[32,256,128]{2,1,0:T(8,128)(2,1)S(1)}, u32[]{:S(2)}, u32[]{:S(2)}) async-start(bf16[32,256,128]{2,1,0:T(8,128)(2,1)} %spread.1), calls=%async_computation | async-start | bytes 4194304 | tf_op jit(solution)/shard_map/all_to_all | solution.py:452
  45.7 0.9 copy-start.11
  46.6 0.9 copy-start.13
  48.5 0.9 copy-start.17
  52.4 16.9 %collective-permute-start.3 = (bf16[400,512]{1,0:T(8,128)(2,1)S(1)}, bf16[400,512]{1,0:T(8,128)(2,1)S(1)}, u32[]{:S(2)}, u32[]{:S(2)}) collective-permute-start(bf16[400,512]{1,0:T(8,128)(2,1)S(1)} %get-tuple-element.49), channel_id=1, source_target_pairs={{0,2},{2,4},{4,6},{6,8},{8,10},{10,12},{12,14},{14,16},{16,18},{18... | collective-permute-start | bytes 1228808 | tf_op jit(solution)/shard_map/ppermute | solution.py:363
  52.5 16.8 %collective-permute-start.4 = (bf16[400,512]{1,0:T(8,128)(2,1)S(1)}, bf16[400,512]{1,0:T(8,128)(2,1)S(1)}, u32[]{:S(2)}, u32[]{:S(2)}) collective-permute-start(bf16[400,512]{1,0:T(8,128)(2,1)S(1)} %get-tuple-element.50), channel_id=1, source_target_pairs={{0,254},{2,0},{4,2},{6,4},{8,6},{10,8},{12,10},{14,12},{16,14},{18... | collective-permute-start | bytes 1228808 | tf_op jit(solution)/shard_map/ppermute | solution.py:363
  78.3 15.8 %collective-permute-start.5 = (bf16[400,512]{1,0:T(8,128)(2,1)S(1)}, bf16[400,512]{1,0:T(8,128)(2,1)S(1)}, u32[]{:S(2)}, u32[]{:S(2)}) collective-permute-start(bf16[400,512]{1,0:T(8,128)(2,1)S(1)} %add_convert_fusion), channel_id=1, source_target_pairs={{0,1},{1,0},{2,3},{3,2},{4,5},{5,4},{6,7},{7,6},{8,9},{9,8},{10,11... | collective-permute-start | bytes 1228808 | tf_op jit(solution)/shard_map/ppermute | solution.py:455
  124.6 3.5 %collective-permute-start.6 = (bf16[32,200,128]{2,1,0:T(8,128)(2,1)S(1)}, bf16[32,200,128]{2,1,0:T(8,128)(2,1)S(1)}, u32[]{:S(2)}, u32[]{:S(2)}) collective-permute-start(bf16[32,200,128]{2,1,0:T(8,128)(2,1)S(1)} %all_to_all.16.in_ref), channel_id=1, source_target_pairs={{0,2},{2,0},{1,3},{3,1},{4,6},{6,4},{5,7},{7,5},{8,10},{10,8},{9,1... | collective-permute-start | bytes 4915208 | tf_op jit(solution)/shard_map/ppermute | solution.py:475
  (6 other events, 4.8 us)

commit v3 on v2

--- a/solution.py
+++ b/solution.py
@@ -27,7 +27,7 @@
 HOT_AT = HALF_D + 8
 SLAB = HOT_AT + 3 * 16
 PIECE = 224
-PARTS = 4
+WIDE = 256
 SPREAD = 512
 BLK = ("y", "xh", "zh", "zl", "core")
 NEAR = ("y", "xh", "zl", "rep")
@@ -70,7 +70,7 @@
     return jnp.concatenate([lr * rr + li * ri, li * rr - lr * ri], axis=0)
 
 
-def bucket_grads(src, rel, low, low_t, far, hot, hot_scores, dst, neg, count):
+def bucket_grads(src, rel, low, low_t, far, hot, dst, neg, count):
     src = src.astype(F32)
     rel = rel.astype(F32)
     product = complex_product(src, rel)
@@ -85,7 +85,7 @@
     )
     bias = jnp.where(times > 0.0, jnp.log(jnp.maximum(times, 1.0)), -1e30)
     score_far = dot(low_t, far) + bias[:, :ENT]
-    score_hot = hot_scores + bias[:, ENT:]
+    score_hot = dot(low_t, hot) + bias[:, ENT:]
     peak = jnp.maximum(
         jnp.max(score_far, axis=1, keepdims=True), jnp.max(score_hot, axis=1, keepdims=True)
     )
@@ -107,40 +107,23 @@
     g_source = conj_product(g_product, rel).astype(BF16)
     g_relation = conj_product(g_product, src).astype(BF16)
     g_target = (g_positive * product).astype(BF16)
-    g_hot = dot(low, w_hot)
-    return g_source, g_relation, g_target, w_far, g_hot
-
-
-def lookup_kernel(rel_hbm, rid_ref, rel_out, acc, rel_ref, sems):
-    chunk = NREL // PARTS
-    copies = []
-    for i in range(PARTS):
-        part = pl.ds(i * chunk, chunk)
-        copies.append(
-            pltpu.make_async_copy(rel_hbm.at[:, part], rel_ref.at[:, part], sems.at[i])
-        )
-    for copy in copies:
-        copy.start()
-    rel_ids = rid_ref[...]
-    for i in range(PARTS):
-        base = i * chunk
-        hits = onehot(chunk, rel_ids - base)
-        copies[i].wait()
-        found = dot(rel_ref[:, base : base + chunk], hits)
-        if i == 0:
-            acc[...] = found
-        elif i < PARTS - 1:
-            acc[...] += found
-        else:
-            rel_out[...] = (acc[...] + found).astype(BF16)
+    g_far = dot(low, w_far) + dot_nt(g_target, dst_hot)
+    return g_source, g_relation, g_far, w_hot
+
+
+def lookup_kernel(rel_ref, rid_ref, out_ref):
+    for start in range(0, rid_ref.shape[1], WIDE):
+        part = slice(start, start + WIDE)
+        out_ref[:, part] = dot(rel_ref[...], onehot(NREL, rid_ref[:, part])).astype(BF16)
 
 
 def front_kernel(
     rel_ref, own_ref, hot_ref, src_ref, dst_ref, neg_ref, count_ref,
-    src_out, low_out, low_t_out, score_out, gs_out, gr_out, gt_out, wf_out, ghot_out,
+    src_out, low_out, low_t_out, gr_out, own_out, wh_out,
 ):
     rel = rel_ref[...]
-    src = dot(own_ref[...], onehot(ENT, src_ref[...]))
+    places = onehot(ENT, src_ref[...])
+    src = dot(own_ref[...], places)
     low = complex_product(src, rel.astype(F32)).astype(BF16)
     low_t = jnp.transpose(low.astype(F32)).astype(BF16)
     src = src.astype(BF16)
@@ -148,42 +131,37 @@
     low_out[...] = low
     low_t_out[...] = low_t
     hot = hot_ref[...]
-    scores = dot(low_t, hot)
-    score_out[...] = scores
     mid = slice(EDGES, 2 * EDGES)
-    g_source, g_relation, g_target, w_far, g_hot = bucket_grads(
-        src[:, mid], rel[:, mid], low[:, mid], low_t[mid], own_ref[...], hot, scores[mid],
+    g_source, g_relation, g_far, w_hot = bucket_grads(
+        src[:, mid], rel[:, mid], low[:, mid], low_t[mid], own_ref[...], hot,
         dst_ref[:, mid], neg_ref[:, NEG : 2 * NEG], count_ref[1],
+    )
+    gr_out[...] = g_relation
+    own_out[...] = g_far + dot_nt(g_source, places[:, mid])
+    wh_out[...] = w_hot
+
+
+def back_kernel(
+    k, far_ref, hot_ref, src_ref, rel_ref, low_ref, low_t_ref, dst_ref, neg_ref, count_ref,
+    gs_out, gr_out, wh_out, far_out,
+):
+    part = slice(k * EDGES, (k + 1) * EDGES)
+    g_source, g_relation, g_far, w_hot = bucket_grads(
+        src_ref[:, part], rel_ref[:, part], low_ref[:, part], low_t_ref[part], far_ref[...],
+        hot_ref[...], dst_ref[:, part], neg_ref[:, k * NEG : (k + 1) * NEG], count_ref[k],
     )
     gs_out[...] = g_source
     gr_out[...] = g_relation
-    gt_out[...] = g_target
-    wf_out[...] = w_far
-    ghot_out[...] = g_hot
-
-
-def back_kernel(
-    next_ref, prev_ref, hot_ref, src_ref, rel_ref, low_ref, low_t_ref, score_ref,
-    gr_ref, ghot_ref, rid_ref, dst_ref, neg_ref, slot_ref, count_ref, core_ref,
-    msg_out, all_out, hot_out, gs0_out, gs2_out, gt0_out, gt2_out, wf0_out, wf2_out,
+    wh_out[...] = w_hot
+    far_out[...] = g_far.astype(BF16)
+
+
+def pack_kernel(
+    gr0_ref, gr1_ref, gr2_ref, wh0_ref, wh1_ref, wh2_ref, low_ref, rid_ref, slot_ref, core_ref,
+    msg_out, all_out, hot_out,
 ):
-    hot = hot_ref[...]
-    relations = [None, gr_ref[...], None]
-    g_hot = ghot_ref[...]
-    for k, far_ref, gs_out, gt_out, wf_out in (
-        (0, next_ref, gs0_out, gt0_out, wf0_out),
-        (2, prev_ref, gs2_out, gt2_out, wf2_out),
-    ):
-        part = slice(k * EDGES, (k + 1) * EDGES)
-        g_source, g_relation, g_target, w_far, g_hot_k = bucket_grads(
-            src_ref[:, part], rel_ref[:, part], low_ref[:, part], low_t_ref[part], far_ref[...],
-            hot, score_ref[part], dst_ref[:, part], neg_ref[:, k * NEG : (k + 1) * NEG], count_ref[k],
-        )
-        relations[k] = g_relation
-        gs_out[...] = g_source
-        gt_out[...] = g_target
-        wf_out[...] = w_far
-        g_hot = g_hot + g_hot_k
+    relations = [gr0_ref[...], gr1_ref[...], gr2_ref[...]]
+    weights = [wh0_ref[...], wh1_ref[...], wh2_ref[...]]
     rel_ids = rid_ref[...]
     place = lax.broadcasted_iota(jnp.int32, (16, LANES), 0)
     for b in range(6):
@@ -205,7 +183,7 @@
         + jnp.bitwise_and(jnp.right_shift(owner, 3), 3) * 4
         + jnp.bitwise_and(slot, 3)
     )
-    g_hot = g_hot.astype(BF16)
+    g_hot = dot(low_ref[...], jnp.concatenate(weights, axis=0)).astype(BF16)
     core = core_ref[0]
     for base, out, first in ((core * 512, hot_out, 0), ((1 - core) * 512, msg_out, HOT_BASE)):
         rows = dot_nt(onehot(512, spot - base), g_hot).astype(BF16)
@@ -219,26 +197,12 @@
                 )
 
 
-def tail_kernel(
-    low_ref, gs0_ref, gs1_ref, gs2_ref, gt0_ref, gt1_ref, gt2_ref, wf0_ref, wf1_ref, wf2_ref,
-    sid_ref, dst_ref, own_out, next_out, prev_out,
-):
+def tail_kernel(own_ref, gs0_ref, gs2_ref, sid_ref, own_out):
     ids = sid_ref[...]
-    own = None
-    for k, gs_ref, gt_ref, wf_ref, far_out in (
-        (0, gs0_ref, gt0_ref, wf0_ref, next_out),
-        (2, gs2_ref, gt2_ref, wf2_ref, prev_out),
-        (1, gs1_ref, gt1_ref, wf1_ref, None),
-    ):
-        part = slice(k * EDGES, (k + 1) * EDGES)
-        far = dot(low_ref[:, part], wf_ref[...]) + dot_nt(gt_ref[...], onehot(ENT, dst_ref[:, part]))
-        near = dot_nt(gs_ref[...], onehot(ENT, ids[:, part]))
-        own = near if own is None else own + near
-        if far_out is None:
-            own = own + far
-        else:
-            far_out[...] = far.astype(BF16)
-    own_out[...] = own
+    total = own_ref[...]
+    for k, gs_ref in ((0, gs0_ref), (2, gs2_ref)):
+        total = total + dot_nt(gs_ref[...], onehot(ENT, ids[:, k * EDGES : (k + 1) * EDGES]))
+    own_out[...] = total
 
 
 def spread_kernel(grad_ref, rid_ref, got_ref, hot_ref, core_ref, out_ref, grads, id_ref, slabs, sems):
@@ -353,7 +317,8 @@
     return jax.ShapeDtypeStruct(shape, dtype)
 
 
-PARAMS = pltpu.CompilerParams(vmem_limit_bytes=48 * 1024 * 1024)
+COST = pl.CostEstimate(flops=10**8, bytes_accessed=10**6, transcendentals=0)
+PARAMS = pltpu.CompilerParams(vmem_limit_bytes=28 * 1024 * 1024)
 VMEM = pl.BlockSpec(memory_space=pltpu.VMEM)
 SMEM = pl.BlockSpec(memory_space=pltpu.SMEM)
 HBM = pl.BlockSpec(memory_space=pltpu.HBM)
@@ -381,59 +346,67 @@
     relg = pl.pallas_call(
         lookup_kernel,
         out_shape=struct((D, edges), BF16),
-        in_specs=[HBM, VMEM],
+        in_specs=[VMEM, VMEM],
         out_specs=VMEM,
-        scratch_shapes=[
-            pltpu.VMEM((D, edges), F32),
-            pltpu.VMEM((D, NREL), BF16),
-            pltpu.SemaphoreType.DMA((PARTS,)),
-        ],
         compiler_params=PARAMS,
         cost_estimate=pl.CostEstimate(flops=3 * 10**9, bytes_accessed=10**7, transcendentals=0),
         name="lookup",
     )(rel, rid)
     half = struct((D, EDGES), BF16)
-    weight = struct((EDGES, ENT), BF16)
-    src, low, low_t, scores, gs1, gr, gt1, wf1, ghot = pl.pallas_call(
+    block = struct((D, ENT), BF16)
+    weight = struct((EDGES, HOT), BF16)
+    src, low, low_t, gr1, own_grad, wh1 = pl.pallas_call(
         front_kernel,
         out_shape=(
-            struct((D, edges), BF16), struct((D, edges), BF16),
-            struct((edges, D), BF16), struct((edges, HOT), F32),
-            half, half, half, weight, struct((D, HOT), F32),
+            struct((D, edges), BF16), struct((D, edges), BF16), struct((edges, D), BF16),
+            half, struct((D, ENT), F32), weight,
         ),
         in_specs=[VMEM] * 6 + [SMEM],
-        out_specs=[VMEM] * 9,
-        compiler_params=PARAMS,
-        cost_estimate=pl.CostEstimate(flops=5 * 10**9, bytes_accessed=10**7, transcendentals=0),
+        out_specs=[VMEM] * 6,
+        compiler_params=PARAMS,
+        cost_estimate=COST,
         name="front",
     )(relg, own, hot, sid, did, nid, count)
-    msg, grads, hot_mine, gs0, gs2, gt0, gt2, wf0, wf2 = pl.pallas_call(
-        back_kernel,
+
+    def back(k, far):
+        return pl.pallas_call(
+            functools.partial(back_kernel, k),
+            out_shape=(half, half, weight, block),
+            in_specs=[VMEM] * 8 + [SMEM],
+            out_specs=[VMEM] * 4,
+            compiler_params=PARAMS,
+            cost_estimate=COST,
+            name="back",
+        )(far, hot, src, relg, low, low_t, did, nid, count)
+
+    gs0, gr0, wh0, next_grad = back(0, after)
+    from_prev = moved(next_grad, BLK, blocks, 1)
+    gs2, gr2, wh2, prev_grad = back(2, before)
+    from_next = moved(prev_grad, BLK, blocks, -1)
+    msg, grads, hot_mine = pl.pallas_call(
+        pack_kernel,
         out_shape=(
             struct((MSG_ROWS, LANES), BF16), struct((D, edges), BF16),
             struct((HOT_BLOCKS * 512, LANES), BF16),
-            half, half, half, half, weight, weight,
         ),
-        in_specs=[VMEM] * 14 + [SMEM] * 2,
-        out_specs=[VMEM] * 9,
-        compiler_params=PARAMS,
-        cost_estimate=pl.CostEstimate(flops=4 * 10**9, bytes_accessed=10**7, transcendentals=0),
-        name="back",
-    )(after, before, hot, src, relg, low, low_t, scores, gr, ghot,
-      rid, did, nid, slot, count, core)
-    own_grad, next_grad, prev_grad = pl.pallas_call(
+        in_specs=[VMEM] * 9 + [SMEM],
+        out_specs=[VMEM] * 3,
+        compiler_params=PARAMS,
+        cost_estimate=COST,
+        name="pack",
+    )(gr0, gr1, gr2, wh0, wh1, wh2, low, rid, slot, core)
+    own_grad = pl.pallas_call(
         tail_kernel,
-        out_shape=(struct((D, ENT), F32), struct((D, ENT), BF16), struct((D, ENT), BF16)),
-        in_specs=[VMEM] * 12,
-        out_specs=[VMEM] * 3,
-        compiler_params=PARAMS,
-        cost_estimate=pl.CostEstimate(flops=4 * 10**9, bytes_accessed=10**7, transcendentals=0),
+        out_shape=struct((D, ENT), F32),
+        in_specs=[VMEM] * 4,
+        out_specs=VMEM,
+        compiler_params=PARAMS,
+        cost_estimate=COST,
         name="tail",
-    )(low, gs0, gs1, gs2, gt0, gt1, gt2, wf0, wf1, wf2, sid, did)
+    )(own_grad, gs0, gs2, sid)
     swap = [(0, 1), (1, 0)]
     got = lax.ppermute(msg, "core", swap)
-    from_prev = moved(next_grad, BLK, blocks, 1)
-    from_next = moved(prev_grad, BLK, blocks, -1)
+    got, own_grad = lax.optimization_barrier((got, own_grad))
     slabs = pl.pallas_call(
         spread_kernel,
         out_shape=struct((GROUP, SLAB, LANES), BF16),
@@ -446,9 +419,10 @@
             pltpu.SemaphoreType.DMA((NREL // 2 // SPREAD,)),
         ],
         compiler_params=PARAMS,
-        cost_estimate=pl.CostEstimate(flops=10**9, bytes_accessed=10**7, transcendentals=0),
+        cost_estimate=COST,
         name="spread",
     )(grads, rid, got, hot_mine, core)
+    slabs, from_prev, from_next = lax.optimization_barrier((slabs, from_prev, from_next))
     slabs = lax.all_to_all(slabs, NEAR, 0, 0, tiled=True)
     part = (own_grad + from_prev.astype(F32) + from_next.astype(F32)).astype(BF16)
     slabs, part = lax.optimization_barrier((slabs, part))

time: 133 us -> 121 us (0.910)
  waiting for transfers between devices: 21.4 us -> 29.1 us
  starting transfers between devices: 23.8 us -> 17.2 us
  Pallas kernels: 30 us -> 23.5 us
  local copies, waits for them, and re-layouts: 9.61 us -> 3.4 us
    all_to_all x1, waiting for transfers between devices: 8.75 us -> 20.4 us  [shards(): slabs = lax.all_to_all(slabs, NEAR, 0, 0, tiled=True)]
    unnamed x44 -> x22, local copies, waits for them, and re-layouts: 9.61 us -> 3.4 us
    ppermute x4, starting transfers between devices: 17 us -> 11.8 us  [moved(): lax.ppermute(value, axis, [(i, (i + steps) % count) for i in range(count)])]
    pallas_call x1, Pallas kernels: 6.01 us -> 2.76 us  [shards(): pl.pallas_call(lookup_kernel, out_shape=struct((D, edges), BF16), in_spec...]
    ppermute x1, waiting for transfers between devices: 3.03 us -> 0.05 us  [shards(): got = lax.ppermute(msg, 'core', swap)]
    all_to_all x1, blocking collectives: 29.9 us -> 27.1 us  [shards(): mine = lax.all_to_all(column, NEAR, 0, 0, tiled=True)]
    all_to_all x1, blocking collectives: 13.7 us -> 15.8 us  [shards(): pieces = lax.all_to_all(pieces, 'zh', 0, 0, tiled=True)]
    pallas_call x2 -> x4, Pallas kernels: 9.79 us -> 8.08 us  [the longest x2 5.54 us: back(): pl.pallas_call(functools.partial(back_kernel, k), out_shape=(half, half,...]
  transfers between devices with their start and end apart: 8 -> 8, of which waited for: 4 -> 4; matrix products, arithmetic and copies ran while one was open for 1% -> 2% of each run, Pallas kernels for 11% -> 13%
where the time goes in v3:
time: 121 us; the launch traced here: 119 us
  blocking collectives  43 us (36%)
  waiting for transfers between devices  29.1 us (24%)
  Pallas kernels  23.5 us (19%)
  starting transfers between devices  17.2 us (14%)
  local copies, waits for them, and re-layouts  3.4 us (3%)
  other arithmetic  2.3 us (2%)
    all_to_all x1, blocking collectives, shards(): mine = lax.all_to_all(column, NEAR, 0, 0, tiled=True)  27.1 us
    all_to_all x1, waiting for transfers between devices, shards(): slabs = lax.all_to_all(slabs, NEAR, 0, 0, tiled=True)  20.4 us
    all_to_all x1, blocking collectives, shards(): pieces = lax.all_to_all(pieces, 'zh', 0, 0, tiled=True)  15.8 us
    ppermute x4, starting transfers between devices, moved(): lax.ppermute(value, axis, [(i, (i + steps) % count) for i in range(count)])  11.8 us
    ppermute x4, waiting for transfers between devices, moved(): lax.ppermute(value, axis, [(i, (i + steps) % count) for i in range(count)])  8.36 us
    pallas_call x2, Pallas kernels, back(): pl.pallas_call(functools.partial(back_kernel, k), out_shape=(half, half,...  5.54 us
    all_to_all x1, starting transfers between devices, shards(): slabs = lax.all_to_all(slabs, NEAR, 0, 0, tiled=True)  5.09 us
    pallas_call x2, Pallas kernels, merged(): pl.pallas_call(merge_kernel, out_shape=struct((D, NREL), F32), grid_spec=...  4.48 us
  transfers between devices with their start and end apart: 8, of which 4 were waited for; matrix products, arithmetic and copies ran while one was open for 2% of the time, Pallas kernels for 13%

profile of v3, /device:TPU:2, one launch (start us, length us, event | category | flops | bytes accessed | tf_op | source)
XLA Modules:
  0.0 119.3 jit_solution(6842552436477454107)
XLA Ops:
  0.7 9.4 %collective-permute-start = (bf16[400,512]{1,0:T(8,128)(2,1)}, bf16[400,512]{1,0:T(8,128)(2,1)S(1)}, u32[]{:S(2)}, u32[]{:S(2)}) collective-permute-start(bf16[400,512]{1,0:T(8,128)(2,1)} %bitcast.17), channel_id=1, source_target_pairs={{0,254},{2,0},{4,2},{6,4},{8,6},{10,8},{12,10},{14,12},{16,14},{18... | collective-permute-start | bytes 1228808 | tf_op jit(solution)/shard_map/ppermute | solution.py:328
  10.1 0.7 copy-done.5
  10.8 1.9 %copy-done.9 = bf16[4096,400]{0,1:T(8,128)(2,1)S(1)} copy-done((bf16[4096,400]{0,1:T(8,128)(2,1)S(1)}, bf16[4096,400]{0,1:T(8,128)(2,1)}, u32[]{:S(2)}) %copy-start.9) | copy-done | bytes 3276824
  12.7 2.8 %lookup.1.rel_ref = bf16[400,768]{1,0:T(8,128)(2,1)S(1)} custom-call(bf16[400,4096]{1,0:T(8,128)(2,1)S(1)} %bitcast.34, s32[1,768]{1,0:T(1,128)S(1)} %bitcast.27), custom_call_target="tpu_custom_call" | custom-call | flops 3000000000 | bytes 10000000 | tf_op jit(solution)/shard_map/lookup/pallas_call | solution.py:346
  15.6 3.5 %front.1 = (bf16[400,768]{1,0:T(8,128)(2,1)S(1)}, bf16[400,768]{1,0:T(8,128)(2,1)S(1)}, bf16[768,400]{1,0:T(8,128)(2,1)S(1)}, bf16[400,256]{1,0:T(8,128)(2,1)S(1...) custom-call(bf16[400,768]{1,0:T(8,128)(2,1)S(1)} %lookup.1.rel_ref, bf16[400,512]{1,0:T(8,128)(2,1)S(1)} %bitcast.18, ...), custom_call_target="tpu_custom_call" | custom-call | flops 100000000 | bytes 1000000 | tf_op jit(solution)/shard_map/front/pallas_call | solution.py:358
  19.1 2.8 %back.3 = (bf16[400,256]{1,0:T(8,128)(2,1)S(1)}, bf16[400,256]{1,0:T(8,128)(2,1)S(1)}, bf16[256,1024]{1,0:T(8,128)(2,1)S(1)}, bf16[400,512]{1,0:T(8,128)(2,1)S(1)}) custom-call(bf16[400,512]{1,0:T(8,128)(2,1)S(1)} %collective-permute-done.1.far_ref, bf16[400,1024]{1,0:T(8,128)(2,1)S(1)} %bitcast.14, bf16[400,768]{1,0:T(8,128)(2,1)S(1)} %get-tuple-element.31.src_ref, ...), custom_call_target="tpu_custom_call" | custom-call | flops 100000000 | bytes 1000000 | tf_op jit(solution)/shard_map/back/pallas_call | solution.py:372
  21.9 2.8 %back.2 = (bf16[400,256]{1,0:T(8,128)(2,1)S(1)}, bf16[400,256]{1,0:T(8,128)(2,1)S(1)}, bf16[256,1024]{1,0:T(8,128)(2,1)S(1)}, bf16[400,512]{1,0:T(8,128)(2,1)S(1)}) custom-call(bf16[400,512]{1,0:T(8,128)(2,1)S(1)} %collective-permute-done.far_ref, bf16[400,1024]{1,0:T(8,128)(2,1)S(1)} %bitcast.15, bf16[400,768]{1,0:T(8,128)(2,1)S(1)} %get-tuple-element.31.src_ref, ...), custom_call_target="tpu_custom_call" | custom-call | flops 100000000 | bytes 1000000 | tf_op jit(solution)/shard_map/back/pallas_call | solution.py:372
  24.7 2.1 %pack.1 = (bf16[4544,128]{1,0:T(8,128)(2,1)S(1)}, bf16[400,768]{1,0:T(8,128)(2,1)S(1)}, bf16[2048,128]{1,0:T(8,128)(2,1)S(1)}) custom-call(bf16[400,256]{1,0:T(8,128)(2,1)S(1)} %get-tuple-element.34.gr0_ref, bf16[400,256]{1,0:T(8,128)(2,1)S(1)} %get-tuple-element.35.gr1_ref, bf16[400,256]{1,0:T(8,128)(2,1)S(1)} %get-tuple-element.36.gr2_ref, ...), custom_call_target="tpu_custom_call" | custom-call | flops 100000000 | bytes 1000000 | tf_op jit(solution)/shard_map/pack/pallas_call | solution.py:386
  27.1 2.3 %collective-permute-start.4 = (bf16[400,512]{1,0:T(8,128)(2,1)S(1)}, bf16[400,512]{1,0:T(8,128)(2,1)S(1)}, u32[]{:S(2)}, u32[]{:S(2)}) collective-permute-start(bf16[400,512]{1,0:T(8,128)(2,1)S(1)} %get-tuple-element.48), channel_id=1, source_target_pairs={{0,254},{2,0},{4,2},{6,4},{8,6},{10,8},{12,10},{14,12},{16,14},{18... | collective-permute-start | bytes 1228808 | tf_op jit(solution)/shard_map/ppermute | solution.py:328
  29.4 0.4 tail.1
  29.9 3.6 %spread.1 = bf16[32,256,128]{2,1,0:T(8,128)(2,1)} custom-call(bf16[400,768]{1,0:T(8,128)(2,1)S(1)} %get-tuple-element.40.grad_ref, s32[1,768]{1,0:T(1,128)S(1)} %bitcast.29, bf16[4544,128]{1,0:T(8,128)(2,1)S(1)} %collective-permute-done.2.got_ref, bf16[2048,128]{1,0:T(8,128)(2,1)S(1)} %get-tuple-element.46.hot_ref, s32[1]{0:T(128)} %bitcast.9.core_ref), custom_call_target="tpu_custom_call" | custom-call | flops 100000000 | bytes 1000000 | tf_op jit(solution)/shard_map/spread/pallas_call | solution.py:410
  33.5 1.4 %collective-permute-done.4 = bf16[400,512]{1,0:T(8,128)(2,1)S(1)} collective-permute-done((bf16[400,512]{1,0:T(8,128)(2,1)S(1)}, bf16[400,512]{1,0:T(8,128)(2,1)S(1)}, u32[]{:S(2)}, u32[]{:S(2)}) %collective-permute-start.4) | collective-permute-done | bytes 409632 | tf_op jit(solution)/shard_map/ppermute | solution.py:328
  34.9 0.7 copy-done.10
  35.6 7.0 %collective-permute-done.3 = bf16[400,512]{1,0:T(8,128)(2,1)} collective-permute-done((bf16[400,512]{1,0:T(8,128)(2,1)S(1)}, bf16[400,512]{1,0:T(8,128)(2,1)}, u32[]{:S(2)}, u32[]{:S(2)}) %collective-permute-start.3) | collective-permute-done | bytes 409632 | tf_op jit(solution)/shard_map/ppermute | solution.py:328
  42.6 5.1 %all-to-all-start = ((bf16[32,256,128]{2,1,0:T(8,128)(2,1)}), bf16[32,256,128]{2,1,0:T(8,128)(2,1)S(1)}, u32[]{:S(2)}, u32[]{:S(2)}) async-start(bf16[32,256,128]{2,1,0:T(8,128)(2,1)} %spread.1), calls=%async_computation | async-start | bytes 4194304 | tf_op jit(solution)/shard_map/all_to_all | solution.py:426
  47.7 1.3 %add_convert_fusion = bf16[400,512]{1,0:T(8,128)(2,1)S(1)} fusion(bf16[400,512]{1,0:T(8,128)(2,1)} %copy-done.10, f32[400,512]{1,0:T(8,128)S(1)} %tail.1, bf16[400,512]{1,0:T(8,128)(2,1)} %collective-permute-done.3), kind=kLoop, calls=%fused_computation.1 | loop fusion | flops 1024000 | bytes 2048000 | tf_op jit(solution)/shard_map/convert_element_type | solution.py:427
  49.0 20.4 %all-to-all-done.in_ref = bf16[32,256,128]{2,1,0:T(8,128)(2,1)S(1)} async-done(((bf16[32,256,128]{2,1,0:T(8,128)(2,1)}), bf16[32,256,128]{2,1,0:T(8,128)(2,1)S(1)}, u32[]{:S(2)}, u32[]{:S(2)}) %all-to-all-start) | async-done | bytes 2097184 | tf_op jit(solution)/shard_map/all_to_all | solution.py:426
  69.4 0.4 near_sum.1
  69.8 15.8 %all_to_all.15.in_ref = bf16[4,224,128]{2,1,0:T(8,128)(2,1)S(1)} all-to-all(bf16[4,224,128]{2,1,0:T(8,128)(2,1)S(1)} %near_sum.1), channel_id=1, replica_groups=mesh['y'=4,'xh'=2,'zh'=4,'zl'=2,'core'=2,'rep'=2] {'zh'}, dimensions={0} | all-to-all | bytes 458752 | tf_op jit(solution)/shard_map/all_to_all | solution.py:438
  85.7 0.7 quad_sum.1
  86.4 27.1 %all_to_all.16.in_ref = bf16[32,200,128]{2,1,0:T(8,128)(2,1)S(1)} all-to-all(bf16[32,200,128]{2,1,0:T(8,128)(2,1)S(1)} %get-tuple-element.57), channel_id=1, replica_groups=mesh['y'=4,'xh'=2,'zh'=4,'zl'=2,'core'=2,'rep'=2] {'y','xh','zl','rep'}, dimensions={0} | all-to-all | bytes 3276800 | tf_op jit(solution)/shard_map/all_to_all | solution.py:448
  113.5 1.0 add_bitcast_fusion
  114.5 2.2 %merge.2.refs_0_ = f32[400,4096]{1,0:T(8,128)} custom-call(s32[1]{0:T(128)} %bitcast.9.core_ref, bf16[32,200,128]{2,1,0:T(8,128)(2,1)S(1)} %all_to_all.16.in_ref), custom_call_target="tpu_custom_call" | custom-call | bytes 10000000 | tf_op jit(solution)/shard_map/merge/pallas_call | solution.py:300
  117.0 2.2 %merge.3 = f32[400,4096]{1,0:T(8,128)} custom-call(s32[1]{0:T(128)} %bitcast.9.core_ref, bf16[32,200,128]{2,1,0:T(8,128)(2,1)S(1)} %collective-permute-done.6.in_ref, f32[400,4096]{1,0:T(8,128)} %merge.2.refs_0_), custom_call_target="tpu_custom_call", output_to_operand_aliasing={{}: (2, {})} | custom-call | bytes 10000000 | tf_op jit(solution)/shard_map/merge/pallas_call | solution.py:300
  (29 shorter events, 0.7 us)
Async XLA Ops:
  0.6 18.4 %collective-permute-start.1 = (bf16[400,512]{1,0:T(8,128)(2,1)}, bf16[400,512]{1,0:T(8,128)(2,1)S(1)}, u32[]{:S(2)}, u32[]{:S(2)}) collective-permute-start(bf16[400,512]{1,0:T(8,128)(2,1)} %bitcast.16), channel_id=1, source_target_pairs={{0,2},{2,4},{4,6},{6,8},{8,10},{10,12},{12,14},{14,16},{16,18},{18... | collective-permute-start | bytes 1228808 | tf_op jit(solution)/shard_map/ppermute | solution.py:328
  0.7 21.1 %collective-permute-start = (bf16[400,512]{1,0:T(8,128)(2,1)}, bf16[400,512]{1,0:T(8,128)(2,1)S(1)}, u32[]{:S(2)}, u32[]{:S(2)}) collective-permute-start(bf16[400,512]{1,0:T(8,128)(2,1)} %bitcast.17), channel_id=1, source_target_pairs={{0,254},{2,0},{4,2},{6,4},{8,6},{10,8},{12,10},{14,12},{16,14},{18... | collective-permute-start | bytes 1228808 | tf_op jit(solution)/shard_map/ppermute | solution.py:328
  10.1 0.7 copy-start.5
  10.8 1.9 %copy-start.9 = (bf16[4096,400]{0,1:T(8,128)(2,1)S(1)}, bf16[4096,400]{0,1:T(8,128)(2,1)}, u32[]{:S(2)}) copy-start(bf16[4096,400]{0,1:T(8,128)(2,1)} %param.11) | copy-start | bytes 9830404
  12.7 2.8 %copy-start = (bf16[1024,400]{0,1:T(8,128)(2,1)S(1)}, bf16[1024,400]{0,1:T(8,128)(2,1)}, u32[]{:S(2)}) copy-start(bf16[1024,400]{0,1:T(8,128)(2,1)} %param.10) | copy-start | bytes 2457604
  12.7 2.8 %copy-start.1 = (bf16[512,400]{0,1:T(8,128)(2,1)S(1)}, bf16[512,400]{0,1:T(8,128)(2,1)}, u32[]{:S(2)}) copy-start(bf16[512,400]{0,1:T(8,128)(2,1)} %param.9) | copy-start | bytes 1228804
  12.7 2.8 %copy-start.2 = (s32[1,1,3,512]{3,1,2,0:T(1,128)S(1)}, s32[1,1,3,512]{3,1,2,0:T(1,128)}, u32[]{:S(2)}) copy-start(s32[1,1,3,512]{3,1,2,0:T(1,128)} %param.15) | copy-start | bytes 18436
  12.7 2.8 %copy-start.3 = (s32[1,1,3,256]{3,1,2,0:T(1,128)S(1)}, s32[1,1,3,256]{3,1,2,0:T(1,128)}, u32[]{:S(2)}) copy-start(s32[1,1,3,256]{3,1,2,0:T(1,128)} %param.14) | copy-start | bytes 9220
  12.7 2.8 %copy-start.4 = (s32[1,1,3,256]{3,1,2,0:T(1,128)S(1)}, s32[1,1,3,256]{3,1,2,0:T(1,128)}, u32[]{:S(2)}) copy-start(s32[1,1,3,256]{3,1,2,0:T(1,128)} %param.12) | copy-start | bytes 9220
  12.7 2.8 %copy-start.7 = (s32[1,1,3]{2,1,0:T(1,128)S(1)}, s32[1,1,3]{2,1,0:T(1,128)}, u32[]{:S(2)}) copy-start(s32[1,1,3]{2,1,0:T(1,128)} %param.16) | copy-start | bytes 40
  21.8 2.8 %copy-start.8 = (s32[1024]{0:T(1024)S(1)}, s32[1024]{0:T(1024)}, u32[]{:S(2)}) copy-start(s32[1024]{0:T(1024)} %param.17) | copy-start | bytes 12292
  24.7 5.2 %copy-start.6 = (s32[1,1,3,256]{3,1,2,0:T(1,128)S(1)}, s32[1,1,3,256]{3,1,2,0:T(1,128)}, u32[]{:S(2)}) copy-start(s32[1,1,3,256]{3,1,2,0:T(1,128)} %param.13) | copy-start | bytes 9220
  26.8 3.1 %collective-permute-start.2 = (bf16[4544,128]{1,0:T(8,128)(2,1)S(1)}, bf16[4544,128]{1,0:T(8,128)(2,1)S(1)}, u32[]{:S(2)}, u32[]{:S(2)}) collective-permute-start(bf16[4544,128]{1,0:T(8,128)(2,1)S(1)} %get-tuple-element.41), channel_id=1, source_target_pairs={{0,2},{2,0},{1,3},{3,1},{4,6},{6,4},{5,7},{7,5},{8,10},{10,8},{9,1... | collective-permute-start | bytes 3489800 | tf_op jit(solution)/shard_map/ppermute | solution.py:408
  27.1 7.8 %collective-permute-start.4 = (bf16[400,512]{1,0:T(8,128)(2,1)S(1)}, bf16[400,512]{1,0:T(8,128)(2,1)S(1)}, u32[]{:S(2)}, u32[]{:S(2)}) collective-permute-start(bf16[400,512]{1,0:T(8,128)(2,1)S(1)} %get-tuple-element.48), channel_id=1, source_target_pairs={{0,254},{2,0},{4,2},{6,4},{8,6},{10,8},{12,10},{14,12},{16,14},{18... | collective-permute-start | bytes 1228808 | tf_op jit(solution)/shard_map/ppermute | solution.py:328
  29.4 13.2 %collective-permute-start.3 = (bf16[400,512]{1,0:T(8,128)(2,1)S(1)}, bf16[400,512]{1,0:T(8,128)(2,1)}, u32[]{:S(2)}, u32[]{:S(2)}) collective-permute-start(bf16[400,512]{1,0:T(8,128)(2,1)S(1)} %get-tuple-element.47), channel_id=1, source_target_pairs={{0,2},{2,4},{4,6},{6,8},{8,10},{10,12},{12,14},{14,16},{16,18},{18... | collective-permute-start | bytes 1228808 | tf_op jit(solution)/shard_map/ppermute | solution.py:328
  34.9 0.8 copy-start.10
  42.6 26.8 %all-to-all-start = ((bf16[32,256,128]{2,1,0:T(8,128)(2,1)}), bf16[32,256,128]{2,1,0:T(8,128)(2,1)S(1)}, u32[]{:S(2)}, u32[]{:S(2)}) async-start(bf16[32,256,128]{2,1,0:T(8,128)(2,1)} %spread.1), calls=%async_computation | async-start | bytes 4194304 | tf_op jit(solution)/shard_map/all_to_all | solution.py:426
  69.4 16.2 %collective-permute-start.5 = (bf16[400,512]{1,0:T(8,128)(2,1)S(1)}, bf16[400,512]{1,0:T(8,128)(2,1)S(1)}, u32[]{:S(2)}, u32[]{:S(2)}) collective-permute-start(bf16[400,512]{1,0:T(8,128)(2,1)S(1)} %add_convert_fusion), channel_id=1, source_target_pairs={{0,1},{1,0},{2,3},{3,2},{4,5},{5,4},{6,7},{7,6},{8,9},{9,8},{10,11... | collective-permute-start | bytes 1228808 | tf_op jit(solution)/shard_map/ppermute | solution.py:429
  113.5 3.5 %collective-permute-start.6 = (bf16[32,200,128]{2,1,0:T(8,128)(2,1)S(1)}, bf16[32,200,128]{2,1,0:T(8,128)(2,1)S(1)}, u32[]{:S(2)}, u32[]{:S(2)}) collective-permute-start(bf16[32,200,128]{2,1,0:T(8,128)(2,1)S(1)} %all_to_all.16.in_ref), channel_id=1, source_target_pairs={{0,2},{2,0},{1,3},{3,1},{4,6},{6,4},{5,7},{7,5},{8,10},{10,8},{9,1... | collective-permute-start | bytes 4915208 | tf_op jit(solution)/shard_map/ppermute | solution.py:449

commit v4 on v3

--- a/solution.py
+++ b/solution.py
@@ -26,7 +26,6 @@
 TAIL = HALF_D
 HOT_AT = HALF_D + 8
 SLAB = HOT_AT + 3 * 16
-PIECE = 224
 WIDE = 256
 SPREAD = 512
 BLK = ("y", "xh", "zh", "zl", "core")
@@ -156,9 +155,28 @@
     far_out[...] = g_far.astype(BF16)
 
 
+def hot_rows(g_hot, slot, core, out, first):
+    owner = jnp.right_shift(slot, 2)
+    spot = (
+        jnp.bitwise_and(jnp.right_shift(owner, 1), 1) * 512
+        + jnp.right_shift(owner, 5) * 64
+        + jnp.bitwise_and(jnp.right_shift(owner, 2), 1) * 32
+        + jnp.bitwise_and(owner, 1) * 16
+        + jnp.bitwise_and(jnp.right_shift(owner, 3), 3) * 4
+        + jnp.bitwise_and(slot, 3)
+    )
+    rows = dot_nt(onehot(512, spot - core * 512), g_hot).astype(BF16)
+    for b in range(3):
+        start = first + b * 512
+        out[start : start + 512, :] = rows[:, b * LANES : (b + 1) * LANES]
+    out[first + 3 * 512 : first + 4 * 512, :] = jnp.concatenate(
+        [rows[:, 3 * LANES :], jnp.zeros((512, HOT_BLOCKS * LANES - D), BF16)], axis=1
+    )
+
+
 def pack_kernel(
     gr0_ref, gr1_ref, gr2_ref, wh0_ref, wh1_ref, wh2_ref, low_ref, rid_ref, slot_ref, core_ref,
-    msg_out, all_out, hot_out,
+    msg_out, all_out, g_hot_out,
 ):
     relations = [gr0_ref[...], gr1_ref[...], gr2_ref[...]]
     weights = [wh0_ref[...], wh1_ref[...], wh2_ref[...]]
@@ -173,36 +191,20 @@
         msg_out[b * REL_ROWS : b * REL_ROWS + D, :] = piece
         all_out[:, b * LANES : (b + 1) * LANES] = piece
         msg_out[b * REL_ROWS + D : (b + 1) * REL_ROWS, :] = tail
-    slot = slot_ref[...]
-    owner = jnp.right_shift(slot, 2)
-    spot = (
-        jnp.bitwise_and(jnp.right_shift(owner, 1), 1) * 512
-        + jnp.right_shift(owner, 5) * 64
-        + jnp.bitwise_and(jnp.right_shift(owner, 2), 1) * 32
-        + jnp.bitwise_and(owner, 1) * 16
-        + jnp.bitwise_and(jnp.right_shift(owner, 3), 3) * 4
-        + jnp.bitwise_and(slot, 3)
-    )
     g_hot = dot(low_ref[...], jnp.concatenate(weights, axis=0)).astype(BF16)
-    core = core_ref[0]
-    for base, out, first in ((core * 512, hot_out, 0), ((1 - core) * 512, msg_out, HOT_BASE)):
-        rows = dot_nt(onehot(512, spot - base), g_hot).astype(BF16)
-        for b in range(HOT_BLOCKS):
-            start = first + b * 512
-            if b < 3:
-                out[start : start + 512, :] = rows[:, b * LANES : (b + 1) * LANES]
-            else:
-                out[start : start + 512, :] = jnp.concatenate(
-                    [rows[:, 3 * LANES :], jnp.zeros((512, HOT_BLOCKS * LANES - D), BF16)], axis=1
-                )
-
-
-def tail_kernel(own_ref, gs0_ref, gs2_ref, sid_ref, own_out):
+    g_hot_out[...] = g_hot
+    hot_rows(g_hot, slot_ref[...], 1 - core_ref[0], msg_out, HOT_BASE)
+
+
+def tail_kernel(
+    own_ref, gs0_ref, gs2_ref, sid_ref, g_hot_ref, slot_ref, core_ref, own_out, hot_out
+):
     ids = sid_ref[...]
     total = own_ref[...]
     for k, gs_ref in ((0, gs0_ref), (2, gs2_ref)):
         total = total + dot_nt(gs_ref[...], onehot(ENT, ids[:, k * EDGES : (k + 1) * EDGES]))
     own_out[...] = total
+    hot_rows(g_hot_ref[...], slot_ref[...], core_ref[0], hot_out, 0)
 
 
 def spread_kernel(grad_ref, rid_ref, got_ref, hot_ref, core_ref, out_ref, grads, id_ref, slabs, sems):
@@ -248,37 +250,34 @@
     total = in_ref[0].astype(F32)
     for j in range(1, GROUP):
         total = total + in_ref[j].astype(F32)
-    for zh in range(QUAD):
-        parts = [total[:HALF_D]]
-        for b in range(3):
-            row = HOT_AT + b * 16 + zh * 4
-            parts.append(total[row : row + 4])
-        row, col = TAIL + (zh % 2) * 4, (zh // 2) * 16
-        parts.append(
-            jnp.concatenate(
-                [total[row : row + 4, col : col + 16], jnp.zeros((4, LANES - 16), F32)], axis=1
-            )
-        )
-        parts.append(jnp.zeros((PIECE - HALF_D - 16, LANES), F32))
-        out_ref[zh] = jnp.concatenate(parts, axis=0).astype(BF16)
-
-
-def quad_sum_kernel(in_ref, rel_ref, hot_ref):
-    total = in_ref[0].astype(F32)
-    for zh in range(1, QUAD):
-        total = total + in_ref[zh].astype(F32)
+    out_ref[...] = total.astype(BF16)
+
+
+def quad_sum_kernel(r0, r1, r2, r3, place_ref, rel_ref, hot_ref, held):
+    place = place_ref[0]
+    for n, ref in enumerate((r0, r1, r2, r3)):
+        held[n] = ref[...]
+    total = None
+    for source in range(QUAD):
+        piece = held[jnp.bitwise_and(place - source, QUAD - 1)].astype(F32)
+        total = piece if total is None else total + piece
     rel = total[:HALF_D].astype(BF16)
     for j in range(GROUP):
         rel_ref[j] = rel
-    for b in range(HOT_BLOCKS):
-        width = min(LANES, D - b * LANES)
-        row = HALF_D + 4 * b
-        hot_ref[:, b * LANES : b * LANES + width] = total[row : row + 4, :width]
+    for q in range(QUAD):
+
+        @pl.when(place == q)
+        def _():
+            for b in range(3):
+                row = HOT_AT + b * 16 + q * 4
+                hot_ref[:, b * LANES : (b + 1) * LANES] = total[row : row + 4]
+            row, col = TAIL + (q % 2) * 4, (q // 2) * 16
+            hot_ref[:, 3 * LANES :] = total[row : row + 4, col : col + 16]
 
 
 def merge_kernel(core_ref, in_ref, *refs):
     out_ref = refs[-1]
-    for near in range(2):
+    for near in range(in_ref.shape[0] // 4):
         for zl in range(2):
             for rep in range(2):
                 col = (2 * near + rep) * LANES
@@ -288,13 +287,13 @@
 
 
 def merged(core, value, before):
-    steps = GROUP // 8
+    steps = GROUP // 16
     first = before is None
     if first:
         place = lambda i, c: (0, c[0] * steps + i)
     else:
         place = lambda i, c: (0, (1 - c[0]) * steps + i)
-    in_specs = [pl.BlockSpec((8, HALF_D, LANES), lambda i, c: (i, 0, 0))]
+    in_specs = [pl.BlockSpec((16, HALF_D, LANES), lambda i, c: (i, 0, 0))]
     if not first:
         in_specs.append(pl.BlockSpec(memory_space=pl.ANY))
     return pl.pallas_call(
@@ -304,7 +303,7 @@
             num_scalar_prefetch=1,
             grid=(steps,),
             in_specs=in_specs,
-            out_specs=pl.BlockSpec((D, 4 * LANES), place),
+            out_specs=pl.BlockSpec((D, 8 * LANES), place),
         ),
         input_output_aliases={} if first else {2: 0},
         compiler_params=PARAMS,
@@ -383,11 +382,11 @@
     from_prev = moved(next_grad, BLK, blocks, 1)
     gs2, gr2, wh2, prev_grad = back(2, before)
     from_next = moved(prev_grad, BLK, blocks, -1)
-    msg, grads, hot_mine = pl.pallas_call(
+    msg, grads, g_hot = pl.pallas_call(
         pack_kernel,
         out_shape=(
             struct((MSG_ROWS, LANES), BF16), struct((D, edges), BF16),
-            struct((HOT_BLOCKS * 512, LANES), BF16),
+            struct((D, HOT), BF16),
         ),
         in_specs=[VMEM] * 9 + [SMEM],
         out_specs=[VMEM] * 3,
@@ -395,18 +394,18 @@
         cost_estimate=COST,
         name="pack",
     )(gr0, gr1, gr2, wh0, wh1, wh2, low, rid, slot, core)
-    own_grad = pl.pallas_call(
+    own_grad, hot_mine = pl.pallas_call(
         tail_kernel,
-        out_shape=struct((D, ENT), F32),
-        in_specs=[VMEM] * 4,
-        out_specs=VMEM,
+        out_shape=(struct((D, ENT), F32), struct((HOT_BLOCKS * 512, LANES), BF16)),
+        in_specs=[VMEM] * 6 + [SMEM],
+        out_specs=[VMEM] * 2,
         compiler_params=PARAMS,
         cost_estimate=COST,
         name="tail",
-    )(own_grad, gs0, gs2, sid)
+    )(own_grad, gs0, gs2, sid, g_hot, slot, core)
     swap = [(0, 1), (1, 0)]
     got = lax.ppermute(msg, "core", swap)
-    got, own_grad = lax.optimization_barrier((got, own_grad))
+    got, own_grad, hot_mine = lax.optimization_barrier((got, own_grad, hot_mine))
     slabs = pl.pallas_call(
         spread_kernel,
         out_shape=struct((GROUP, SLAB, LANES), BF16),
@@ -429,22 +428,24 @@
     twin = lax.ppermute(part, "rep", swap)
     pieces = pl.pallas_call(
         near_sum_kernel,
-        out_shape=struct((QUAD, PIECE, LANES), BF16),
+        out_shape=struct((SLAB, LANES), BF16),
         in_specs=[VMEM],
         out_specs=VMEM,
         compiler_params=PARAMS,
         name="near_sum",
     )(slabs)
-    pieces = lax.all_to_all(pieces, "zh", 0, 0, tiled=True)
+    pieces = [pieces] + [moved(pieces, "zh", QUAD, n) for n in range(1, QUAD)]
+    place = lax.axis_index("zh").astype(jnp.int32).reshape(1)
     pieces, twin = lax.optimization_barrier((pieces, twin))
     column, hot_grad = pl.pallas_call(
         quad_sum_kernel,
         out_shape=(struct((GROUP, HALF_D, LANES), BF16), struct((4, D), F32)),
-        in_specs=[VMEM],
+        in_specs=[VMEM] * QUAD + [SMEM],
         out_specs=(VMEM, VMEM),
+        scratch_shapes=[pltpu.VMEM((QUAD, SLAB, LANES), BF16)],
         compiler_params=PARAMS,
         name="quad_sum",
-    )(pieces)
+    )(*pieces, place)
     mine = lax.all_to_all(column, NEAR, 0, 0, tiled=True)
     other = lax.ppermute(mine, "core", swap)
     relation_grad = merged(core, other, merged(core, mine, None))

time: 121 us -> 121 us (level)
  blocking collectives: 43 us -> 28.7 us
  starting transfers between devices: 17.2 us -> 25.1 us
  waiting for transfers between devices: 29.1 us -> 36.1 us
    all_to_all x1 -> x0, blocking collectives: 15.8 us -> none  [shards(): pieces = lax.all_to_all(pieces, 'zh', 0, 0, tiled=True)]
    ppermute x4 -> x7, starting transfers between devices: 11.8 us -> 19.9 us  [moved(): lax.ppermute(value, axis, [(i, (i + steps) % count) for i in range(count)])]
    ppermute x4 -> x7, waiting for transfers between devices: 8.36 us -> 15.7 us  [moved(): lax.ppermute(value, axis, [(i, (i + steps) % count) for i in range(count)])]
    all_to_all x1, blocking collectives: 27.1 us -> 28.7 us  [shards(): mine = lax.all_to_all(column, NEAR, 0, 0, tiled=True)]
    unnamed x22 -> x20, local copies, waits for them, and re-layouts: 3.4 us -> 2.65 us
  transfers between devices with their start and end apart: 8 -> 11, of which waited for: 4 -> 7; matrix products, arithmetic and copies ran while one was open for 2% -> 2% of each run, Pallas kernels for 13% -> 13%
where the time goes in v4:
time: 121 us; the launch traced here: 119 us
  waiting for transfers between devices  36.1 us (30%)
  blocking collectives  28.7 us (24%)
  starting transfers between devices  25.1 us (21%)
  Pallas kernels  22.8 us (19%)
  local copies, waits for them, and re-layouts  2.65 us (2%)
  other arithmetic  2.3 us (2%)
    all_to_all x1, blocking collectives, shards(): mine = lax.all_to_all(column, NEAR, 0, 0, tiled=True)  28.7 us
    ppermute x7, starting transfers between devices, moved(): lax.ppermute(value, axis, [(i, (i + steps) % count) for i in range(count)])  19.9 us
    all_to_all x1, waiting for transfers between devices, shards(): slabs = lax.all_to_all(slabs, NEAR, 0, 0, tiled=True)  19.8 us
    ppermute x7, waiting for transfers between devices, moved(): lax.ppermute(value, axis, [(i, (i + steps) % count) for i in range(count)])  15.7 us
    pallas_call x2, Pallas kernels, back(): pl.pallas_call(functools.partial(back_kernel, k), out_shape=(half, half,...  5.6 us
    all_to_all x1, starting transfers between devices, shards(): slabs = lax.all_to_all(slabs, NEAR, 0, 0, tiled=True)  5.09 us
    pallas_call x2, Pallas kernels, merged(): pl.pallas_call(merge_kernel, out_shape=struct((D, NREL), F32), grid_spec=...  3.77 us
    pallas_call x1, Pallas kernels, shards(): pl.pallas_call(spread_kernel, out_shape=struct((GROUP, SLAB, LANES), BF16...  3.61 us
  transfers between devices with their start and end apart: 11, of which 7 were waited for; matrix products, arithmetic and copies ran while one was open for 2% of the time, Pallas kernels for 13%

profile of v4, /device:TPU:2, one launch (start us, length us, event | category | flops | bytes accessed | tf_op | source)
XLA Modules:
  0.0 118.5 jit_solution(5508118386754386800)
XLA Ops:
  0.7 9.4 %collective-permute-start = (bf16[400,512]{1,0:T(8,128)(2,1)}, bf16[400,512]{1,0:T(8,128)(2,1)S(1)}, u32[]{:S(2)}, u32[]{:S(2)}) collective-permute-start(bf16[400,512]{1,0:T(8,128)(2,1)} %bitcast.18), channel_id=1, source_target_pairs={{0,254},{2,0},{4,2},{6,4},{8,6},{10,8},{12,10},{14,12},{16,14},{18... | collective-permute-start | bytes 1228808 | tf_op jit(solution)/shard_map/ppermute | solution.py:327
  10.1 0.7 copy-done.6
  10.8 1.9 %copy-done.9 = bf16[4096,400]{0,1:T(8,128)(2,1)S(1)} copy-done((bf16[4096,400]{0,1:T(8,128)(2,1)S(1)}, bf16[4096,400]{0,1:T(8,128)(2,1)}, u32[]{:S(2)}) %copy-start.9) | copy-done | bytes 3276824
  12.7 2.8 %lookup.1.rel_ref = bf16[400,768]{1,0:T(8,128)(2,1)S(1)} custom-call(bf16[400,4096]{1,0:T(8,128)(2,1)S(1)} %bitcast.36, s32[1,768]{1,0:T(1,128)S(1)} %bitcast.30), custom_call_target="tpu_custom_call" | custom-call | flops 3000000000 | bytes 10000000 | tf_op jit(solution)/shard_map/lookup/pallas_call | solution.py:345
  15.6 3.5 %front.1 = (bf16[400,768]{1,0:T(8,128)(2,1)S(1)}, bf16[400,768]{1,0:T(8,128)(2,1)S(1)}, bf16[768,400]{1,0:T(8,128)(2,1)S(1)}, bf16[400,256]{1,0:T(8,128)(2,1)S(1...) custom-call(bf16[400,768]{1,0:T(8,128)(2,1)S(1)} %lookup.1.rel_ref, bf16[400,512]{1,0:T(8,128)(2,1)S(1)} %bitcast.19, ...), custom_call_target="tpu_custom_call" | custom-call | flops 100000000 | bytes 1000000 | tf_op jit(solution)/shard_map/front/pallas_call | solution.py:357
  19.1 2.8 %back.3 = (bf16[400,256]{1,0:T(8,128)(2,1)S(1)}, bf16[400,256]{1,0:T(8,128)(2,1)S(1)}, bf16[256,1024]{1,0:T(8,128)(2,1)S(1)}, bf16[400,512]{1,0:T(8,128)(2,1)S(1)}) custom-call(bf16[400,512]{1,0:T(8,128)(2,1)S(1)} %collective-permute-done.1.far_ref, bf16[400,1024]{1,0:T(8,128)(2,1)S(1)} %bitcast.15, bf16[400,768]{1,0:T(8,128)(2,1)S(1)} %get-tuple-element.37.src_ref, ...), custom_call_target="tpu_custom_call" | custom-call | flops 100000000 | bytes 1000000 | tf_op jit(solution)/shard_map/back/pallas_call | solution.py:371
  21.9 2.8 %back.2 = (bf16[400,256]{1,0:T(8,128)(2,1)S(1)}, bf16[400,256]{1,0:T(8,128)(2,1)S(1)}, bf16[256,1024]{1,0:T(8,128)(2,1)S(1)}, bf16[400,512]{1,0:T(8,128)(2,1)S(1)}) custom-call(bf16[400,512]{1,0:T(8,128)(2,1)S(1)} %collective-permute-done.far_ref, bf16[400,1024]{1,0:T(8,128)(2,1)S(1)} %bitcast.16, bf16[400,768]{1,0:T(8,128)(2,1)S(1)} %get-tuple-element.37.src_ref, ...), custom_call_target="tpu_custom_call" | custom-call | flops 100000000 | bytes 1000000 | tf_op jit(solution)/shard_map/back/pallas_call | solution.py:371
  24.8 1.6 %pack.1 = (bf16[4544,128]{1,0:T(8,128)(2,1)S(1)}, bf16[400,768]{1,0:T(8,128)(2,1)S(1)}, bf16[400,1024]{1,0:T(8,128)(2,1)S(1)}) custom-call(bf16[400,256]{1,0:T(8,128)(2,1)S(1)} %get-tuple-element.40.gr0_ref, bf16[400,256]{1,0:T(8,128)(2,1)S(1)} %get-tuple-element.41.gr1_ref, bf16[400,256]{1,0:T(8,128)(2,1)S(1)} %get-tuple-element.42.gr2_ref, ...), custom_call_target="tpu_custom_call" | custom-call | flops 100000000 | bytes 1000000 | tf_op jit(solution)/shard_map/pack/pallas_call | solution.py:385
  26.4 2.3 %collective-permute-start.4 = (bf16[400,512]{1,0:T(8,128)(2,1)S(1)}, bf16[400,512]{1,0:T(8,128)(2,1)}, u32[]{:S(2)}, u32[]{:S(2)}) collective-permute-start(bf16[400,512]{1,0:T(8,128)(2,1)S(1)} %get-tuple-element.57), channel_id=1, source_target_pairs={{0,254},{2,0},{4,2},{6,4},{8,6},{10,8},{12,10},{14,12},{16,14},{18... | collective-permute-start | bytes 1228808 | tf_op jit(solution)/shard_map/ppermute | solution.py:327
  28.7 1.0 tail.1
  29.7 3.6 %spread.1 = bf16[32,256,128]{2,1,0:T(8,128)(2,1)} custom-call(bf16[400,768]{1,0:T(8,128)(2,1)S(1)} %get-tuple-element.46.grad_ref, s32[1,768]{1,0:T(1,128)S(1)} %bitcast.32, bf16[4544,128]{1,0:T(8,128)(2,1)S(1)} %collective-permute-done.2.got_ref, bf16[2048,128]{1,0:T(8,128)(2,1)S(1)} %get-tuple-element.55.hot_ref, s32[1]{0:T(128)} %bitcast.9.core_ref), custom_call_target="tpu_custom_call" | custom-call | flops 100000000 | bytes 1000000 | tf_op jit(solution)/shard_map/spread/pallas_call | solution.py:409
  33.4 0.9 collective-permute-done.4
  34.2 7.7 %collective-permute-done.3 = bf16[400,512]{1,0:T(8,128)(2,1)} collective-permute-done((bf16[400,512]{1,0:T(8,128)(2,1)S(1)}, bf16[400,512]{1,0:T(8,128)(2,1)}, u32[]{:S(2)}, u32[]{:S(2)}) %collective-permute-start.3) | collective-permute-done | bytes 409632 | tf_op jit(solution)/shard_map/ppermute | solution.py:327
  41.9 5.1 %all-to-all-start = ((bf16[32,256,128]{2,1,0:T(8,128)(2,1)}), bf16[32,256,128]{2,1,0:T(8,128)(2,1)S(1)}, u32[]{:S(2)}, u32[]{:S(2)}) async-start(bf16[32,256,128]{2,1,0:T(8,128)(2,1)} %spread.1), calls=%async_computation | async-start | bytes 4194304 | tf_op jit(solution)/shard_map/all_to_all | solution.py:425
  47.1 1.3 %add_convert_fusion = bf16[400,512]{1,0:T(8,128)(2,1)S(1)} fusion(bf16[400,512]{1,0:T(8,128)(2,1)} %collective-permute-done.4, f32[400,512]{1,0:T(8,128)S(1)} %get-tuple-element.59, bf16[400,512]{1,0:T(8,128)(2,1)} %collective-permute-done.3), kind=kLoop, calls=%fused_computation.1 | loop fusion | flops 1024000 | bytes 2048000 | tf_op jit(solution)/shard_map/convert_element_type | solution.py:426
  48.3 19.8 %all-to-all-done.in_ref = bf16[32,256,128]{2,1,0:T(8,128)(2,1)S(1)} async-done(((bf16[32,256,128]{2,1,0:T(8,128)(2,1)}), bf16[32,256,128]{2,1,0:T(8,128)(2,1)S(1)}, u32[]{:S(2)}, u32[]{:S(2)}) %all-to-all-start) | async-done | bytes 2097184 | tf_op jit(solution)/shard_map/all_to_all | solution.py:425
  68.5 8.0 %collective-permute-start.6 = (bf16[256,128]{1,0:T(8,128)(2,1)S(1)}, bf16[256,128]{1,0:T(8,128)(2,1)S(1)}, u32[]{:S(2)}, u32[]{:S(2)}) collective-permute-start(bf16[256,128]{1,0:T(8,128)(2,1)S(1)} %near_sum.1.r0), channel_id=1, source_target_pairs={{0,16},{8,24},{16,0},{24,8},{1,17},{9,25},{17,1},{25,9},{2,18},{10... | collective-permute-start | bytes 196616 | tf_op jit(solution)/shard_map/ppermute | solution.py:327
  76.7 3.6 %collective-permute-done.6.r2 = bf16[256,128]{1,0:T(8,128)(2,1)S(1)} collective-permute-done((bf16[256,128]{1,0:T(8,128)(2,1)S(1)}, bf16[256,128]{1,0:T(8,128)(2,1)S(1)}, u32[]{:S(2)}, u32[]{:S(2)}) %collective-permute-start.6) | collective-permute-done | bytes 65568 | tf_op jit(solution)/shard_map/ppermute | solution.py:327
  80.3 3.4 %collective-permute-done.5.r1 = bf16[256,128]{1,0:T(8,128)(2,1)S(1)} collective-permute-done((bf16[256,128]{1,0:T(8,128)(2,1)S(1)}, bf16[256,128]{1,0:T(8,128)(2,1)S(1)}, u32[]{:S(2)}, u32[]{:S(2)}) %collective-permute-start.5) | collective-permute-done | bytes 65568 | tf_op jit(solution)/shard_map/ppermute | solution.py:327
  83.7 0.8 quad_sum.1
  84.5 28.7 %all_to_all.10.in_ref = bf16[32,200,128]{2,1,0:T(8,128)(2,1)S(1)} all-to-all(bf16[32,200,128]{2,1,0:T(8,128)(2,1)S(1)} %get-tuple-element.69), channel_id=1, replica_groups=mesh['y'=4,'xh'=2,'zh'=4,'zl'=2,'core'=2,'rep'=2] {'y','xh','zl','rep'}, dimensions={0} | all-to-all | bytes 3276800 | tf_op jit(solution)/shard_map/all_to_all | solution.py:449
  113.1 1.0 add_bitcast_fusion
  114.1 1.9 %merge.2.refs_0_ = f32[400,4096]{1,0:T(8,128)} custom-call(s32[1]{0:T(128)} %bitcast.9.core_ref, bf16[32,200,128]{2,1,0:T(8,128)(2,1)S(1)} %all_to_all.10.in_ref), custom_call_target="tpu_custom_call" | custom-call | bytes 10000000 | tf_op jit(solution)/shard_map/merge/pallas_call | solution.py:299
  116.6 1.9 %merge.3 = f32[400,4096]{1,0:T(8,128)} custom-call(s32[1]{0:T(128)} %bitcast.9.core_ref, bf16[32,200,128]{2,1,0:T(8,128)(2,1)S(1)} %collective-permute-done.9.in_ref, f32[400,4096]{1,0:T(8,128)} %merge.2.refs_0_), custom_call_target="tpu_custom_call", output_to_operand_aliasing={{}: (2, {})} | custom-call | bytes 10000000 | tf_op jit(solution)/shard_map/merge/pallas_call | solution.py:299
  (32 shorter events, 1.4 us)
Async XLA Ops:
  0.6 18.5 %collective-permute-start.1 = (bf16[400,512]{1,0:T(8,128)(2,1)}, bf16[400,512]{1,0:T(8,128)(2,1)S(1)}, u32[]{:S(2)}, u32[]{:S(2)}) collective-permute-start(bf16[400,512]{1,0:T(8,128)(2,1)} %bitcast.17), channel_id=1, source_target_pairs={{0,2},{2,4},{4,6},{6,8},{8,10},{10,12},{12,14},{14,16},{16,18},{18... | collective-permute-start | bytes 1228808 | tf_op jit(solution)/shard_map/ppermute | solution.py:327
  0.7 21.2 %collective-permute-start = (bf16[400,512]{1,0:T(8,128)(2,1)}, bf16[400,512]{1,0:T(8,128)(2,1)S(1)}, u32[]{:S(2)}, u32[]{:S(2)}) collective-permute-start(bf16[400,512]{1,0:T(8,128)(2,1)} %bitcast.18), channel_id=1, source_target_pairs={{0,254},{2,0},{4,2},{6,4},{8,6},{10,8},{12,10},{14,12},{16,14},{18... | collective-permute-start | bytes 1228808 | tf_op jit(solution)/shard_map/ppermute | solution.py:327
  10.1 0.7 copy-start.6
  10.8 1.9 %copy-start.9 = (bf16[4096,400]{0,1:T(8,128)(2,1)S(1)}, bf16[4096,400]{0,1:T(8,128)(2,1)}, u32[]{:S(2)}) copy-start(bf16[4096,400]{0,1:T(8,128)(2,1)} %param.11) | copy-start | bytes 9830404
  12.7 2.8 %copy-start = (bf16[1024,400]{0,1:T(8,128)(2,1)S(1)}, bf16[1024,400]{0,1:T(8,128)(2,1)}, u32[]{:S(2)}) copy-start(bf16[1024,400]{0,1:T(8,128)(2,1)} %param.10) | copy-start | bytes 2457604
  12.7 2.8 %copy-start.1 = (bf16[512,400]{0,1:T(8,128)(2,1)S(1)}, bf16[512,400]{0,1:T(8,128)(2,1)}, u32[]{:S(2)}) copy-start(bf16[512,400]{0,1:T(8,128)(2,1)} %param.9) | copy-start | bytes 1228804
  12.7 2.8 %copy-start.2 = (s32[1,1,3,512]{3,1,2,0:T(1,128)S(1)}, s32[1,1,3,512]{3,1,2,0:T(1,128)}, u32[]{:S(2)}) copy-start(s32[1,1,3,512]{3,1,2,0:T(1,128)} %param.15) | copy-start | bytes 18436
  12.7 2.8 %copy-start.3 = (s32[1,1,3,256]{3,1,2,0:T(1,128)S(1)}, s32[1,1,3,256]{3,1,2,0:T(1,128)}, u32[]{:S(2)}) copy-start(s32[1,1,3,256]{3,1,2,0:T(1,128)} %param.14) | copy-start | bytes 9220
  12.7 2.8 %copy-start.5 = (s32[1,1,3,256]{3,1,2,0:T(1,128)S(1)}, s32[1,1,3,256]{3,1,2,0:T(1,128)}, u32[]{:S(2)}) copy-start(s32[1,1,3,256]{3,1,2,0:T(1,128)} %param.12) | copy-start | bytes 9220
  12.7 2.8 %copy-start.8 = (s32[1,1,3]{2,1,0:T(1,128)S(1)}, s32[1,1,3]{2,1,0:T(1,128)}, u32[]{:S(2)}) copy-start(s32[1,1,3]{2,1,0:T(1,128)} %param.16) | copy-start | bytes 40
  21.9 2.8 %copy-start.4 = (s32[1024]{0:T(1024)S(1)}, s32[1024]{0:T(1024)}, u32[]{:S(2)}) copy-start(s32[1024]{0:T(1024)} %param.17) | copy-start | bytes 12292
  24.7 5.0 %copy-start.7 = (s32[1,1,3,256]{3,1,2,0:T(1,128)S(1)}, s32[1,1,3,256]{3,1,2,0:T(1,128)}, u32[]{:S(2)}) copy-start(s32[1,1,3,256]{3,1,2,0:T(1,128)} %param.13) | copy-start | bytes 9220
  26.3 3.4 %collective-permute-start.2 = (bf16[4544,128]{1,0:T(8,128)(2,1)S(1)}, bf16[4544,128]{1,0:T(8,128)(2,1)S(1)}, u32[]{:S(2)}, u32[]{:S(2)}) collective-permute-start(bf16[4544,128]{1,0:T(8,128)(2,1)S(1)} %get-tuple-element.47), channel_id=1, source_target_pairs={{0,2},{2,0},{1,3},{3,1},{4,6},{6,4},{5,7},{7,5},{8,10},{10,8},{9,1... | collective-permute-start | bytes 3489800 | tf_op jit(solution)/shard_map/ppermute | solution.py:407
  26.4 7.8 %collective-permute-start.4 = (bf16[400,512]{1,0:T(8,128)(2,1)S(1)}, bf16[400,512]{1,0:T(8,128)(2,1)}, u32[]{:S(2)}, u32[]{:S(2)}) collective-permute-start(bf16[400,512]{1,0:T(8,128)(2,1)S(1)} %get-tuple-element.57), channel_id=1, source_target_pairs={{0,254},{2,0},{4,2},{6,4},{8,6},{10,8},{12,10},{14,12},{16,14},{18... | collective-permute-start | bytes 1228808 | tf_op jit(solution)/shard_map/ppermute | solution.py:327
  28.7 13.2 %collective-permute-start.3 = (bf16[400,512]{1,0:T(8,128)(2,1)S(1)}, bf16[400,512]{1,0:T(8,128)(2,1)}, u32[]{:S(2)}, u32[]{:S(2)}) collective-permute-start(bf16[400,512]{1,0:T(8,128)(2,1)S(1)} %get-tuple-element.56), channel_id=1, source_target_pairs={{0,2},{2,4},{4,6},{6,8},{8,10},{10,12},{12,14},{14,16},{16,18},{18... | collective-permute-start | bytes 1228808 | tf_op jit(solution)/shard_map/ppermute | solution.py:327
  41.9 26.2 %all-to-all-start = ((bf16[32,256,128]{2,1,0:T(8,128)(2,1)}), bf16[32,256,128]{2,1,0:T(8,128)(2,1)S(1)}, u32[]{:S(2)}, u32[]{:S(2)}) async-start(bf16[32,256,128]{2,1,0:T(8,128)(2,1)} %spread.1), calls=%async_computation | async-start | bytes 4194304 | tf_op jit(solution)/shard_map/all_to_all | solution.py:425
  68.1 15.5 %collective-permute-start.8 = (bf16[400,512]{1,0:T(8,128)(2,1)S(1)}, bf16[400,512]{1,0:T(8,128)(2,1)S(1)}, u32[]{:S(2)}, u32[]{:S(2)}) collective-permute-start(bf16[400,512]{1,0:T(8,128)(2,1)S(1)} %add_convert_fusion), channel_id=1, source_target_pairs={{0,1},{1,0},{2,3},{3,2},{4,5},{5,4},{6,7},{7,6},{8,9},{9,8},{10,11... | collective-permute-start | bytes 1228808 | tf_op jit(solution)/shard_map/ppermute | solution.py:428
  68.5 8.2 %collective-permute-start.7 = (bf16[256,128]{1,0:T(8,128)(2,1)S(1)}, bf16[256,128]{1,0:T(8,128)(2,1)S(1)}, u32[]{:S(2)}, u32[]{:S(2)}) collective-permute-start(bf16[256,128]{1,0:T(8,128)(2,1)S(1)} %near_sum.1.r0), channel_id=1, source_target_pairs={{0,24},{8,0},{16,8},{24,16},{1,25},{9,1},{17,9},{25,17},{2,26},{10... | collective-permute-start | bytes 196616 | tf_op jit(solution)/shard_map/ppermute | solution.py:327
  68.5 11.7 %collective-permute-start.6 = (bf16[256,128]{1,0:T(8,128)(2,1)S(1)}, bf16[256,128]{1,0:T(8,128)(2,1)S(1)}, u32[]{:S(2)}, u32[]{:S(2)}) collective-permute-start(bf16[256,128]{1,0:T(8,128)(2,1)S(1)} %near_sum.1.r0), channel_id=1, source_target_pairs={{0,16},{8,24},{16,0},{24,8},{1,17},{9,25},{17,1},{25,9},{2,18},{10... | collective-permute-start | bytes 196616 | tf_op jit(solution)/shard_map/ppermute | solution.py:327
  76.5 7.1 %collective-permute-start.5 = (bf16[256,128]{1,0:T(8,128)(2,1)S(1)}, bf16[256,128]{1,0:T(8,128)(2,1)S(1)}, u32[]{:S(2)}, u32[]{:S(2)}) collective-permute-start(bf16[256,128]{1,0:T(8,128)(2,1)S(1)} %near_sum.1.r0), channel_id=1, source_target_pairs={{0,8},{8,16},{16,24},{24,0},{1,9},{9,17},{17,25},{25,1},{2,10},{10... | collective-permute-start | bytes 196616 | tf_op jit(solution)/shard_map/ppermute | solution.py:327
  113.1 3.5 %collective-permute-start.9 = (bf16[32,200,128]{2,1,0:T(8,128)(2,1)S(1)}, bf16[32,200,128]{2,1,0:T(8,128)(2,1)S(1)}, u32[]{:S(2)}, u32[]{:S(2)}) collective-permute-start(bf16[32,200,128]{2,1,0:T(8,128)(2,1)S(1)} %all_to_all.10.in_ref), channel_id=1, source_target_pairs={{0,2},{2,0},{1,3},{3,1},{4,6},{6,4},{5,7},{7,5},{8,10},{10,8},{9,1... | collective-permute-start | bytes 4915208 | tf_op jit(solution)/shard_map/ppermute | solution.py:450

commit v5 on v4

--- a/solution.py
+++ b/solution.py
@@ -253,14 +253,13 @@
     out_ref[...] = total.astype(BF16)
 
 
-def quad_sum_kernel(r0, r1, r2, r3, place_ref, rel_ref, hot_ref, held):
+def pair_sum_kernel(mine_ref, got_ref, out_ref):
+    out_ref[...] = (mine_ref[...].astype(F32) + got_ref[...].astype(F32)).astype(BF16)
+
+
+def quad_sum_kernel(mine_ref, got_ref, place_ref, rel_ref, hot_ref):
     place = place_ref[0]
-    for n, ref in enumerate((r0, r1, r2, r3)):
-        held[n] = ref[...]
-    total = None
-    for source in range(QUAD):
-        piece = held[jnp.bitwise_and(place - source, QUAD - 1)].astype(F32)
-        total = piece if total is None else total + piece
+    total = mine_ref[...].astype(F32) + got_ref[...].astype(F32)
     rel = total[:HALF_D].astype(BF16)
     for j in range(GROUP):
         rel_ref[j] = rel
@@ -434,18 +433,26 @@
         compiler_params=PARAMS,
         name="near_sum",
     )(slabs)
-    pieces = [pieces] + [moved(pieces, "zh", QUAD, n) for n in range(1, QUAD)]
+    beside = lax.ppermute(pieces, "zh", [(i, i ^ 1) for i in range(QUAD)])
+    pieces = pl.pallas_call(
+        pair_sum_kernel,
+        out_shape=struct((SLAB, LANES), BF16),
+        in_specs=[VMEM] * 2,
+        out_specs=VMEM,
+        compiler_params=PARAMS,
+        name="pair_sum",
+    )(pieces, beside)
+    across = lax.ppermute(pieces, "zh", [(i, i ^ 3) for i in range(QUAD)])
     place = lax.axis_index("zh").astype(jnp.int32).reshape(1)
-    pieces, twin = lax.optimization_barrier((pieces, twin))
+    across, twin = lax.optimization_barrier((across, twin))
     column, hot_grad = pl.pallas_call(
         quad_sum_kernel,
         out_shape=(struct((GROUP, HALF_D, LANES), BF16), struct((4, D), F32)),
-        in_specs=[VMEM] * QUAD + [SMEM],
+        in_specs=[VMEM] * 2 + [SMEM],
         out_specs=(VMEM, VMEM),
-        scratch_shapes=[pltpu.VMEM((QUAD, SLAB, LANES), BF16)],
         compiler_params=PARAMS,
         name="quad_sum",
-    )(*pieces, place)
+    )(pieces, across, place)
     mine = lax.all_to_all(column, NEAR, 0, 0, tiled=True)
     other = lax.ppermute(mine, "core", swap)
     relation_grad = merged(core, other, merged(core, mine, None))

time: 121 us -> 118 us (0.975)
  starting transfers between devices: 25.1 us -> 19.9 us
  waiting for transfers between devices: 36.1 us -> 39.1 us
  blocking collectives: 28.7 us -> 27.3 us
    ppermute x0 -> x2, waiting for transfers between devices: none -> 10.2 us  [the longest x1 5.21 us: shards(): beside = lax.ppermute(pieces, 'zh', [(i, i ^ 1) for i in range(QUAD)])]
    ppermute x7 -> x4, starting transfers between devices: 19.9 us -> 11.8 us  [moved(): lax.ppermute(value, axis, [(i, (i + steps) % count) for i in range(count)])]
    ppermute x7 -> x4, waiting for transfers between devices: 15.7 us -> 7.85 us  [moved(): lax.ppermute(value, axis, [(i, (i + steps) % count) for i in range(count)])]
    ppermute x0 -> x2, starting transfers between devices: none -> 2.9 us  [the longest x1 1.49 us: shards(): across = lax.ppermute(pieces, 'zh', [(i, i ^ 3) for i in range(QUAD)])]
    all_to_all x1, blocking collectives: 28.7 us -> 27.3 us  [shards(): mine = lax.all_to_all(column, NEAR, 0, 0, tiled=True)]
    unnamed x20 -> x22, local copies, waits for them, and re-layouts: 2.65 us -> 3.4 us
  transfers between devices with their start and end apart: 11 -> 10, of which waited for: 7 -> 6; matrix products, arithmetic and copies ran while one was open for 2% -> 2% of each run, Pallas kernels for 13% -> 14%
where the time goes in v5:
time: 118 us; the launch traced here: 116 us
  waiting for transfers between devices  39.1 us (33%)
  blocking collectives  27.3 us (23%)
  Pallas kernels  22.9 us (19%)
  starting transfers between devices  19.9 us (17%)
  local copies, waits for them, and re-layouts  3.4 us (3%)
  other arithmetic  2.3 us (2%)
    all_to_all x1, blocking collectives, shards(): mine = lax.all_to_all(column, NEAR, 0, 0, tiled=True)  27.3 us
    all_to_all x1, waiting for transfers between devices, shards(): slabs = lax.all_to_all(slabs, NEAR, 0, 0, tiled=True)  20.4 us
    ppermute x4, starting transfers between devices, moved(): lax.ppermute(value, axis, [(i, (i + steps) % count) for i in range(count)])  11.8 us
    ppermute x4, waiting for transfers between devices, moved(): lax.ppermute(value, axis, [(i, (i + steps) % count) for i in range(count)])  7.85 us
    pallas_call x2, Pallas kernels, back(): pl.pallas_call(functools.partial(back_kernel, k), out_shape=(half, half,...  5.61 us
    ppermute x1, waiting for transfers between devices, shards(): beside = lax.ppermute(pieces, 'zh', [(i, i ^ 1) for i in range(QUAD)])  5.21 us
    all_to_all x1, starting transfers between devices, shards(): slabs = lax.all_to_all(slabs, NEAR, 0, 0, tiled=True)  5.11 us
    ppermute x1, waiting for transfers between devices, shards(): across = lax.ppermute(pieces, 'zh', [(i, i ^ 3) for i in range(QUAD)])  4.97 us
  transfers between devices with their start and end apart: 10, of which 6 were waited for; matrix products, arithmetic and copies ran while one was open for 2% of the time, Pallas kernels for 14%

profile of v5, /device:TPU:2, one launch (start us, length us, event | category | flops | bytes accessed | tf_op | source)
XLA Modules:
  0.0 115.6 jit_solution(90701825532287524)
XLA Ops:
  0.7 9.4 %collective-permute-start = (bf16[400,512]{1,0:T(8,128)(2,1)}, bf16[400,512]{1,0:T(8,128)(2,1)S(1)}, u32[]{:S(2)}, u32[]{:S(2)}) collective-permute-start(bf16[400,512]{1,0:T(8,128)(2,1)} %bitcast.18), channel_id=1, source_target_pairs={{0,254},{2,0},{4,2},{6,4},{8,6},{10,8},{12,10},{14,12},{16,14},{18... | collective-permute-start | bytes 1228808 | tf_op jit(solution)/shard_map/ppermute | solution.py:326
  10.8 1.9 %copy-done.9 = bf16[4096,400]{0,1:T(8,128)(2,1)S(1)} copy-done((bf16[4096,400]{0,1:T(8,128)(2,1)S(1)}, bf16[4096,400]{0,1:T(8,128)(2,1)}, u32[]{:S(2)}) %copy-start.9) | copy-done | bytes 3276824
  12.7 2.8 %lookup.1.rel_ref = bf16[400,768]{1,0:T(8,128)(2,1)S(1)} custom-call(bf16[400,4096]{1,0:T(8,128)(2,1)S(1)} %bitcast.36, s32[1,768]{1,0:T(1,128)S(1)} %bitcast.30), custom_call_target="tpu_custom_call" | custom-call | flops 3000000000 | bytes 10000000 | tf_op jit(solution)/shard_map/lookup/pallas_call | solution.py:344
  15.6 3.6 %front.1 = (bf16[400,768]{1,0:T(8,128)(2,1)S(1)}, bf16[400,768]{1,0:T(8,128)(2,1)S(1)}, bf16[768,400]{1,0:T(8,128)(2,1)S(1)}, bf16[400,256]{1,0:T(8,128)(2,1)S(1...) custom-call(bf16[400,768]{1,0:T(8,128)(2,1)S(1)} %lookup.1.rel_ref, bf16[400,512]{1,0:T(8,128)(2,1)S(1)} %bitcast.19, ...), custom_call_target="tpu_custom_call" | custom-call | flops 100000000 | bytes 1000000 | tf_op jit(solution)/shard_map/front/pallas_call | solution.py:356
  19.2 2.8 %back.3 = (bf16[400,256]{1,0:T(8,128)(2,1)S(1)}, bf16[400,256]{1,0:T(8,128)(2,1)S(1)}, bf16[256,1024]{1,0:T(8,128)(2,1)S(1)}, bf16[400,512]{1,0:T(8,128)(2,1)S(1)}) custom-call(bf16[400,512]{1,0:T(8,128)(2,1)S(1)} %collective-permute-done.1.far_ref, bf16[400,1024]{1,0:T(8,128)(2,1)S(1)} %bitcast.15, bf16[400,768]{1,0:T(8,128)(2,1)S(1)} %get-tuple-element.34.src_ref, ...), custom_call_target="tpu_custom_call" | custom-call | flops 100000000 | bytes 1000000 | tf_op jit(solution)/shard_map/back/pallas_call | solution.py:370
  22.0 2.8 %back.2 = (bf16[400,256]{1,0:T(8,128)(2,1)S(1)}, bf16[400,256]{1,0:T(8,128)(2,1)S(1)}, bf16[256,1024]{1,0:T(8,128)(2,1)S(1)}, bf16[400,512]{1,0:T(8,128)(2,1)S(1)}) custom-call(bf16[400,512]{1,0:T(8,128)(2,1)S(1)} %collective-permute-done.far_ref, bf16[400,1024]{1,0:T(8,128)(2,1)S(1)} %bitcast.16, bf16[400,768]{1,0:T(8,128)(2,1)S(1)} %get-tuple-element.34.src_ref, ...), custom_call_target="tpu_custom_call" | custom-call | flops 100000000 | bytes 1000000 | tf_op jit(solution)/shard_map/back/pallas_call | solution.py:370
  24.8 1.6 %pack.1 = (bf16[4544,128]{1,0:T(8,128)(2,1)S(1)}, bf16[400,768]{1,0:T(8,128)(2,1)S(1)}, bf16[400,1024]{1,0:T(8,128)(2,1)S(1)}) custom-call(bf16[400,256]{1,0:T(8,128)(2,1)S(1)} %get-tuple-element.37.gr0_ref, bf16[400,256]{1,0:T(8,128)(2,1)S(1)} %get-tuple-element.38.gr1_ref, bf16[400,256]{1,0:T(8,128)(2,1)S(1)} %get-tuple-element.39.gr2_ref, ...), custom_call_target="tpu_custom_call" | custom-call | flops 100000000 | bytes 1000000 | tf_op jit(solution)/shard_map/pack/pallas_call | solution.py:384
  26.5 2.3 %collective-permute-start.4 = (bf16[400,512]{1,0:T(8,128)(2,1)S(1)}, bf16[400,512]{1,0:T(8,128)(2,1)S(1)}, u32[]{:S(2)}, u32[]{:S(2)}) collective-permute-start(bf16[400,512]{1,0:T(8,128)(2,1)S(1)} %get-tuple-element.54), channel_id=1, source_target_pairs={{0,254},{2,0},{4,2},{6,4},{8,6},{10,8},{12,10},{14,12},{16,14},{18... | collective-permute-start | bytes 1228808 | tf_op jit(solution)/shard_map/ppermute | solution.py:326
  28.8 1.0 tail.1
  29.8 3.6 %spread.1 = bf16[32,256,128]{2,1,0:T(8,128)(2,1)} custom-call(bf16[400,768]{1,0:T(8,128)(2,1)S(1)} %get-tuple-element.43.grad_ref, s32[1,768]{1,0:T(1,128)S(1)} %bitcast.32, bf16[4544,128]{1,0:T(8,128)(2,1)S(1)} %collective-permute-done.2.got_ref, bf16[2048,128]{1,0:T(8,128)(2,1)S(1)} %get-tuple-element.52.hot_ref, s32[1]{0:T(128)} %bitcast.9.core_ref), custom_call_target="tpu_custom_call" | custom-call | flops 100000000 | bytes 1000000 | tf_op jit(solution)/shard_map/spread/pallas_call | solution.py:408
  33.4 0.9 collective-permute-done.4
  34.3 0.7 copy-done.10
  35.0 7.0 %collective-permute-done.3 = bf16[400,512]{1,0:T(8,128)(2,1)} collective-permute-done((bf16[400,512]{1,0:T(8,128)(2,1)S(1)}, bf16[400,512]{1,0:T(8,128)(2,1)}, u32[]{:S(2)}, u32[]{:S(2)}) %collective-permute-start.3) | collective-permute-done | bytes 409632 | tf_op jit(solution)/shard_map/ppermute | solution.py:326
  42.0 5.1 %all-to-all-start = ((bf16[32,256,128]{2,1,0:T(8,128)(2,1)}), bf16[32,256,128]{2,1,0:T(8,128)(2,1)S(1)}, u32[]{:S(2)}, u32[]{:S(2)}) async-start(bf16[32,256,128]{2,1,0:T(8,128)(2,1)} %spread.1), calls=%async_computation | async-start | bytes 4194304 | tf_op jit(solution)/shard_map/all_to_all | solution.py:424
  47.1 1.3 %add_convert_fusion = bf16[400,512]{1,0:T(8,128)(2,1)S(1)} fusion(bf16[400,512]{1,0:T(8,128)(2,1)} %copy-done.10, f32[400,512]{1,0:T(8,128)S(1)} %get-tuple-element.56, bf16[400,512]{1,0:T(8,128)(2,1)} %collective-permute-done.3), kind=kLoop, calls=%fused_computation.1 | loop fusion | flops 1024000 | bytes 2048000 | tf_op jit(solution)/shard_map/convert_element_type | solution.py:425
  48.4 20.4 %all-to-all-done.in_ref = bf16[32,256,128]{2,1,0:T(8,128)(2,1)S(1)} async-done(((bf16[32,256,128]{2,1,0:T(8,128)(2,1)}), bf16[32,256,128]{2,1,0:T(8,128)(2,1)S(1)}, u32[]{:S(2)}, u32[]{:S(2)}) %all-to-all-start) | async-done | bytes 2097184 | tf_op jit(solution)/shard_map/all_to_all | solution.py:424
  69.1 1.4 %collective-permute-start.5 = (bf16[256,128]{1,0:T(8,128)(2,1)S(1)}, bf16[256,128]{1,0:T(8,128)(2,1)S(1)}, u32[]{:S(2)}, u32[]{:S(2)}) collective-permute-start(bf16[256,128]{1,0:T(8,128)(2,1)S(1)} %near_sum.1.mine_ref), channel_id=1, source_target_pairs={{0,8},{8,0},{16,24},{24,16},{1,9},{9,1},{17,25},{25,17},{2,10},{10... | collective-permute-start | bytes 196616 | tf_op jit(solution)/shard_map/ppermute | solution.py:436
  70.5 5.2 %collective-permute-done.5.got_ref = bf16[256,128]{1,0:T(8,128)(2,1)S(1)} collective-permute-done((bf16[256,128]{1,0:T(8,128)(2,1)S(1)}, bf16[256,128]{1,0:T(8,128)(2,1)S(1)}, u32[]{:S(2)}, u32[]{:S(2)}) %collective-permute-start.5) | collective-permute-done | bytes 65568 | tf_op jit(solution)/shard_map/ppermute | solution.py:436
  75.8 1.5 %collective-permute-start.6 = (bf16[256,128]{1,0:T(8,128)(2,1)S(1)}, bf16[256,128]{1,0:T(8,128)(2,1)S(1)}, u32[]{:S(2)}, u32[]{:S(2)}) collective-permute-start(bf16[256,128]{1,0:T(8,128)(2,1)S(1)} %pair_sum.1.mine_ref), channel_id=1, source_target_pairs={{0,24},{8,16},{16,8},{24,0},{1,25},{9,17},{17,9},{25,1},{2,26},{10... | collective-permute-start | bytes 196616 | tf_op jit(solution)/shard_map/ppermute | solution.py:445
  77.3 5.0 %collective-permute-done.6.got_ref = bf16[256,128]{1,0:T(8,128)(2,1)S(1)} collective-permute-done((bf16[256,128]{1,0:T(8,128)(2,1)S(1)}, bf16[256,128]{1,0:T(8,128)(2,1)S(1)}, u32[]{:S(2)}, u32[]{:S(2)}) %collective-permute-start.6) | collective-permute-done | bytes 65568 | tf_op jit(solution)/shard_map/ppermute | solution.py:445
  83.0 27.3 %all_to_all.10.in_ref = bf16[32,200,128]{2,1,0:T(8,128)(2,1)S(1)} all-to-all(bf16[32,200,128]{2,1,0:T(8,128)(2,1)S(1)} %get-tuple-element.63), channel_id=1, replica_groups=mesh['y'=4,'xh'=2,'zh'=4,'zl'=2,'core'=2,'rep'=2] {'y','xh','zl','rep'}, dimensions={0} | all-to-all | bytes 3276800 | tf_op jit(solution)/shard_map/all_to_all | solution.py:456
  110.2 1.0 add_bitcast_fusion
  111.2 1.9 %merge.2.refs_0_ = f32[400,4096]{1,0:T(8,128)} custom-call(s32[1]{0:T(128)} %bitcast.9.core_ref, bf16[32,200,128]{2,1,0:T(8,128)(2,1)S(1)} %all_to_all.10.in_ref), custom_call_target="tpu_custom_call" | custom-call | bytes 10000000 | tf_op jit(solution)/shard_map/merge/pallas_call | solution.py:298
  113.7 1.9 %merge.3 = f32[400,4096]{1,0:T(8,128)} custom-call(s32[1]{0:T(128)} %bitcast.9.core_ref, bf16[32,200,128]{2,1,0:T(8,128)(2,1)S(1)} %collective-permute-done.8.in_ref, f32[400,4096]{1,0:T(8,128)} %merge.2.refs_0_), custom_call_target="tpu_custom_call", output_to_operand_aliasing={{}: (2, {})} | custom-call | bytes 10000000 | tf_op jit(solution)/shard_map/merge/pallas_call | solution.py:298
  (33 shorter events, 2.5 us)
Async XLA Ops:
  0.6 18.5 %collective-permute-start.1 = (bf16[400,512]{1,0:T(8,128)(2,1)}, bf16[400,512]{1,0:T(8,128)(2,1)S(1)}, u32[]{:S(2)}, u32[]{:S(2)}) collective-permute-start(bf16[400,512]{1,0:T(8,128)(2,1)} %bitcast.17), channel_id=1, source_target_pairs={{0,2},{2,4},{4,6},{6,8},{8,10},{10,12},{12,14},{14,16},{16,18},{18... | collective-permute-start | bytes 1228808 | tf_op jit(solution)/shard_map/ppermute | solution.py:326
  0.7 21.3 %collective-permute-start = (bf16[400,512]{1,0:T(8,128)(2,1)}, bf16[400,512]{1,0:T(8,128)(2,1)S(1)}, u32[]{:S(2)}, u32[]{:S(2)}) collective-permute-start(bf16[400,512]{1,0:T(8,128)(2,1)} %bitcast.18), channel_id=1, source_target_pairs={{0,254},{2,0},{4,2},{6,4},{8,6},{10,8},{12,10},{14,12},{16,14},{18... | collective-permute-start | bytes 1228808 | tf_op jit(solution)/shard_map/ppermute | solution.py:326
  10.1 0.7 copy-start.6
  10.8 1.9 %copy-start.9 = (bf16[4096,400]{0,1:T(8,128)(2,1)S(1)}, bf16[4096,400]{0,1:T(8,128)(2,1)}, u32[]{:S(2)}) copy-start(bf16[4096,400]{0,1:T(8,128)(2,1)} %param.11) | copy-start | bytes 9830404
  12.7 2.8 %copy-start = (bf16[1024,400]{0,1:T(8,128)(2,1)S(1)}, bf16[1024,400]{0,1:T(8,128)(2,1)}, u32[]{:S(2)}) copy-start(bf16[1024,400]{0,1:T(8,128)(2,1)} %param.10) | copy-start | bytes 2457604
  12.7 2.8 %copy-start.1 = (bf16[512,400]{0,1:T(8,128)(2,1)S(1)}, bf16[512,400]{0,1:T(8,128)(2,1)}, u32[]{:S(2)}) copy-start(bf16[512,400]{0,1:T(8,128)(2,1)} %param.9) | copy-start | bytes 1228804
  12.7 2.8 %copy-start.2 = (s32[1,1,3,512]{3,1,2,0:T(1,128)S(1)}, s32[1,1,3,512]{3,1,2,0:T(1,128)}, u32[]{:S(2)}) copy-start(s32[1,1,3,512]{3,1,2,0:T(1,128)} %param.15) | copy-start | bytes 18436
  12.7 2.8 %copy-start.3 = (s32[1,1,3,256]{3,1,2,0:T(1,128)S(1)}, s32[1,1,3,256]{3,1,2,0:T(1,128)}, u32[]{:S(2)}) copy-start(s32[1,1,3,256]{3,1,2,0:T(1,128)} %param.14) | copy-start | bytes 9220
  12.7 2.8 %copy-start.5 = (s32[1,1,3,256]{3,1,2,0:T(1,128)S(1)}, s32[1,1,3,256]{3,1,2,0:T(1,128)}, u32[]{:S(2)}) copy-start(s32[1,1,3,256]{3,1,2,0:T(1,128)} %param.12) | copy-start | bytes 9220
  12.7 2.8 %copy-start.8 = (s32[1,1,3]{2,1,0:T(1,128)S(1)}, s32[1,1,3]{2,1,0:T(1,128)}, u32[]{:S(2)}) copy-start(s32[1,1,3]{2,1,0:T(1,128)} %param.16) | copy-start | bytes 40
  22.0 2.8 %copy-start.4 = (s32[1024]{0:T(1024)S(1)}, s32[1024]{0:T(1024)}, u32[]{:S(2)}) copy-start(s32[1024]{0:T(1024)} %param.17) | copy-start | bytes 12292
  24.8 5.0 %copy-start.7 = (s32[1,1,3,256]{3,1,2,0:T(1,128)S(1)}, s32[1,1,3,256]{3,1,2,0:T(1,128)}, u32[]{:S(2)}) copy-start(s32[1,1,3,256]{3,1,2,0:T(1,128)} %param.13) | copy-start | bytes 9220
  26.4 3.4 %collective-permute-start.2 = (bf16[4544,128]{1,0:T(8,128)(2,1)S(1)}, bf16[4544,128]{1,0:T(8,128)(2,1)S(1)}, u32[]{:S(2)}, u32[]{:S(2)}) collective-permute-start(bf16[4544,128]{1,0:T(8,128)(2,1)S(1)} %get-tuple-element.44), channel_id=1, source_target_pairs={{0,2},{2,0},{1,3},{3,1},{4,6},{6,4},{5,7},{7,5},{8,10},{10,8},{9,1... | collective-permute-start | bytes 3489800 | tf_op jit(solution)/shard_map/ppermute | solution.py:406
  26.5 7.8 %collective-permute-start.4 = (bf16[400,512]{1,0:T(8,128)(2,1)S(1)}, bf16[400,512]{1,0:T(8,128)(2,1)S(1)}, u32[]{:S(2)}, u32[]{:S(2)}) collective-permute-start(bf16[400,512]{1,0:T(8,128)(2,1)S(1)} %get-tuple-element.54), channel_id=1, source_target_pairs={{0,254},{2,0},{4,2},{6,4},{8,6},{10,8},{12,10},{14,12},{16,14},{18... | collective-permute-start | bytes 1228808 | tf_op jit(solution)/shard_map/ppermute | solution.py:326
  28.8 13.2 %collective-permute-start.3 = (bf16[400,512]{1,0:T(8,128)(2,1)S(1)}, bf16[400,512]{1,0:T(8,128)(2,1)}, u32[]{:S(2)}, u32[]{:S(2)}) collective-permute-start(bf16[400,512]{1,0:T(8,128)(2,1)S(1)} %get-tuple-element.53), channel_id=1, source_target_pairs={{0,2},{2,4},{4,6},{6,8},{8,10},{10,12},{12,14},{14,16},{16,18},{18... | collective-permute-start | bytes 1228808 | tf_op jit(solution)/shard_map/ppermute | solution.py:326
  34.3 0.8 copy-start.10
  42.0 26.8 %all-to-all-start = ((bf16[32,256,128]{2,1,0:T(8,128)(2,1)}), bf16[32,256,128]{2,1,0:T(8,128)(2,1)S(1)}, u32[]{:S(2)}, u32[]{:S(2)}) async-start(bf16[32,256,128]{2,1,0:T(8,128)(2,1)} %spread.1), calls=%async_computation | async-start | bytes 4194304 | tf_op jit(solution)/shard_map/all_to_all | solution.py:424
  68.9 13.4 %collective-permute-start.7 = (bf16[400,512]{1,0:T(8,128)(2,1)S(1)}, bf16[400,512]{1,0:T(8,128)(2,1)S(1)}, u32[]{:S(2)}, u32[]{:S(2)}) collective-permute-start(bf16[400,512]{1,0:T(8,128)(2,1)S(1)} %add_convert_fusion), channel_id=1, source_target_pairs={{0,1},{1,0},{2,3},{3,2},{4,5},{5,4},{6,7},{7,6},{8,9},{9,8},{10,11... | collective-permute-start | bytes 1228808 | tf_op jit(solution)/shard_map/ppermute | solution.py:427
  69.1 6.6 %collective-permute-start.5 = (bf16[256,128]{1,0:T(8,128)(2,1)S(1)}, bf16[256,128]{1,0:T(8,128)(2,1)S(1)}, u32[]{:S(2)}, u32[]{:S(2)}) collective-permute-start(bf16[256,128]{1,0:T(8,128)(2,1)S(1)} %near_sum.1.mine_ref), channel_id=1, source_target_pairs={{0,8},{8,0},{16,24},{24,16},{1,9},{9,1},{17,25},{25,17},{2,10},{10... | collective-permute-start | bytes 196616 | tf_op jit(solution)/shard_map/ppermute | solution.py:436
  75.8 6.5 %collective-permute-start.6 = (bf16[256,128]{1,0:T(8,128)(2,1)S(1)}, bf16[256,128]{1,0:T(8,128)(2,1)S(1)}, u32[]{:S(2)}, u32[]{:S(2)}) collective-permute-start(bf16[256,128]{1,0:T(8,128)(2,1)S(1)} %pair_sum.1.mine_ref), channel_id=1, source_target_pairs={{0,24},{8,16},{16,8},{24,0},{1,25},{9,17},{17,9},{25,1},{2,26},{10... | collective-permute-start | bytes 196616 | tf_op jit(solution)/shard_map/ppermute | solution.py:445
  110.2 3.5 %collective-permute-start.8 = (bf16[32,200,128]{2,1,0:T(8,128)(2,1)S(1)}, bf16[32,200,128]{2,1,0:T(8,128)(2,1)S(1)}, u32[]{:S(2)}, u32[]{:S(2)}) collective-permute-start(bf16[32,200,128]{2,1,0:T(8,128)(2,1)S(1)} %all_to_all.10.in_ref), channel_id=1, source_target_pairs={{0,2},{2,0},{1,3},{3,1},{4,6},{6,4},{5,7},{7,5},{8,10},{10,8},{9,1... | collective-permute-start | bytes 4915208 | tf_op jit(solution)/shard_map/ppermute | solution.py:457

commit v6 on v5

--- a/solution.py
+++ b/solution.py
@@ -444,7 +444,6 @@
     )(pieces, beside)
     across = lax.ppermute(pieces, "zh", [(i, i ^ 3) for i in range(QUAD)])
     place = lax.axis_index("zh").astype(jnp.int32).reshape(1)
-    across, twin = lax.optimization_barrier((across, twin))
     column, hot_grad = pl.pallas_call(
         quad_sum_kernel,
         out_shape=(struct((GROUP, HALF_D, LANES), BF16), struct((4, D), F32)),
@@ -453,6 +452,7 @@
         compiler_params=PARAMS,
         name="quad_sum",
     )(pieces, across, place)
+    column, twin = lax.optimization_barrier((column, twin))
     mine = lax.all_to_all(column, NEAR, 0, 0, tiled=True)
     other = lax.ppermute(mine, "core", swap)
     relation_grad = merged(core, other, merged(core, mine, None))

time: 118 us -> 118 us (level)
  no operation moved by 1% of the time
where the time goes in v6:
time: 118 us; the launch traced here: 116 us
  waiting for transfers between devices  39.1 us (33%)
  blocking collectives  27.3 us (23%)
  Pallas kernels  22.9 us (19%)
  starting transfers between devices  19.9 us (17%)
  local copies, waits for them, and re-layouts  3.4 us (3%)
  other arithmetic  2.3 us (2%)
    all_to_all x1, blocking collectives, shards(): mine = lax.all_to_all(column, NEAR, 0, 0, tiled=True)  27.3 us
    all_to_all x1, waiting for transfers between devices, shards(): slabs = lax.all_to_all(slabs, NEAR, 0, 0, tiled=True)  20.4 us
    ppermute x4, starting transfers between devices, moved(): lax.ppermute(value, axis, [(i, (i + steps) % count) for i in range(count)])  11.8 us
    ppermute x4, waiting for transfers between devices, moved(): lax.ppermute(value, axis, [(i, (i + steps) % count) for i in range(count)])  7.85 us
    pallas_call x2, Pallas kernels, back(): pl.pallas_call(functools.partial(back_kernel, k), out_shape=(half, half,...  5.61 us
    ppermute x1, waiting for transfers between devices, shards(): beside = lax.ppermute(pieces, 'zh', [(i, i ^ 1) for i in range(QUAD)])  5.21 us
    all_to_all x1, starting transfers between devices, shards(): slabs = lax.all_to_all(slabs, NEAR, 0, 0, tiled=True)  5.11 us
    ppermute x1, waiting for transfers between devices, shards(): across = lax.ppermute(pieces, 'zh', [(i, i ^ 3) for i in range(QUAD)])  4.97 us
  transfers between devices with their start and end apart: 10, of which 6 were waited for; matrix products, arithmetic and copies ran while one was open for 2% of the time, Pallas kernels for 14%

profile of v6, /device:TPU:2, one launch (start us, length us, event | category | flops | bytes accessed | tf_op | source)
XLA Modules:
  0.0 115.6 jit_solution(4215901395082642840)
XLA Ops:
  0.7 9.4 %collective-permute-start = (bf16[400,512]{1,0:T(8,128)(2,1)}, bf16[400,512]{1,0:T(8,128)(2,1)S(1)}, u32[]{:S(2)}, u32[]{:S(2)}) collective-permute-start(bf16[400,512]{1,0:T(8,128)(2,1)} %bitcast.18), channel_id=1, source_target_pairs={{0,254},{2,0},{4,2},{6,4},{8,6},{10,8},{12,10},{14,12},{16,14},{18... | collective-permute-start | bytes 1228808 | tf_op jit(solution)/shard_map/ppermute | solution.py:326
  10.8 1.9 %copy-done.9 = bf16[4096,400]{0,1:T(8,128)(2,1)S(1)} copy-done((bf16[4096,400]{0,1:T(8,128)(2,1)S(1)}, bf16[4096,400]{0,1:T(8,128)(2,1)}, u32[]{:S(2)}) %copy-start.9) | copy-done | bytes 3276824
  12.7 2.8 %lookup.1.rel_ref = bf16[400,768]{1,0:T(8,128)(2,1)S(1)} custom-call(bf16[400,4096]{1,0:T(8,128)(2,1)S(1)} %bitcast.36, s32[1,768]{1,0:T(1,128)S(1)} %bitcast.30), custom_call_target="tpu_custom_call" | custom-call | flops 3000000000 | bytes 10000000 | tf_op jit(solution)/shard_map/lookup/pallas_call | solution.py:344
  15.6 3.6 %front.1 = (bf16[400,768]{1,0:T(8,128)(2,1)S(1)}, bf16[400,768]{1,0:T(8,128)(2,1)S(1)}, bf16[768,400]{1,0:T(8,128)(2,1)S(1)}, bf16[400,256]{1,0:T(8,128)(2,1)S(1...) custom-call(bf16[400,768]{1,0:T(8,128)(2,1)S(1)} %lookup.1.rel_ref, bf16[400,512]{1,0:T(8,128)(2,1)S(1)} %bitcast.19, ...), custom_call_target="tpu_custom_call" | custom-call | flops 100000000 | bytes 1000000 | tf_op jit(solution)/shard_map/front/pallas_call | solution.py:356
  19.2 2.8 %back.3 = (bf16[400,256]{1,0:T(8,128)(2,1)S(1)}, bf16[400,256]{1,0:T(8,128)(2,1)S(1)}, bf16[256,1024]{1,0:T(8,128)(2,1)S(1)}, bf16[400,512]{1,0:T(8,128)(2,1)S(1)}) custom-call(bf16[400,512]{1,0:T(8,128)(2,1)S(1)} %collective-permute-done.1.far_ref, bf16[400,1024]{1,0:T(8,128)(2,1)S(1)} %bitcast.15, bf16[400,768]{1,0:T(8,128)(2,1)S(1)} %get-tuple-element.34.src_ref, ...), custom_call_target="tpu_custom_call" | custom-call | flops 100000000 | bytes 1000000 | tf_op jit(solution)/shard_map/back/pallas_call | solution.py:370
  22.0 2.8 %back.2 = (bf16[400,256]{1,0:T(8,128)(2,1)S(1)}, bf16[400,256]{1,0:T(8,128)(2,1)S(1)}, bf16[256,1024]{1,0:T(8,128)(2,1)S(1)}, bf16[400,512]{1,0:T(8,128)(2,1)S(1)}) custom-call(bf16[400,512]{1,0:T(8,128)(2,1)S(1)} %collective-permute-done.far_ref, bf16[400,1024]{1,0:T(8,128)(2,1)S(1)} %bitcast.16, bf16[400,768]{1,0:T(8,128)(2,1)S(1)} %get-tuple-element.34.src_ref, ...), custom_call_target="tpu_custom_call" | custom-call | flops 100000000 | bytes 1000000 | tf_op jit(solution)/shard_map/back/pallas_call | solution.py:370
  24.8 1.6 %pack.1 = (bf16[4544,128]{1,0:T(8,128)(2,1)S(1)}, bf16[400,768]{1,0:T(8,128)(2,1)S(1)}, bf16[400,1024]{1,0:T(8,128)(2,1)S(1)}) custom-call(bf16[400,256]{1,0:T(8,128)(2,1)S(1)} %get-tuple-element.37.gr0_ref, bf16[400,256]{1,0:T(8,128)(2,1)S(1)} %get-tuple-element.38.gr1_ref, bf16[400,256]{1,0:T(8,128)(2,1)S(1)} %get-tuple-element.39.gr2_ref, ...), custom_call_target="tpu_custom_call" | custom-call | flops 100000000 | bytes 1000000 | tf_op jit(solution)/shard_map/pack/pallas_call | solution.py:384
  26.5 2.3 %collective-permute-start.4 = (bf16[400,512]{1,0:T(8,128)(2,1)S(1)}, bf16[400,512]{1,0:T(8,128)(2,1)S(1)}, u32[]{:S(2)}, u32[]{:S(2)}) collective-permute-start(bf16[400,512]{1,0:T(8,128)(2,1)S(1)} %get-tuple-element.54), channel_id=1, source_target_pairs={{0,254},{2,0},{4,2},{6,4},{8,6},{10,8},{12,10},{14,12},{16,14},{18... | collective-permute-start | bytes 1228808 | tf_op jit(solution)/shard_map/ppermute | solution.py:326
  28.8 1.0 tail.1
  29.8 3.6 %spread.1 = bf16[32,256,128]{2,1,0:T(8,128)(2,1)} custom-call(bf16[400,768]{1,0:T(8,128)(2,1)S(1)} %get-tuple-element.43.grad_ref, s32[1,768]{1,0:T(1,128)S(1)} %bitcast.32, bf16[4544,128]{1,0:T(8,128)(2,1)S(1)} %collective-permute-done.2.got_ref, bf16[2048,128]{1,0:T(8,128)(2,1)S(1)} %get-tuple-element.52.hot_ref, s32[1]{0:T(128)} %bitcast.9.core_ref), custom_call_target="tpu_custom_call" | custom-call | flops 100000000 | bytes 1000000 | tf_op jit(solution)/shard_map/spread/pallas_call | solution.py:408
  33.4 0.9 collective-permute-done.4
  34.3 0.7 copy-done.10
  35.0 7.0 %collective-permute-done.3 = bf16[400,512]{1,0:T(8,128)(2,1)} collective-permute-done((bf16[400,512]{1,0:T(8,128)(2,1)S(1)}, bf16[400,512]{1,0:T(8,128)(2,1)}, u32[]{:S(2)}, u32[]{:S(2)}) %collective-permute-start.3) | collective-permute-done | bytes 409632 | tf_op jit(solution)/shard_map/ppermute | solution.py:326
  42.0 5.1 %all-to-all-start = ((bf16[32,256,128]{2,1,0:T(8,128)(2,1)}), bf16[32,256,128]{2,1,0:T(8,128)(2,1)S(1)}, u32[]{:S(2)}, u32[]{:S(2)}) async-start(bf16[32,256,128]{2,1,0:T(8,128)(2,1)} %spread.1), calls=%async_computation | async-start | bytes 4194304 | tf_op jit(solution)/shard_map/all_to_all | solution.py:424
  47.1 1.3 %add_convert_fusion = bf16[400,512]{1,0:T(8,128)(2,1)S(1)} fusion(bf16[400,512]{1,0:T(8,128)(2,1)} %copy-done.10, f32[400,512]{1,0:T(8,128)S(1)} %get-tuple-element.56, bf16[400,512]{1,0:T(8,128)(2,1)} %collective-permute-done.3), kind=kLoop, calls=%fused_computation.1 | loop fusion | flops 1024000 | bytes 2048000 | tf_op jit(solution)/shard_map/convert_element_type | solution.py:425
  48.4 20.4 %all-to-all-done.in_ref = bf16[32,256,128]{2,1,0:T(8,128)(2,1)S(1)} async-done(((bf16[32,256,128]{2,1,0:T(8,128)(2,1)}), bf16[32,256,128]{2,1,0:T(8,128)(2,1)S(1)}, u32[]{:S(2)}, u32[]{:S(2)}) %all-to-all-start) | async-done | bytes 2097184 | tf_op jit(solution)/shard_map/all_to_all | solution.py:424
  69.1 1.4 %collective-permute-start.5 = (bf16[256,128]{1,0:T(8,128)(2,1)S(1)}, bf16[256,128]{1,0:T(8,128)(2,1)S(1)}, u32[]{:S(2)}, u32[]{:S(2)}) collective-permute-start(bf16[256,128]{1,0:T(8,128)(2,1)S(1)} %near_sum.1.mine_ref), channel_id=1, source_target_pairs={{0,8},{8,0},{16,24},{24,16},{1,9},{9,1},{17,25},{25,17},{2,10},{10... | collective-permute-start | bytes 196616 | tf_op jit(solution)/shard_map/ppermute | solution.py:436
  70.5 5.2 %collective-permute-done.5.got_ref = bf16[256,128]{1,0:T(8,128)(2,1)S(1)} collective-permute-done((bf16[256,128]{1,0:T(8,128)(2,1)S(1)}, bf16[256,128]{1,0:T(8,128)(2,1)S(1)}, u32[]{:S(2)}, u32[]{:S(2)}) %collective-permute-start.5) | collective-permute-done | bytes 65568 | tf_op jit(solution)/shard_map/ppermute | solution.py:436
  75.8 1.5 %collective-permute-start.6 = (bf16[256,128]{1,0:T(8,128)(2,1)S(1)}, bf16[256,128]{1,0:T(8,128)(2,1)S(1)}, u32[]{:S(2)}, u32[]{:S(2)}) collective-permute-start(bf16[256,128]{1,0:T(8,128)(2,1)S(1)} %pair_sum.1.mine_ref), channel_id=1, source_target_pairs={{0,24},{8,16},{16,8},{24,0},{1,25},{9,17},{17,9},{25,1},{2,26},{10... | collective-permute-start | bytes 196616 | tf_op jit(solution)/shard_map/ppermute | solution.py:445
  77.3 5.0 %collective-permute-done.6.got_ref = bf16[256,128]{1,0:T(8,128)(2,1)S(1)} collective-permute-done((bf16[256,128]{1,0:T(8,128)(2,1)S(1)}, bf16[256,128]{1,0:T(8,128)(2,1)S(1)}, u32[]{:S(2)}, u32[]{:S(2)}) %collective-permute-start.6) | collective-permute-done | bytes 65568 | tf_op jit(solution)/shard_map/ppermute | solution.py:445
  83.0 27.3 %all_to_all.10.in_ref = bf16[32,200,128]{2,1,0:T(8,128)(2,1)S(1)} all-to-all(bf16[32,200,128]{2,1,0:T(8,128)(2,1)S(1)} %get-tuple-element.63), channel_id=1, replica_groups=mesh['y'=4,'xh'=2,'zh'=4,'zl'=2,'core'=2,'rep'=2] {'y','xh','zl','rep'}, dimensions={0} | all-to-all | bytes 3276800 | tf_op jit(solution)/shard_map/all_to_all | solution.py:456
  110.2 1.0 add_bitcast_fusion
  111.2 1.9 %merge.2.refs_0_ = f32[400,4096]{1,0:T(8,128)} custom-call(s32[1]{0:T(128)} %bitcast.9.core_ref, bf16[32,200,128]{2,1,0:T(8,128)(2,1)S(1)} %all_to_all.10.in_ref), custom_call_target="tpu_custom_call" | custom-call | bytes 10000000 | tf_op jit(solution)/shard_map/merge/pallas_call | solution.py:298
  113.7 1.9 %merge.3 = f32[400,4096]{1,0:T(8,128)} custom-call(s32[1]{0:T(128)} %bitcast.9.core_ref, bf16[32,200,128]{2,1,0:T(8,128)(2,1)S(1)} %collective-permute-done.8.in_ref, f32[400,4096]{1,0:T(8,128)} %merge.2.refs_0_), custom_call_target="tpu_custom_call", output_to_operand_aliasing={{}: (2, {})} | custom-call | bytes 10000000 | tf_op jit(solution)/shard_map/merge/pallas_call | solution.py:298
  (33 shorter events, 2.5 us)
Async XLA Ops:
  0.6 18.5 %collective-permute-start.1 = (bf16[400,512]{1,0:T(8,128)(2,1)}, bf16[400,512]{1,0:T(8,128)(2,1)S(1)}, u32[]{:S(2)}, u32[]{:S(2)}) collective-permute-start(bf16[400,512]{1,0:T(8,128)(2,1)} %bitcast.17), channel_id=1, source_target_pairs={{0,2},{2,4},{4,6},{6,8},{8,10},{10,12},{12,14},{14,16},{16,18},{18... | collective-permute-start | bytes 1228808 | tf_op jit(solution)/shard_map/ppermute | solution.py:326
  0.7 21.3 %collective-permute-start = (bf16[400,512]{1,0:T(8,128)(2,1)}, bf16[400,512]{1,0:T(8,128)(2,1)S(1)}, u32[]{:S(2)}, u32[]{:S(2)}) collective-permute-start(bf16[400,512]{1,0:T(8,128)(2,1)} %bitcast.18), channel_id=1, source_target_pairs={{0,254},{2,0},{4,2},{6,4},{8,6},{10,8},{12,10},{14,12},{16,14},{18... | collective-permute-start | bytes 1228808 | tf_op jit(solution)/shard_map/ppermute | solution.py:326
  10.1 0.7 copy-start.6
  10.8 1.9 %copy-start.9 = (bf16[4096,400]{0,1:T(8,128)(2,1)S(1)}, bf16[4096,400]{0,1:T(8,128)(2,1)}, u32[]{:S(2)}) copy-start(bf16[4096,400]{0,1:T(8,128)(2,1)} %param.11) | copy-start | bytes 9830404
  12.7 2.8 %copy-start = (bf16[1024,400]{0,1:T(8,128)(2,1)S(1)}, bf16[1024,400]{0,1:T(8,128)(2,1)}, u32[]{:S(2)}) copy-start(bf16[1024,400]{0,1:T(8,128)(2,1)} %param.10) | copy-start | bytes 2457604
  12.7 2.8 %copy-start.1 = (bf16[512,400]{0,1:T(8,128)(2,1)S(1)}, bf16[512,400]{0,1:T(8,128)(2,1)}, u32[]{:S(2)}) copy-start(bf16[512,400]{0,1:T(8,128)(2,1)} %param.9) | copy-start | bytes 1228804
  12.7 2.8 %copy-start.2 = (s32[1,1,3,512]{3,1,2,0:T(1,128)S(1)}, s32[1,1,3,512]{3,1,2,0:T(1,128)}, u32[]{:S(2)}) copy-start(s32[1,1,3,512]{3,1,2,0:T(1,128)} %param.15) | copy-start | bytes 18436
  12.7 2.8 %copy-start.3 = (s32[1,1,3,256]{3,1,2,0:T(1,128)S(1)}, s32[1,1,3,256]{3,1,2,0:T(1,128)}, u32[]{:S(2)}) copy-start(s32[1,1,3,256]{3,1,2,0:T(1,128)} %param.14) | copy-start | bytes 9220
  12.7 2.8 %copy-start.5 = (s32[1,1,3,256]{3,1,2,0:T(1,128)S(1)}, s32[1,1,3,256]{3,1,2,0:T(1,128)}, u32[]{:S(2)}) copy-start(s32[1,1,3,256]{3,1,2,0:T(1,128)} %param.12) | copy-start | bytes 9220
  12.7 2.8 %copy-start.8 = (s32[1,1,3]{2,1,0:T(1,128)S(1)}, s32[1,1,3]{2,1,0:T(1,128)}, u32[]{:S(2)}) copy-start(s32[1,1,3]{2,1,0:T(1,128)} %param.16) | copy-start | bytes 40
  22.0 2.8 %copy-start.4 = (s32[1024]{0:T(1024)S(1)}, s32[1024]{0:T(1024)}, u32[]{:S(2)}) copy-start(s32[1024]{0:T(1024)} %param.17) | copy-start | bytes 12292
  24.8 5.0 %copy-start.7 = (s32[1,1,3,256]{3,1,2,0:T(1,128)S(1)}, s32[1,1,3,256]{3,1,2,0:T(1,128)}, u32[]{:S(2)}) copy-start(s32[1,1,3,256]{3,1,2,0:T(1,128)} %param.13) | copy-start | bytes 9220
  26.4 3.4 %collective-permute-start.2 = (bf16[4544,128]{1,0:T(8,128)(2,1)S(1)}, bf16[4544,128]{1,0:T(8,128)(2,1)S(1)}, u32[]{:S(2)}, u32[]{:S(2)}) collective-permute-start(bf16[4544,128]{1,0:T(8,128)(2,1)S(1)} %get-tuple-element.44), channel_id=1, source_target_pairs={{0,2},{2,0},{1,3},{3,1},{4,6},{6,4},{5,7},{7,5},{8,10},{10,8},{9,1... | collective-permute-start | bytes 3489800 | tf_op jit(solution)/shard_map/ppermute | solution.py:406
  26.5 7.8 %collective-permute-start.4 = (bf16[400,512]{1,0:T(8,128)(2,1)S(1)}, bf16[400,512]{1,0:T(8,128)(2,1)S(1)}, u32[]{:S(2)}, u32[]{:S(2)}) collective-permute-start(bf16[400,512]{1,0:T(8,128)(2,1)S(1)} %get-tuple-element.54), channel_id=1, source_target_pairs={{0,254},{2,0},{4,2},{6,4},{8,6},{10,8},{12,10},{14,12},{16,14},{18... | collective-permute-start | bytes 1228808 | tf_op jit(solution)/shard_map/ppermute | solution.py:326
  28.8 13.2 %collective-permute-start.3 = (bf16[400,512]{1,0:T(8,128)(2,1)S(1)}, bf16[400,512]{1,0:T(8,128)(2,1)}, u32[]{:S(2)}, u32[]{:S(2)}) collective-permute-start(bf16[400,512]{1,0:T(8,128)(2,1)S(1)} %get-tuple-element.53), channel_id=1, source_target_pairs={{0,2},{2,4},{4,6},{6,8},{8,10},{10,12},{12,14},{14,16},{16,18},{18... | collective-permute-start | bytes 1228808 | tf_op jit(solution)/shard_map/ppermute | solution.py:326
  34.3 0.8 copy-start.10
  42.0 26.8 %all-to-all-start = ((bf16[32,256,128]{2,1,0:T(8,128)(2,1)}), bf16[32,256,128]{2,1,0:T(8,128)(2,1)S(1)}, u32[]{:S(2)}, u32[]{:S(2)}) async-start(bf16[32,256,128]{2,1,0:T(8,128)(2,1)} %spread.1), calls=%async_computation | async-start | bytes 4194304 | tf_op jit(solution)/shard_map/all_to_all | solution.py:424
  68.9 14.1 %collective-permute-start.7 = (bf16[400,512]{1,0:T(8,128)(2,1)S(1)}, bf16[400,512]{1,0:T(8,128)(2,1)S(1)}, u32[]{:S(2)}, u32[]{:S(2)}) collective-permute-start(bf16[400,512]{1,0:T(8,128)(2,1)S(1)} %add_convert_fusion), channel_id=1, source_target_pairs={{0,1},{1,0},{2,3},{3,2},{4,5},{5,4},{6,7},{7,6},{8,9},{9,8},{10,11... | collective-permute-start | bytes 1228808 | tf_op jit(solution)/shard_map/ppermute | solution.py:427
  69.1 6.6 %collective-permute-start.5 = (bf16[256,128]{1,0:T(8,128)(2,1)S(1)}, bf16[256,128]{1,0:T(8,128)(2,1)S(1)}, u32[]{:S(2)}, u32[]{:S(2)}) collective-permute-start(bf16[256,128]{1,0:T(8,128)(2,1)S(1)} %near_sum.1.mine_ref), channel_id=1, source_target_pairs={{0,8},{8,0},{16,24},{24,16},{1,9},{9,1},{17,25},{25,17},{2,10},{10... | collective-permute-start | bytes 196616 | tf_op jit(solution)/shard_map/ppermute | solution.py:436
  75.8 6.5 %collective-permute-start.6 = (bf16[256,128]{1,0:T(8,128)(2,1)S(1)}, bf16[256,128]{1,0:T(8,128)(2,1)S(1)}, u32[]{:S(2)}, u32[]{:S(2)}) collective-permute-start(bf16[256,128]{1,0:T(8,128)(2,1)S(1)} %pair_sum.1.mine_ref), channel_id=1, source_target_pairs={{0,24},{8,16},{16,8},{24,0},{1,25},{9,17},{17,9},{25,1},{2,26},{10... | collective-permute-start | bytes 196616 | tf_op jit(solution)/shard_map/ppermute | solution.py:445
  110.2 3.5 %collective-permute-start.8 = (bf16[32,200,128]{2,1,0:T(8,128)(2,1)S(1)}, bf16[32,200,128]{2,1,0:T(8,128)(2,1)S(1)}, u32[]{:S(2)}, u32[]{:S(2)}) collective-permute-start(bf16[32,200,128]{2,1,0:T(8,128)(2,1)S(1)} %all_to_all.10.in_ref), channel_id=1, source_target_pairs={{0,2},{2,0},{1,3},{3,1},{4,6},{6,4},{5,7},{7,5},{8,10},{10,8},{9,1... | collective-permute-start | bytes 4915208 | tf_op jit(solution)/shard_map/ppermute | solution.py:457
